TPU v7x, 128 devices: a whole 4x4x4 slice. The times are simulated.
128 devices in a mesh: depth: 4 (over y), row: 8 (over x, z_hi), column: 4 (over z_lo, core).
Axes of the slice: x: 4, y: 4, z: 4 (z_hi: 2, z_lo: 2; z = z_hi * 2 + z_lo), core: 2. Of those that a mesh axis runs over, the one named last changes fastest.
Arguments:
- vir_irrep: int32 [1024], replicated, may hold values from 0 to 7, as said below
- occ_irrep: int32 [150], replicated, may hold values from 0 to 7, as said below
- allowed: int32 [8, 8, 8], replicated, may hold values 0 or 1
- pair_list: int32 [32, 2], replicated, may hold values from 0 to 149, as said below
- occ_energy: float32 [150], replicated, may hold values from -2 to -0.3
- vir_energy: float32 [1024], replicated, may hold values from 0.1 to 3
- ladder_amp: float32 [32, 1024, 256], P(None, 'depth', ('row', 'column')), may hold values from -6 to 6
- int_slab: float32 [8, 256, 1024, 256], P('row', 'column', 'depth'), may hold values from -0.015625 to 0.015625
- cycle_amp: float32 [32, 8, 153600], P(None, None, ('depth', 'row')), may hold values from -6 to 6
- cycle_int: float32 [153600, 4, 256], P(('depth', 'row'), None, 'column'), may hold values from -0.015625 to 0.015625
Outputs:
- new_amp: float32 [8, 32, 256], P('row', 'depth', 'column')
Inputs may be any that keep to these rules, and one draw needn't show every extreme that they name: `vir_irrep`: Nondecreasing; every irrep labels one run of between a quarter of 256 and 256 orbitals, and one run has exactly 256. `occ_irrep`: every irrep labels at least one occupied orbital. `pair_list`: column 0 is an occupied orbital i, column 1 an occupied orbital j below 4; occ_irrep[i] XOR occ_irrep[j] is the same for all pairs.
All inputs are finite; a program needn't handle non-finite values.
Results may differ from a plain program's by a relative error of at most 0.0003.
Values sent between devices are 32-bit elements; how exact they have to be, the bound alone decides.
No kernel may reach another device: no remote copies, remote signals or barrier semaphores. Data moves between devices by JAX's collectives and lax.ppermute only.
A program may use at most 128 MiB of HBM per device.

v0:
```python
import jax
import jax.numpy as jnp
from jax import lax
from jax.sharding import PartitionSpec as P


def lookup(table, index):
    hits = (index[..., None] == jnp.arange(table.shape[0], dtype=jnp.int32)).astype(table.dtype)
    return jnp.sum(hits * table, axis=-1)


def on_device(
    vir_irrep,
    occ_irrep,
    allowed,
    pair_list,
    occ_energy,
    vir_energy,
    ladder_amp,
    int_slab,
    cycle_amp,
    cycle_int,
):
    depth_count = lax.axis_size("depth")
    depth_index = lax.axis_index("depth")
    row_index = lax.axis_index("row")
    column_index = lax.axis_index("column")
    a_dev = int_slab.shape[0]
    slot_width = int_slab.shape[1]
    cells = int_slab.shape[2]
    total_vir = vir_irrep.shape[0]
    pairs_total = ladder_amp.shape[0]
    a_total = cycle_amp.shape[1]
    per_depth = pairs_total // depth_count
    window_j = cycle_int.shape[1]
    groups = jnp.arange(allowed.shape[0], dtype=jnp.int32)
    pair_irrep = jnp.bitwise_xor(
        lookup(occ_irrep, pair_list[0, 0]), lookup(occ_irrep, pair_list[0, 1])
    )
    counts = jnp.sum((vir_irrep[None, :] == groups[:, None]).astype(jnp.int32), axis=1)
    starts = jnp.sum((vir_irrep[None, :] < groups[:, None]).astype(jnp.int32), axis=1)
    a_orb = (row_index * a_dev + jnp.arange(a_dev, dtype=jnp.int32)) * (total_vir // a_total)
    a_irrep = lookup(vir_irrep, a_orb)
    b_irrep = jnp.bitwise_xor(a_irrep, pair_irrep)
    slots = column_index * slot_width + jnp.arange(slot_width, dtype=jnp.int32)
    b_orb = lookup(starts, b_irrep)[:, None] + slots[None, :]
    row_live = slots[None, :] < lookup(counts, b_irrep)[:, None]
    c_irrep = lax.dynamic_slice_in_dim(vir_irrep, depth_index * cells, cells)
    d_count = lookup(counts, jnp.bitwise_xor(c_irrep, pair_irrep))
    pattern = allowed.astype(jnp.float32)
    sel_a = (a_irrep[:, None] == groups[None, :]).astype(jnp.float32)
    sel_b = (b_irrep[:, None] == groups[None, :]).astype(jnp.float32)
    kept_rows = jnp.einsum("xyg,ax,ay->ag", pattern, sel_a, sel_b, precision=lax.Precision.HIGHEST)
    sel_c = (c_irrep[:, None] == groups[None, :]).astype(jnp.float32)
    allow = jnp.dot(
        kept_rows, sel_c.T, precision=lax.Precision.HIGHEST, preferred_element_type=jnp.float32
    )
    full_amp = lax.all_gather(ladder_amp, ("row", "column"), axis=2, tiled=True)
    width = full_amp.shape[2]
    d_slots = jnp.arange(width, dtype=jnp.int32)
    live = (d_slots[None, :] < d_count[:, None]).astype(jnp.float32)
    weights = full_amp[None] * (allow[:, :, None] * live[None])[:, None]
    ladder_total = jnp.einsum(
        "apcd,abcd->apb",
        weights,
        int_slab,
        precision=lax.Precision.HIGHEST,
        preferred_element_type=jnp.float32,
    )
    amp_split = cycle_amp.reshape(depth_count, per_depth, a_total, cycle_amp.shape[2])
    cycle_full = jnp.einsum(
        "qsak,kjb->qasjb",
        amp_split,
        cycle_int,
        precision=lax.Precision.HIGHEST,
        preferred_element_type=jnp.float32,
    )
    j_choice = (
        pair_list[:, 1].reshape(depth_count, per_depth)[:, :, None]
        == jnp.arange(window_j, dtype=jnp.int32)
    ).astype(jnp.float32)
    cycle_term = jnp.einsum(
        "qasjb,qsj->qasb", cycle_full, j_choice, precision=lax.Precision.HIGHEST
    )
    ladder_part = lax.psum_scatter(ladder_total, "depth", scatter_dimension=1, tiled=True)
    flat_term = cycle_term.reshape(depth_count * a_total, per_depth, slot_width)
    cycle_part = lax.psum_scatter(flat_term, ("depth", "row"), scatter_dimension=0, tiled=True)
    summed = ladder_part + cycle_part
    local_pairs = lax.dynamic_slice_in_dim(pair_list, depth_index * per_depth, per_depth, 0)
    eps_i = lookup(occ_energy, local_pairs[:, 0])
    eps_j = lookup(occ_energy, local_pairs[:, 1])
    eps_a = lookup(vir_energy, a_orb)
    eps_b = lookup(vir_energy, b_orb)
    denom = (eps_i + eps_j)[None, :, None] - eps_a[:, None, None] - eps_b[:, None, :]
    return jnp.where(row_live[:, None, :], summed / denom, jnp.float32(0.0))


def solution(mesh):
    return jax.shard_map(
        on_device,
        mesh=mesh,
        in_specs=(
            P(),
            P(),
            P(),
            P(),
            P(),
            P(),
            P(None, "depth", ("row", "column")),
            P("row", "column", "depth", None),
            P(None, None, ("depth", "row")),
            P(("depth", "row"), None, "column"),
        ),
        out_specs=P("row", "depth", "column"),
        check_vma=False,
    )
```

profile of v0, /device:TPU:0, one launch (start us, length us, event | category | flops | bytes accessed | tf_op | source)
XLA Modules:
  0.0 370.4 jit_solution(10233737414963339761)
XLA Ops:
  7.4 0.0 copy-start.2
  7.4 0.0 copy-start
  7.4 0.0 copy-start.5
  7.4 0.0 all-gather.2.cloned.1.call-start
  7.5 0.7 all-gather.2.cloned.1.call-update
  8.1 0.0 all-reduce.4.cloned.1.call-start
  8.2 0.7 slice_reduce_fusion
  8.9 0.1 eq.227
  9.0 0.1 fusion.17
  9.1 11.0 %fusion.4 = f32[4,8,8,4,64]{4,1,2,0,3:T(8,128)S(1)} fusion(f32[4,8,8,4800,1]{3,2,1,0,4:T(8,128)} %bitcast.49, f32[4800,4,64]{0,2,1:T(8,128)} %param.19), kind=kOutput, calls=%fused_computation.5 | convolution fusion | flops 3774873600 | bytes 10092544 | tf_op jit(solution)/shard_map/qsak,kjb->qasjb/dot_general | solution.py:71
  20.1 0.9 fusion.10
  21.0 0.7 copy.21
  21.7 0.0 all-reduce.4.cloned.1.call-update
  21.7 0.0 copy-done.3
  21.7 0.5 fusion.28
  22.2 0.0 copy-done.1
  22.2 0.1 convert_reduce_fusion
  22.4 0.6 select_reduce_fusion.5
  23.0 0.0 copy-done.4
  23.0 1.8 fusion.21
  26.7 0.6 fusion.24
  27.4 0.1 multiply_bitcast_fusion
  27.4 0.1 copy.17
  27.5 0.1 broadcast_xor_fusion
  27.6 0.6 fusion.22
  28.2 0.1 select_reduce_fusion.3
  28.3 0.1 constant_dynamic-slice_fusion
  28.4 0.0 copy-done.2
  28.4 0.6 select_reduce_fusion.4
  29.0 0.6 fusion.23
  29.6 0.6 fusion.27
  30.2 0.7 fusion.26
  30.9 0.2 select_reduce_fusion
  31.1 0.0 copy-done.7
  31.1 0.6 dynamic-slice
  31.7 0.6 dynamic-slice.2
  32.3 0.2 convolution_bitcast_fusion
  32.5 0.2 fusion.13
  32.7 0.1 fusion.12
  33.5 0.2 select_reduce_fusion.1
  33.7 0.6 add_subtract_fusion
  34.3 38.7 %all-gather.2.cloned.1.call-done = f32[32,256,256]{1,2,0:T(8,128)} async-done(((f32[32,256,8]{1,2,0:T(8,128)}), f32[32,256,256]{1,2,0:T(8,128)}) %all-gather.2.cloned.1.call-update) | async-done | bytes 8388624 | tf_op jit(solution)/shard_map/all_gather | solution.py:58
  73.0 7.5 %broadcast_multiply_fusion = f32[32,256,256]{1,2,0:T(8,128)} fusion(f32[32,256,256]{1,2,0:T(8,128)} %all-gather.2.cloned.1.call-done, f32[256,256]{0,1:T(8,128)S(1)} %fusion.12), kind=kLoop, calls=%fused_computation.4 | loop fusion | flops 2097152 | bytes 17039360 | tf_op jit(solution)/shard_map/mul | solution.py:62
  80.5 10.3 %copy.15 = f32[32,256,256]{2,0,1:T(8,128)} copy(f32[32,256,256]{1,2,0:T(8,128)} %broadcast_multiply_fusion) | data formatting | bytes 16777216 | tf_op jit(solution)/shard_map/mul | solution.py:62
  90.8 29.7 %fusion.7 = f32[1,32,64]{2,1,0:T(8,128)S(1)} fusion(f32[32,256,256]{2,0,1:T(8,128)} %copy.15, f32[64,256,256]{2,1,0:T(8,128)} %bitcast.48), kind=kOutput, calls=%fused_computation.6 | convolution fusion | flops 1610612736 | bytes 25174016 | tf_op jit(solution)/shard_map/apcd,abcd->apb/dot_general | solution.py:63
  120.4 16.8 %all-reduce = f32[1,32,64]{2,1,0:T(8,128)S(1)} all-reduce(f32[1,32,64]{2,1,0:T(8,128)S(1)} %fusion.7), channel_id=2, replica_groups=mesh['depth'=4,'row'=8,'column'=4] {'depth'}, use_global_device_ids=true, to_apply=%region_6.0.clone | all-reduce | flops 2048 | bytes 16384
  137.3 223.7 %all-reduce.4.cloned.1.call-done = f32[32,8,64]{2,1,0:T(8,128)} async-done(((f32[32,8,64]{2,1,0:T(8,128)}), f32[32,8,64]{2,1,0:T(8,128)}) %all-reduce.4.cloned.1.call-update) | async-done | bytes 65552
  361.0 2.0 fusion.19
  (9 shorter events, 0.0 us)
Async XLA Ops:
  7.4 23.7 %copy-start.7 = (u32[128]{0:T(128)S(1)}, u32[128]{0:T(128)}, u32[]{:S(2)}) copy-start(u32[128]{0:T(128)} %constant.45) | copy-start | bytes 1540
  7.4 24.3 %copy-start.6 = (u32[128]{0:T(128)S(1)}, u32[128]{0:T(128)}, u32[]{:S(2)}) copy-start(u32[128]{0:T(128)} %constant.49) | copy-start | bytes 1540
  7.4 14.3 %copy-start.3 = (s32[32,2]{0,1:T(2,128)S(1)}, s32[32,2]{0,1:T(2,128)}, u32[]{:S(2)}) copy-start(s32[32,2]{0,1:T(2,128)} %param.13) | copy-start | bytes 772
  7.4 14.9 %copy-start.1 = (s32[1024]{0:T(1024)S(1)}, s32[1024]{0:T(1024)}, u32[]{:S(2)}) copy-start(s32[1024]{0:T(1024)} %param.10) | copy-start | bytes 12292
  7.4 15.6 %copy-start.4 = (s32[150]{0:T(256)S(1)}, s32[150]{0:T(256)}, u32[]{:S(2)}) copy-start(s32[150]{0:T(256)} %param.11) | copy-start | bytes 1804
  7.4 21.0 %copy-start.2 = (f32[1024]{0:T(1024)S(1)}, f32[1024]{0:T(1024)}, u32[]{:S(2)}) copy-start(f32[1024]{0:T(1024)} %param.15) | copy-start | bytes 12292
  7.4 24.9 %copy-start = (s32[8,8,8]{2,1,0:T(8,128)S(1)}, s32[8,8,8]{2,1,0:T(8,128)}, u32[]{:S(2)}) copy-start(s32[8,8,8]{2,1,0:T(8,128)} %param.12) | copy-start | bytes 6148
  7.4 26.1 %copy-start.5 = (f32[150]{0:T(256)S(1)}, f32[150]{0:T(256)}, u32[]{:S(2)}) copy-start(f32[150]{0:T(256)} %param.14) | copy-start | bytes 1804
  7.4 65.5 %all-gather.2.cloned.1.call-start = ((), (), s32[]{:S(2)}) async-start(), calls=%async_computation | async-start | bytes 8650752 | tf_op jit(solution)/shard_map/all_gather | solution.py:58
  8.1 352.9 %all-reduce.4.cloned.1.call-start = ((), (), s32[]{:S(2)}) async-start(), calls=%async_computation.1 | async-start | bytes 262144
Sparse Core Ops, SparseCore 0:
  10.7 62.2 all-gather.1
Sparse Core Ops, SparseCore 1:
  21.8 339.2 all-reduce.3
where the time goes:
time: 371 us; the launch traced here: 370 us
  waiting for transfers between devices  263 us (71%)
  matrix products  42 us (11%)
  between operations  17.5 us (5%)
  other arithmetic  17.3 us (5%)
  blocking collectives  16.8 us (5%)
  local copies, waits for them, and re-layouts  13.7 us (4%)
    unnamed x3, waiting for transfers between devices  224 us
    all_gather x1, waiting for transfers between devices, on_device(): full_amp = lax.all_gather(ladder_amp, ('row', 'column'), axis=2, tiled=True)  38.7 us
    dot_general x1, matrix products, on_device(): jnp.einsum('apcd,abcd->apb', weights, int_slab, precision=lax.Precision.H...  29.7 us
    unnamed x1, blocking collectives  16.8 us
    dot_general x1, matrix products, on_device(): jnp.einsum('qsak,kjb->qasjb', amp_split, cycle_int, precision=lax.Precisi...  11 us
    mul x1, local copies, waits for them, and re-layouts, on_device(): weights = full_amp[None] * (allow[:, :, None] * live[None])[:, None]  10.3 us
    mul x2, other arithmetic, on_device(): weights = full_amp[None] * (allow[:, :, None] * live[None])[:, None]  7.59 us
  transfers between devices with their start and end apart: 2, of which 2 were waited for; matrix products, arithmetic and copies ran while one was open for 19% of the time, Pallas kernels for 0%

commit v1 on v0

v1 whole, which is shorter than its diff:
```python
import functools

import jax
import jax.numpy as jnp
from jax import lax
from jax.experimental import pallas as pl
from jax.experimental.pallas import tpu as pltpu
from jax.sharding import PartitionSpec as P

AXES = ("depth", "row", "column")
F32 = jnp.float32
BF16 = jnp.bfloat16
MIB = 1 << 20


def pairs_of(core0, core1):
    out = []
    for y in range(4):
        for x in range(4):
            for z in range(4):
                for k in range(2):
                    ty, tx, tz, tk = (core1 if k else core0)(y, x, z, k)
                    out.append((y * 32 + x * 8 + z * 2 + k, (ty % 4) * 32 + (tx % 4) * 8 + (tz % 4) * 2 + tk % 2))
    return out


def along_x(n):
    return lambda y, x, z, k: (y, x + n, z, k)


def along_y(n):
    return lambda y, x, z, k: (y + n, x, z, k)


def along_z(n):
    return lambda y, x, z, k: (y, x, z + n, k)


def other_core(y, x, z, k):
    return (y, x, z, k + 1)


FIRST = {n: pairs_of(along_x(n), along_z(n)) for n in (1, -1, 2)}
SECOND = {n: pairs_of(along_z(n), along_x(n)) for n in (1, -1, 2)}
ALONG_X = {n: pairs_of(along_x(n), along_x(n)) for n in (1, -1, 2)}
ALONG_Y = {n: pairs_of(along_y(n), along_y(n)) for n in (1, -1, 2)}
Z_ACROSS = pairs_of(along_z(2), along_z(2))
SWAP = pairs_of(other_core, other_core)


def send(value, pairs):
    return lax.ppermute(value, AXES, pairs)


def smem():
    return pl.BlockSpec(memory_space=pltpu.SMEM)


def vmem():
    return pl.BlockSpec(memory_space=pltpu.VMEM)


def hbm():
    return pl.BlockSpec(memory_space=pl.ANY)


def relayout_body(amp_ref, out_ref, turned):
    pairs, slots, cells = amp_ref.shape
    groups = cells // 8
    for t in range(slots):
        turned[t] = amp_ref[:, t, :].T
    for t in range(slots):
        pieces = [turned[t, pl.ds(j, groups, stride=8), :] for j in range(8)]
        out_ref[:, t, :] = jnp.concatenate(pieces, axis=1)


def relayout(amp):
    pairs, slots, cells = amp.shape
    return pl.pallas_call(
        relayout_body,
        out_shape=jax.ShapeDtypeStruct((cells // 8, slots, 8 * pairs), F32),
        in_specs=[vmem()],
        out_specs=vmem(),
        scratch_shapes=[pltpu.VMEM((slots, cells, pairs), F32)],
        cost_estimate=pl.CostEstimate(flops=1000, bytes_accessed=2 * MIB, transcendentals=0),
    )(amp)


def stack_body(place, b0, b1, b2, b3, q0, q1, q2, q3, sems):
    core = place[3]
    own = jnp.where(core == 0, place[1], place[2])
    copies = []
    for n, (source, shift) in enumerate(((b0, 0), (b1, 3), (b2, 1), (b3, 2))):
        at = lax.rem(own + shift, 4)
        for i, q in enumerate((q0, q1, q2, q3)):
            copies.append(pltpu.make_async_copy(source.at[pl.ds(8 * i, 8)], q.at[:, at], sems.at[n, i]))
    for c in copies:
        c.start()
    for c in copies:
        c.wait()


def stack(place, blocks):
    groups, slots, lanes = blocks[0].shape
    quarter = jax.ShapeDtypeStruct((groups // 4, 4, slots, lanes), F32)
    return pl.pallas_call(
        stack_body,
        out_shape=(quarter,) * 4,
        in_specs=[smem()] + [hbm()] * 4,
        out_specs=(hbm(),) * 4,
        scratch_shapes=[pltpu.SemaphoreType.DMA((4, 4))],
        cost_estimate=pl.CostEstimate(flops=1000, bytes_accessed=4 * MIB, transcendentals=0),
    )(place, *blocks)


def dot_nt(a, b):
    return lax.dot_general(a, b, (((1,), (1,)), ((), ())), preferred_element_type=F32)


def split(value):
    high = value.astype(BF16)
    return high, (value - high.astype(F32)).astype(BF16)


def cycle_body(place, amp_ref, int_ref, choice_ref, o0, o1, o2, o3, int_high, int_low, by_row):
    step = pl.program_id(0)
    width = int_ref.shape[1]
    window = int_ref.shape[0]

    @pl.when(step == 0)
    def _():
        for j in range(window):
            high, low = split(int_ref[j])
            int_high[pl.ds(j * width, width), :] = high
            int_low[pl.ds(j * width, width), :] = low

    pairs, rows, depth = amp_ref.shape
    high, low = split(amp_ref[...].reshape(pairs * rows, depth))
    full = dot_nt(high, int_high[...]) + dot_nt(high, int_low[...]) + dot_nt(low, int_high[...])
    total = jnp.zeros((pairs * rows, width), F32)
    for j in range(window):
        pick = choice_ref[:, j : j + 1]
        total = total + pick * full[:, j * width : (j + 1) * width]
    by_row[pl.ds(step * pairs, pairs)] = total.reshape(pairs, rows, width)

    @pl.when(step == pl.num_programs(0) - 1)
    def _():
        x = place[1]
        for out, shift in ((o0, 0), (o1, 1), (o2, 3), (o3, 2)):
            at = lax.rem(x + shift, 4)
            for other in range(4):

                @pl.when(at == other)
                def _(out=out, other=other):
                    for h in range(2):
                        out[h] = by_row[:, 2 * other + h, :]


def cycle(place, amp, ints, choice):
    pairs, rows, depth = amp.shape
    window, width, _ = ints.shape
    steps = 4
    block = pairs // steps
    part = jax.ShapeDtypeStruct((2, pairs, width), F32)
    whole = pl.BlockSpec((2, pairs, width), lambda i: (0, 0, 0))
    return pl.pallas_call(
        cycle_body,
        grid=(steps,),
        out_shape=(part,) * 4,
        in_specs=[
            smem(),
            pl.BlockSpec((block, rows, depth), lambda i: (i, 0, 0)),
            pl.BlockSpec((window, width, depth), lambda i: (0, 0, 0)),
            pl.BlockSpec((block * rows, window), lambda i: (i, 0)),
        ],
        out_specs=(whole,) * 4,
        scratch_shapes=[
            pltpu.VMEM((window * width, depth), BF16),
            pltpu.VMEM((window * width, depth), BF16),
            pltpu.VMEM((pairs, rows, width), F32),
        ],
        compiler_params=pltpu.CompilerParams(vmem_limit_bytes=40 * MIB),
        cost_estimate=pl.CostEstimate(flops=2 * 3 * 256 * 256 * 4800, bytes_accessed=10 * MIB, transcendentals=0),
    )(place, amp, ints, choice)


def join_body(place, a0, a1, a2, a3, keep, away):
    half = lax.div(place[2], 2)
    total = a0[...] + a1[...] + a2[...] + a3[...]
    keep[...] = jnp.where(half == 0, total[0], total[1])
    away[...] = jnp.where(half == 0, total[1], total[0])


def join(place, parts):
    one = jax.ShapeDtypeStruct(parts[0].shape[1:], F32)
    return pl.pallas_call(
        join_body,
        out_shape=(one, one),
        in_specs=[smem()] + [vmem()] * 4,
        out_specs=(vmem(), vmem()),
        cost_estimate=pl.CostEstimate(flops=1000, bytes_accessed=100000, transcendentals=0),
    )(place, *parts)


def labels_body(place, vir, occ, allowed, pair_list, occ_e, vir_e, vir_tile, cell_irrep, bound, denom, live):
    y, x, z, core = place[0], place[1], place[2], place[3]
    row = x * 2 + lax.div(z, 2)
    column = lax.rem(z, 2) * 2 + core
    groups = 8
    pair_irrep = jnp.bitwise_xor(occ[pair_list[0, 0]], occ[pair_list[0, 1]])
    a_orb = row * 128
    ga = vir[a_orb]
    gb = jnp.bitwise_xor(ga, pair_irrep)
    tile = vir_tile[...]
    count_b = jnp.int32(0)
    start_b = jnp.int32(0)
    below = jnp.int32(0)
    irrep = cell_irrep[...]
    limit = jnp.zeros(irrep.shape, jnp.int32)
    for g in range(groups):
        count = jnp.sum((tile == g).astype(jnp.int32))
        count_b = jnp.where(gb == g, count, count_b)
        start_b = jnp.where(gb == g, below, start_b)
        below = below + count
        partner = jnp.bitwise_xor(pair_irrep, g)
        kept = allowed[ga, gb, partner]
        limit = jnp.where(irrep == partner, count * kept, limit)
    lanes = bound.shape[1] // 8
    bound[...] = jnp.concatenate(
        [jnp.broadcast_to(limit[:, j : j + 1], (bound.shape[0], lanes)) for j in range(8)], axis=1
    )
    own, width = denom.shape
    slot = column * width + lax.broadcasted_iota(jnp.int32, (own, width), 1)
    line = lax.broadcasted_iota(jnp.int32, (own, width), 0)
    first = start_b + column * width
    total = vir.shape[0]

    def put(s, acc):
        orb = first + s
        value = jnp.where(orb < total, vir_e[jnp.minimum(orb, total - 1)], 0.0)
        return jnp.where(slot == column * width + s, value, acc)

    eps_b = lax.fori_loop(0, width, put, jnp.zeros((own, width), F32))
    eps_ij = jnp.zeros((own, width), F32)
    for p in range(own):
        i, j = pair_list[y * own + p, 0], pair_list[y * own + p, 1]
        eps_ij = jnp.where(line == p, occ_e[i] + occ_e[j], eps_ij)
    denom[...] = eps_ij - vir_e[a_orb] - eps_b
    live[...] = (slot < count_b).astype(jnp.int32)


def labels(place, vir, occ, allowed, pair_list, occ_e, vir_e, width, own, pairs):
    total = vir.shape[0]
    cells = vir.reshape(4, total // 32, 8)
    mine = lax.dynamic_index_in_dim(cells, place[0], 0, keepdims=False)
    return pl.pallas_call(
        labels_body,
        out_shape=(
            jax.ShapeDtypeStruct((total // 32, 8 * pairs), jnp.int32),
            jax.ShapeDtypeStruct((own, width), F32),
            jax.ShapeDtypeStruct((own, width), jnp.int32),
        ),
        in_specs=[smem()] * 7 + [vmem()] * 2,
        out_specs=(vmem(),) * 3,
        cost_estimate=pl.CostEstimate(flops=1000, bytes_accessed=2 * MIB, transcendentals=0),
    )(place, vir, occ, allowed, pair_list, occ_e, vir_e, vir.reshape(8, total // 8), mine)


STEP = 4


def ladder_body(last, base, groups, place, bound, slab, *rest):
    pieces = rest[:16]
    rest = rest[16:]
    if last:
        before, cyc0, cyc1, o0, o1, o2, o3 = rest[:7]
        rest = rest[7:]
    else:
        (out,) = rest[:1]
        rest = rest[1:]
    ints, amps, acc, final, int_sems, amp_sems = rest
    y, x, z, core = place[0], place[1], place[2], place[3]
    steps = groups // STEP

    def int_copy(s):
        return pltpu.make_async_copy(
            slab.at[:, pl.ds((base + s * STEP) * 8, STEP * 8), :], ints.at[s % 2], int_sems.at[s % 2]
        )

    def amp_copies(s, is_core):
        half = (s * STEP) // 8
        inner = (s * STEP) % 8
        out = []
        for side in range(2):
            k = is_core if side == 0 else 1 - is_core
            for g, shift in enumerate((0, 3, 1, 2)):
                source = pieces[(side * 4 + g) * 2 + half].at[pl.ds(inner, STEP)]
                if k == 0:
                    target = amps.at[s % 2, :, :, lax.rem(z + shift, 4), 0]
                else:
                    target = amps.at[s % 2, :, lax.rem(x + shift, 4), :, 1]
                out.append(pltpu.make_async_copy(source, target, amp_sems.at[s % 2, side * 4 + g]))
        return out

    def start(s):
        int_copy(s).start()
        for c in range(2):

            @pl.when(core == c)
            def _(c=c):
                for copy in amp_copies(s, c):
                    copy.start()

    def wait(s):
        int_copy(s).wait()
        for c in range(2):

            @pl.when(core == c)
            def _(c=c):
                for copy in amp_copies(s, c):
                    copy.wait()

    width = slab.shape[0]
    lanes = acc.shape[1]
    slots = slab.shape[2]
    t_of = lax.broadcasted_iota(jnp.int32, (slots, lanes), 0)
    acc[...] = jnp.zeros_like(acc)
    start(0)
    for s in range(steps):
        if s + 1 < steps:
            start(s + 1)
        wait(s)

        def one(g, carry, s=s):
            amp = amps[s % 2, g].reshape(slots, lanes)
            edge = bound[pl.ds(base + s * STEP + g, 1), :]
            high, low = split(jnp.where(t_of < edge, amp, 0.0))
            block = ints[s % 2, :, pl.ds(pl.multiple_of(g * 8, 8), 8), :].reshape(width * 8, slots)
            int_high, int_low = split(block)
            acc[...] += (
                jnp.dot(int_high, high, preferred_element_type=F32)
                + jnp.dot(int_high, low, preferred_element_type=F32)
                + jnp.dot(int_low, high, preferred_element_type=F32)
            )
            return carry

        lax.fori_loop(0, STEP, one, 0)
    pairs = lanes // 8
    shape = (width, 8, lanes)
    same = lax.broadcasted_iota(jnp.int32, shape, 1) == lax.div(lax.broadcasted_iota(jnp.int32, shape, 2), pairs)
    folded = jnp.sum(jnp.where(same, acc[...].reshape(shape), 0.0), axis=1)
    total = folded[:, :pairs]
    for j in range(1, 8):
        total = total + folded[:, j * pairs : (j + 1) * pairs]
    total = total.T
    if not last:
        out[...] = total
        return
    final[...] = total + before[...] + cyc0[...] + cyc1[...]
    own = pairs // 4
    for o, shift in ((o0, 0), (o1, 1), (o2, 3), (o3, 2)):
        o[...] = final[pl.ds(pl.multiple_of(lax.rem(y + shift, 4) * own, 8), own), :]


def ladder(place, bound, slab, pieces, base, extra=None):
    last = extra is not None
    width, cells, slots = slab.shape
    groups = 2 * pieces[0].shape[0]
    lanes = pieces[0].shape[3]
    pairs = lanes // 8
    if last:
        out_shape = (jax.ShapeDtypeStruct((pairs // 4, width), F32),) * 4
        out_specs = (vmem(),) * 4
    else:
        out_shape = jax.ShapeDtypeStruct((pairs, width), F32)
        out_specs = vmem()
        extra = ()
    return pl.pallas_call(
        functools.partial(ladder_body, last, base, groups),
        out_shape=out_shape,
        in_specs=[smem(), vmem(), hbm()] + [hbm()] * 16 + [vmem()] * len(extra),
        out_specs=out_specs,
        scratch_shapes=[
            pltpu.VMEM((2, width, STEP * 8, slots), F32),
            pltpu.VMEM((2, STEP, 4, 4, 2, 8, lanes), F32),
            pltpu.VMEM((width * 8, lanes), F32),
            pltpu.VMEM((pairs, width), F32),
            pltpu.SemaphoreType.DMA((2,)),
            pltpu.SemaphoreType.DMA((2, 8)),
        ],
        compiler_params=pltpu.CompilerParams(vmem_limit_bytes=40 * MIB),
        cost_estimate=pl.CostEstimate(
            flops=2 * 3 * groups * width * 8 * slots * lanes, bytes_accessed=groups * MIB // 2, transcendentals=0
        ),
    )(place, bound, slab, *pieces, *extra)


def on_device(vir, occ, allowed, pair_list, occ_e, vir_e, ladder_amp, int_slab, cycle_amp, cycle_int):
    row, column = lax.axis_index("row"), lax.axis_index("column")
    place = jnp.stack(
        [lax.axis_index("depth"), row // 2, (row % 2) * 2 + column // 2, column % 2]
    ).astype(jnp.int32)
    pairs = ladder_amp.shape[0]
    width = int_slab.shape[1]
    own = pairs // 4

    mine = relayout(jnp.transpose(ladder_amp, (0, 2, 1)))
    blocks = [mine] + [send(mine, FIRST[n]) for n in (1, -1, 2)]
    quarters = stack(place, blocks)
    below = [send(q, SECOND[1]) for q in quarters]
    above = [send(q, SECOND[-1]) for q in quarters]
    across = [send(below[i], SECOND[1]) if i % 2 == 0 else send(above[i], SECOND[-1]) for i in range(4)]

    bound, denom, live = labels(place, vir, occ, allowed, pair_list, occ_e, vir_e, width, own, pairs)
    choice = (pair_list[:, 1:] == jnp.arange(cycle_int.shape[1], dtype=jnp.int32)).astype(F32)
    choice = jnp.repeat(choice, cycle_amp.shape[1], axis=0)
    c0, c1, c2, c3 = cycle(place, cycle_amp, jnp.transpose(cycle_int, (1, 2, 0)), choice)
    keep, away = join(place, (c0, send(c1, ALONG_X[1]), send(c2, ALONG_X[-1]), send(c3, ALONG_X[2])))
    got = send(away, Z_ACROSS)

    slab = int_slab.reshape(int_slab.shape[1:])
    held = []
    for i in range(4):
        held.append([quarters[i], below[i], above[i], across[i]])
    other = [[send(v, SWAP) for v in h] for h in held]
    sums = None
    for half in range(2):
        pieces = []
        for side in (held, other):
            for g in range(4):
                pieces += [side[2 * half][g], side[2 * half + 1][g]]
        extra = (sums, keep, got) if half else None
        sums = ladder(place, bound, slab, pieces, half * 16, extra)
    s0, s1, s2, s3 = sums
    total = s0 + send(s1, ALONG_Y[1]) + send(s2, ALONG_Y[-1]) + send(s3, ALONG_Y[2])
    return jnp.where(live > 0, total / denom, jnp.float32(0.0))[None]


def solution(mesh):
    return jax.shard_map(
        on_device,
        mesh=mesh,
        in_specs=(
            P(),
            P(),
            P(),
            P(),
            P(),
            P(),
            P(None, "depth", ("row", "column")),
            P("row", "column", "depth", None),
            P(None, None, ("depth", "row")),
            P(("depth", "row"), None, "column"),
        ),
        out_specs=P("row", "depth", "column"),
        check_vma=False,
    )
```

time: 371 us -> 155 us (0.42)
  waiting for transfers between devices: 263 us -> 23.3 us
  Pallas kernels: 0 us -> 71.2 us
  matrix products: 42 us -> 0 us
  starting transfers between devices: 0.08 us -> 38.3 us
  between operations: 17.5 us -> 0.26 us
  blocking collectives: 16.8 us -> 0 us
  other arithmetic: 17.3 us -> 1.34 us
  local copies, waits for them, and re-layouts: 13.7 us -> 20 us
    unnamed x3 -> x0, waiting for transfers between devices: 224 us -> none
    pallas_call x0 -> x7, Pallas kernels: none -> 71.2 us  [the longest x1 33.7 us: stack(): pl.pallas_call(stack_body, out_shape=(quarter,) * 4, in_specs=[smem()] +...]
    dot_general x5 -> x0, matrix products: 42 us -> none  [the longest x1 29.7 us: on_device(): jnp.einsum('apcd,abcd->apb', weights, int_slab, precision=lax.Precision.H...]
    all_gather x1 -> x0, waiting for transfers between devices: 38.7 us -> none  [on_device(): full_amp = lax.all_gather(ladder_amp, ('row', 'column'), axis=2, tiled=True)]
    ppermute x0 -> x38, starting transfers between devices: none -> 38.3 us  [send(): return lax.ppermute(value, AXES, pairs)]
    ppermute x0 -> x38, waiting for transfers between devices: none -> 23.3 us  [send(): return lax.ppermute(value, AXES, pairs)]
    unnamed x18 -> x71, local copies, waits for them, and re-layouts: 1.22 us -> 18.6 us
    unnamed x1 -> x0, blocking collectives: 16.8 us -> none
  transfers between devices with their start and end apart: 2 -> 38, of which waited for: 2 -> 11; matrix products, arithmetic and copies ran while one was open for 19% -> 2% of each run, Pallas kernels for 0% -> 17%
where the time goes in v1:
time: 155 us; the launch traced here: 154 us
  Pallas kernels  71.2 us (46%)
  starting transfers between devices  38.3 us (25%)
  waiting for transfers between devices  23.3 us (15%)
  local copies, waits for them, and re-layouts  20 us (13%)
    ppermute x38, starting transfers between devices, send(): return lax.ppermute(value, AXES, pairs)  38.3 us
    pallas_call x1, Pallas kernels, stack(): pl.pallas_call(stack_body, out_shape=(quarter,) * 4, in_specs=[smem()] +...  33.7 us
    ppermute x38, waiting for transfers between devices, send(): return lax.ppermute(value, AXES, pairs)  23.3 us
    pallas_call x2, Pallas kernels, ladder(): pl.pallas_call(functools.partial(ladder_body, last, base, groups), out_sh...  19.5 us
    unnamed x71, local copies, waits for them, and re-layouts  18.6 us
    pallas_call x1, Pallas kernels, cycle(): pl.pallas_call(cycle_body, grid=(steps,), out_shape=(part,) * 4, in_specs...  11.3 us
  transfers between devices with their start and end apart: 38, of which 11 were waited for; matrix products, arithmetic and copies ran while one was open for 2% of the time, Pallas kernels for 17%

profile of v1, /device:TPU:0, one launch (start us, length us, event | category | flops | bytes accessed | tf_op | source)
XLA Modules:
  0.0 154.5 jit_solution(16363081200835555760)
XLA Ops:
  0.0 2.2 %shard_map.101.b0 = f32[32,8,256]{2,1,0:T(8,128)} custom-call(f32[32,8,256]{2,1,0:T(8,128)} %bitcast.19), custom_call_target="tpu_custom_call" | custom-call | flops 1000 | bytes 2097152 | tf_op jit(solution)/shard_map/pallas_call | solution.py:79
  2.2 1.6 %collective-permute-start = (f32[32,8,256]{2,1,0:T(8,128)}, f32[32,8,256]{2,1,0:T(8,128)S(1)}, u32[]{:S(2)}, u32[]{:S(2)}) collective-permute-start(f32[32,8,256]{2,1,0:T(8,128)} %shard_map.101.b0), channel_id=1, source_target_pairs={{0,8},{1,3},{2,10},{3,5},{4,12},{5,7},{6,14},{7,1},{8,16},{9,11},{... | collective-permute-start | bytes 786440 | tf_op jit(solution)/shard_map/ppermute | solution.py:52
  3.8 1.7 %collective-permute-start.1 = (f32[32,8,256]{2,1,0:T(8,128)}, f32[32,8,256]{2,1,0:T(8,128)S(1)}, u32[]{:S(2)}, u32[]{:S(2)}) collective-permute-start(f32[32,8,256]{2,1,0:T(8,128)} %shard_map.101.b0), channel_id=1, source_target_pairs={{0,24},{1,7},{2,26},{3,1},{4,28},{5,3},{6,30},{7,5},{8,0},{9,15},{... | collective-permute-start | bytes 786440 | tf_op jit(solution)/shard_map/ppermute | solution.py:52
  5.5 1.9 %collective-permute-start.2 = (f32[32,8,256]{2,1,0:T(8,128)}, f32[32,8,256]{2,1,0:T(8,128)S(1)}, u32[]{:S(2)}, u32[]{:S(2)}) collective-permute-start(f32[32,8,256]{2,1,0:T(8,128)} %shard_map.101.b0), channel_id=1, source_target_pairs={{0,16},{1,5},{2,18},{3,7},{4,20},{5,1},{6,22},{7,3},{8,24},{9,13},... | collective-permute-start | bytes 786440 | tf_op jit(solution)/shard_map/ppermute | solution.py:52
  7.4 0.7 slice_bitcast_fusion
  8.8 1.2 collective-permute-done.b1
  10.4 3.5 %collective-permute-done.2.b3 = f32[32,8,256]{2,1,0:T(8,128)S(1)} collective-permute-done((f32[32,8,256]{2,1,0:T(8,128)}, f32[32,8,256]{2,1,0:T(8,128)S(1)}, u32[]{:S(2)}, u32[]{:S(2)}) %collective-permute-start.2) | collective-permute-done | bytes 262176 | tf_op jit(solution)/shard_map/ppermute | solution.py:52
  13.9 0.7 copy-done.27
  14.6 33.7 %shard_map.102 = (f32[8,4,8,256]{3,2,1,0:T(8,128)}, f32[8,4,8,256]{3,2,1,0:T(8,128)}, f32[8,4,8,256]{3,2,1,0:T(8,128)}, f32[8,4,8,256]{3,2,1,0:T(8,128)}) custom-call(s32[4]{0:T(128)} %pad_add_fusion.place, f32[32,8,256]{2,1,0:T(8,128)} %shard_map.101.b0, f32[32,8,256]{2,1,0:T(8,128)} %copy-done.25, f32[32,8,256]{2,1,0:T(8,128)} %copy-done.26, ...), custom_call_target="tpu_custom_call" | custom-call | flops 1000 | bytes 4194304 | tf_op jit(solution)/shard_map/pallas_call | solution.py:106
  48.3 4.1 %collective-permute-start.20 = (f32[8,4,8,256]{3,2,1,0:T(8,128)}, f32[8,4,8,256]{3,2,1,0:T(8,128)S(1)}, u32[]{:S(2)}, u32[]{:S(2)}) collective-permute-start(f32[8,4,8,256]{3,2,1,0:T(8,128)} %get-tuple-element.27.rest_1_), channel_id=1, source_target_pairs={{0,6},{1,25},{2,0},{3,27},{4,2},{5,29},{6,4},{7,31},{8,14},{9,1},{... | collective-permute-start | bytes 786440 | tf_op jit(solution)/shard_map/ppermute | solution.py:52
  52.5 2.4 %copy-done = f32[32,8,4800]{2,1,0:T(8,128)S(1)} copy-done((f32[32,8,4800]{2,1,0:T(8,128)S(1)}, f32[32,8,4800]{2,1,0:T(8,128)}, u32[]{:S(2)}) %copy-start) | copy-done | bytes 4915224
  54.9 2.4 %copy-done.1 = f32[4800,4,64]{0,2,1:T(8,128)S(1)} copy-done((f32[4800,4,64]{0,2,1:T(8,128)S(1)}, f32[4800,4,64]{0,2,1:T(8,128)}, u32[]{:S(2)}) %copy-start.1) | copy-done | bytes 4915224
  58.0 11.3 %shard_map.104 = (f32[2,32,64]{2,1,0:T(8,128)S(1)}, f32[2,32,64]{2,1,0:T(8,128)S(1)}, f32[2,32,64]{2,1,0:T(8,128)S(1)}, f32[2,32,64]{2,1,0:T(8,128)S(1)}) custom-call(s32[4]{0:T(128)S(1)} %copy-done.22, f32[32,8,4800]{2,1,0:T(8,128)S(1)} %copy-done, f32[4,64,4800]{2,1,0:T(8,128)S(1)} %bitcast.16, f32[256,4]{1,0:T(8,128)S(1)} %broadcast_bitcast_fusion.choice_ref), custom_call_target="tpu_custom_call" | custom-call | flops 1887436800 | bytes 10485760 | tf_op jit(solution)/shard_map/pallas_call | solution.py:166
  69.9 1.4 collective-permute-start.31
  71.4 1.8 %collective-permute-start.32 = (f32[2,32,64]{2,1,0:T(8,128)S(1)}, f32[2,32,64]{2,1,0:T(8,128)S(1)}, u32[]{:S(2)}, u32[]{:S(2)}) collective-permute-start(f32[2,32,64]{2,1,0:T(8,128)S(1)} %get-tuple-element.30), channel_id=1, source_target_pairs={{0,24},{1,25},{2,26},{3,27},{4,28},{5,29},{6,30},{7,31},{8,0},{9,1... | collective-permute-start | bytes 49160 | tf_op jit(solution)/shard_map/ppermute | solution.py:52
  73.2 1.9 %collective-permute-done.31.a1 = f32[2,32,64]{2,1,0:T(8,128)S(1)} collective-permute-done((f32[2,32,64]{2,1,0:T(8,128)S(1)}, f32[2,32,64]{2,1,0:T(8,128)S(1)}, u32[]{:S(2)}, u32[]{:S(2)}) %collective-permute-start.31) | collective-permute-done | bytes 16416 | tf_op jit(solution)/shard_map/ppermute | solution.py:52
  75.1 0.9 collective-permute-start.33
  76.0 4.5 %collective-permute-done.33.a3 = f32[2,32,64]{2,1,0:T(8,128)S(1)} collective-permute-done((f32[2,32,64]{2,1,0:T(8,128)S(1)}, f32[2,32,64]{2,1,0:T(8,128)S(1)}, u32[]{:S(2)}, u32[]{:S(2)}) %collective-permute-start.33) | collective-permute-done | bytes 16416 | tf_op jit(solution)/shard_map/ppermute | solution.py:52
  81.1 1.4 shard_map.105
  82.5 4.7 %collective-permute-start.34 = (f32[32,64]{1,0:T(8,128)}, f32[32,64]{1,0:T(8,128)S(1)}, u32[]{:S(2)}, u32[]{:S(2)}) collective-permute-start(f32[32,64]{1,0:T(8,128)} %get-tuple-element.33), channel_id=1, source_target_pairs={{0,4},{1,5},{2,6},{3,7},{4,0},{5,1},{6,2},{7,3},{8,12},{9,13},{10,... | collective-permute-start | bytes 24584 | tf_op jit(solution)/shard_map/ppermute | solution.py:52
  87.2 1.9 %collective-permute-done.34.rest_18_ = f32[32,64]{1,0:T(8,128)S(1)} collective-permute-done((f32[32,64]{1,0:T(8,128)}, f32[32,64]{1,0:T(8,128)S(1)}, u32[]{:S(2)}, u32[]{:S(2)}) %collective-permute-start.34) | collective-permute-done | bytes 8224 | tf_op jit(solution)/shard_map/ppermute | solution.py:52
  90.3 2.6 %collective-permute-start.6 = (f32[8,4,8,256]{3,2,1,0:T(8,128)S(1)}, f32[8,4,8,256]{3,2,1,0:T(8,128)S(1)}, u32[]{:S(2)}, u32[]{:S(2)}) collective-permute-start(f32[8,4,8,256]{3,2,1,0:T(8,128)S(1)} %copy-done.3), channel_id=1, source_target_pairs={{0,6},{1,25},{2,0},{3,27},{4,2},{5,29},{6,4},{7,31},{8,14},{9,1},{... | collective-permute-start | bytes 786440 | tf_op jit(solution)/shard_map/ppermute | solution.py:52
  93.6 3.2 %collective-permute-start.5 = (f32[8,4,8,256]{3,2,1,0:T(8,128)S(1)}, f32[8,4,8,256]{3,2,1,0:T(8,128)S(1)}, u32[]{:S(2)}, u32[]{:S(2)}) collective-permute-start(f32[8,4,8,256]{3,2,1,0:T(8,128)S(1)} %copy-done.2), channel_id=1, source_target_pairs={{0,6},{1,25},{2,0},{3,27},{4,2},{5,29},{6,4},{7,31},{8,14},{9,1},{... | collective-permute-start | bytes 786440 | tf_op jit(solution)/shard_map/ppermute | solution.py:52
  96.8 0.7 copy-done.8
  98.1 1.5 collective-permute-start.21
  99.5 1.6 %collective-permute-done.4.rest_3_ = f32[8,4,8,256]{3,2,1,0:T(8,128)S(1)} collective-permute-done((f32[8,4,8,256]{3,2,1,0:T(8,128)S(1)}, f32[8,4,8,256]{3,2,1,0:T(8,128)S(1)}, u32[]{:S(2)}, u32[]{:S(2)}) %collective-permute-start.4) | collective-permute-done | bytes 262176 | tf_op jit(solution)/shard_map/ppermute | solution.py:52
  101.3 0.7 copy-done.6
  102.6 0.7 copy-done.10
  103.3 2.5 %collective-permute-done.21.rest_6_ = f32[8,4,8,256]{3,2,1,0:T(8,128)} collective-permute-done((f32[8,4,8,256]{3,2,1,0:T(8,128)S(1)}, f32[8,4,8,256]{3,2,1,0:T(8,128)}, u32[]{:S(2)}, u32[]{:S(2)}) %collective-permute-start.21) | collective-permute-done | bytes 262176 | tf_op jit(solution)/shard_map/ppermute | solution.py:52
  105.8 1.9 %collective-permute-done.22.rest_7_ = f32[8,4,8,256]{3,2,1,0:T(8,128)} collective-permute-done((f32[8,4,8,256]{3,2,1,0:T(8,128)S(1)}, f32[8,4,8,256]{3,2,1,0:T(8,128)}, u32[]{:S(2)}, u32[]{:S(2)}) %collective-permute-start.22) | collective-permute-done | bytes 262176 | tf_op jit(solution)/shard_map/ppermute | solution.py:52
  107.7 0.7 copy-done.12
  108.4 3.2 %collective-permute-start.8 = (f32[8,4,8,256]{3,2,1,0:T(8,128)S(1)}, f32[8,4,8,256]{3,2,1,0:T(8,128)}, u32[]{:S(2)}, u32[]{:S(2)}) collective-permute-start(f32[8,4,8,256]{3,2,1,0:T(8,128)S(1)} %collective-permute-done.6.rest_5_), channel_id=1, source_target_pairs={{0,6},{1,25},{2,0},{3,27},{4,2},{5,29},{6,4},{7,31},{8,14},{9,1},{... | collective-permute-start | bytes 786440 | tf_op jit(solution)/shard_map/ppermute | solution.py:52
  112.3 0.7 copy-done.16
  113.5 0.7 copy-done.18
  114.2 0.7 copy.12.pair_list
  115.6 3.1 %shard_map.100 = (s32[32,256]{1,0:T(8,128)}, f32[8,64]{1,0:T(8,128)}, s32[8,64]{1,0:T(8,128)}) custom-call(s32[4]{0:T(128)} %pad_add_fusion.place, s32[1024]{0:T(1024)} %vir.1, s32[150]{0:T(256)} %occ.1, s32[8,8,8]{2,1,0:T(8,128)} %allowed.1, s32[32,2]{1,0:T(8,128)} %copy.12.pair_list, f32[150]{0:T(256)} %occ_e.1, f32[1024]{0:T(1024)} %vir_e.1, ...), custom_call_target="tpu_custom_call" | custom-call | flops 1000 | bytes 2097152 | tf_op jit(solution)/shard_map/pallas_call | solution.py:256
  120.3 0.9 copy-done.9
  121.3 0.9 copy-done.13
  122.2 0.9 copy-done.15
  123.2 0.9 copy-done.17
  124.1 0.9 copy-done.19
  125.1 0.8 copy-done.20
  125.8 9.7 %shard_map.103.rest_16_ = f32[32,64]{1,0:T(8,128)S(1)} custom-call(s32[4]{0:T(128)S(1)} %copy-done.23, s32[32,256]{1,0:T(8,128)S(1)} %copy-done.20, f32[64,256,256]{2,1,0:T(8,128)} %bitcast.17, f32[8,4,8,256]{3,2,1,0:T(8,128)S(1)} %copy-done.4, f32[8,4,8,256]{3,2,1,0:T(8,128)S(1)} %copy-done.5, f32[8,4,8,256]{3,2,1,0:T(8,128)S(1)} %collective-permute-done.17.rest_2_, ...), custom_call_target="tpu_custom_call" | custom-call | flops 3221225472 | bytes 8388608 | tf_op jit(solution)/shard_map/pallas_call | solution.py:378
  135.7 9.8 %shard_map.106 = (f32[8,64]{1,0:T(8,128)S(1)}, f32[8,64]{1,0:T(8,128)S(1)}, f32[8,64]{1,0:T(8,128)S(1)}, f32[8,64]{1,0:T(8,128)S(1)}) custom-call(s32[4]{0:T(128)S(1)} %copy-done.23, s32[32,256]{1,0:T(8,128)S(1)} %copy-done.20, f32[64,256,256]{2,1,0:T(8,128)} %bitcast.18, f32[8,4,8,256]{3,2,1,0:T(8,128)S(1)} %copy-done.2, f32[8,4,8,256]{3,2,1,0:T(8,128)S(1)} %copy-done.3, ...), custom_call_target="tpu_custom_call" | custom-call | flops 3221225472 | bytes 8388608 | tf_op jit(solution)/shard_map/pallas_call | solution.py:378
  145.4 1.6 %collective-permute-start.35 = (f32[8,64]{1,0:T(8,128)S(1)}, f32[8,64]{1,0:T(8,128)S(1)}, u32[]{:S(2)}, u32[]{:S(2)}) collective-permute-start(f32[8,64]{1,0:T(8,128)S(1)} %get-tuple-element.35), channel_id=1, source_target_pairs={{0,32},{1,33},{2,34},{3,35},{4,36},{5,37},{6,38},{7,39},{8,40},{9,... | collective-permute-start | bytes 6152 | tf_op jit(solution)/shard_map/ppermute | solution.py:52
  147.1 1.7 %collective-permute-start.36 = (f32[8,64]{1,0:T(8,128)S(1)}, f32[8,64]{1,0:T(8,128)S(1)}, u32[]{:S(2)}, u32[]{:S(2)}) collective-permute-start(f32[8,64]{1,0:T(8,128)S(1)} %get-tuple-element.36), channel_id=1, source_target_pairs={{0,96},{1,97},{2,98},{3,99},{4,100},{5,101},{6,102},{7,103},{8,104... | collective-permute-start | bytes 6152 | tf_op jit(solution)/shard_map/ppermute | solution.py:52
  148.7 2.0 %collective-permute-start.37 = (f32[8,64]{1,0:T(8,128)S(1)}, f32[8,64]{1,0:T(8,128)S(1)}, u32[]{:S(2)}, u32[]{:S(2)}) collective-permute-start(f32[8,64]{1,0:T(8,128)S(1)} %get-tuple-element.37), channel_id=1, source_target_pairs={{0,64},{1,65},{2,66},{3,67},{4,68},{5,69},{6,70},{7,71},{8,72},{9,... | collective-permute-start | bytes 6152 | tf_op jit(solution)/shard_map/ppermute | solution.py:52
  150.7 3.1 %collective-permute-done.37 = f32[8,64]{1,0:T(8,128)S(1)} collective-permute-done((f32[8,64]{1,0:T(8,128)S(1)}, f32[8,64]{1,0:T(8,128)S(1)}, u32[]{:S(2)}, u32[]{:S(2)}) %collective-permute-start.37) | collective-permute-done | bytes 2080 | tf_op jit(solution)/shard_map/ppermute | solution.py:52
  (113 shorter events, 10.3 us)
Async XLA Ops:
  2.2 7.8 %collective-permute-start = (f32[32,8,256]{2,1,0:T(8,128)}, f32[32,8,256]{2,1,0:T(8,128)S(1)}, u32[]{:S(2)}, u32[]{:S(2)}) collective-permute-start(f32[32,8,256]{2,1,0:T(8,128)} %shard_map.101.b0), channel_id=1, source_target_pairs={{0,8},{1,3},{2,10},{3,5},{4,12},{5,7},{6,14},{7,1},{8,16},{9,11},{... | collective-permute-start | bytes 786440 | tf_op jit(solution)/shard_map/ppermute | solution.py:52
  3.8 6.6 %collective-permute-start.1 = (f32[32,8,256]{2,1,0:T(8,128)}, f32[32,8,256]{2,1,0:T(8,128)S(1)}, u32[]{:S(2)}, u32[]{:S(2)}) collective-permute-start(f32[32,8,256]{2,1,0:T(8,128)} %shard_map.101.b0), channel_id=1, source_target_pairs={{0,24},{1,7},{2,26},{3,1},{4,28},{5,3},{6,30},{7,5},{8,0},{9,15},{... | collective-permute-start | bytes 786440 | tf_op jit(solution)/shard_map/ppermute | solution.py:52
  5.5 8.4 %collective-permute-start.2 = (f32[32,8,256]{2,1,0:T(8,128)}, f32[32,8,256]{2,1,0:T(8,128)S(1)}, u32[]{:S(2)}, u32[]{:S(2)}) collective-permute-start(f32[32,8,256]{2,1,0:T(8,128)} %shard_map.101.b0), channel_id=1, source_target_pairs={{0,16},{1,5},{2,18},{3,7},{4,20},{5,1},{6,22},{7,3},{8,24},{9,13},... | collective-permute-start | bytes 786440 | tf_op jit(solution)/shard_map/ppermute | solution.py:52
  48.3 41.4 %collective-permute-start.20 = (f32[8,4,8,256]{3,2,1,0:T(8,128)}, f32[8,4,8,256]{3,2,1,0:T(8,128)S(1)}, u32[]{:S(2)}, u32[]{:S(2)}) collective-permute-start(f32[8,4,8,256]{3,2,1,0:T(8,128)} %get-tuple-element.27.rest_1_), channel_id=1, source_target_pairs={{0,6},{1,25},{2,0},{3,27},{4,2},{5,29},{6,4},{7,31},{8,14},{9,1},{... | collective-permute-start | bytes 786440 | tf_op jit(solution)/shard_map/ppermute | solution.py:52
  52.4 37.9 %collective-permute-start.18 = (f32[8,4,8,256]{3,2,1,0:T(8,128)}, f32[8,4,8,256]{3,2,1,0:T(8,128)S(1)}, u32[]{:S(2)}, u32[]{:S(2)}) collective-permute-start(f32[8,4,8,256]{3,2,1,0:T(8,128)} %get-tuple-element.27.rest_1_), channel_id=1, source_target_pairs={{0,2},{1,9},{2,4},{3,11},{4,6},{5,13},{6,0},{7,15},{8,10},{9,17},{... | collective-permute-start | bytes 786440 | tf_op jit(solution)/shard_map/ppermute | solution.py:52
  52.4 36.7 %collective-permute-start.17 = (f32[8,4,8,256]{3,2,1,0:T(8,128)}, f32[8,4,8,256]{3,2,1,0:T(8,128)S(1)}, u32[]{:S(2)}, u32[]{:S(2)}) collective-permute-start(f32[8,4,8,256]{3,2,1,0:T(8,128)} %get-tuple-element.26.rest_0_), channel_id=1, source_target_pairs={{0,2},{1,9},{2,4},{3,11},{4,6},{5,13},{6,0},{7,15},{8,10},{9,17},{... | collective-permute-start | bytes 786440 | tf_op jit(solution)/shard_map/ppermute | solution.py:52
  58.0 29.3 %copy-start.4 = (f32[8,4,8,256]{3,2,1,0:T(8,128)S(1)}, f32[8,4,8,256]{3,2,1,0:T(8,128)}, u32[]{:S(2)}) copy-start(f32[8,4,8,256]{3,2,1,0:T(8,128)} %get-tuple-element.26.rest_0_) | copy-start | bytes 786436
  58.0 31.2 %copy-start.5 = (f32[8,4,8,256]{3,2,1,0:T(8,128)S(1)}, f32[8,4,8,256]{3,2,1,0:T(8,128)}, u32[]{:S(2)}) copy-start(f32[8,4,8,256]{3,2,1,0:T(8,128)} %get-tuple-element.27.rest_1_) | copy-start | bytes 786436
  58.0 31.7 %copy-start.2 = (f32[8,4,8,256]{3,2,1,0:T(8,128)S(1)}, f32[8,4,8,256]{3,2,1,0:T(8,128)}, u32[]{:S(2)}) copy-start(f32[8,4,8,256]{3,2,1,0:T(8,128)} %get-tuple-element.24.rest_0_) | copy-start | bytes 786436
  58.0 32.4 %copy-start.3 = (f32[8,4,8,256]{3,2,1,0:T(8,128)S(1)}, f32[8,4,8,256]{3,2,1,0:T(8,128)}, u32[]{:S(2)}) copy-start(f32[8,4,8,256]{3,2,1,0:T(8,128)} %get-tuple-element.25.rest_1_) | copy-start | bytes 786436
  58.0 56.3 %copy-start.34 = (s32[32,2]{0,1:T(2,128)S(1)}, s32[32,2]{0,1:T(2,128)}, u32[]{:S(2)}) copy-start(s32[32,2]{0,1:T(2,128)} %param.13) | copy-start | bytes 772
  58.0 56.9 %copy-start.28 = (s32[1024]{0:T(1024)S(1)}, s32[1024]{0:T(1024)}, u32[]{:S(2)}) copy-start(s32[1024]{0:T(1024)} %vir.1) | copy-start | bytes 12292
  58.0 62.3 %copy-start.23 = (s32[4]{0:T(128)S(1)}, s32[4]{0:T(128)}, u32[]{:S(2)}) copy-start(s32[4]{0:T(128)} %pad_add_fusion.place) | copy-start | bytes 52
  69.9 5.1 %collective-permute-start.31 = (f32[2,32,64]{2,1,0:T(8,128)S(1)}, f32[2,32,64]{2,1,0:T(8,128)S(1)}, u32[]{:S(2)}, u32[]{:S(2)}) collective-permute-start(f32[2,32,64]{2,1,0:T(8,128)S(1)} %get-tuple-element.29), channel_id=1, source_target_pairs={{0,8},{1,9},{2,10},{3,11},{4,12},{5,13},{6,14},{7,15},{8,16},{9,17... | collective-permute-start | bytes 49160 | tf_op jit(solution)/shard_map/ppermute | solution.py:52
  71.4 4.6 %collective-permute-start.32 = (f32[2,32,64]{2,1,0:T(8,128)S(1)}, f32[2,32,64]{2,1,0:T(8,128)S(1)}, u32[]{:S(2)}, u32[]{:S(2)}) collective-permute-start(f32[2,32,64]{2,1,0:T(8,128)S(1)} %get-tuple-element.30), channel_id=1, source_target_pairs={{0,24},{1,25},{2,26},{3,27},{4,28},{5,29},{6,30},{7,31},{8,0},{9,1... | collective-permute-start | bytes 49160 | tf_op jit(solution)/shard_map/ppermute | solution.py:52
  75.1 5.4 %collective-permute-start.33 = (f32[2,32,64]{2,1,0:T(8,128)S(1)}, f32[2,32,64]{2,1,0:T(8,128)S(1)}, u32[]{:S(2)}, u32[]{:S(2)}) collective-permute-start(f32[2,32,64]{2,1,0:T(8,128)S(1)} %get-tuple-element.31), channel_id=1, source_target_pairs={{0,16},{1,17},{2,18},{3,19},{4,20},{5,21},{6,22},{7,23},{8,24},{9,... | collective-permute-start | bytes 49160 | tf_op jit(solution)/shard_map/ppermute | solution.py:52
  82.5 6.6 %collective-permute-start.34 = (f32[32,64]{1,0:T(8,128)}, f32[32,64]{1,0:T(8,128)S(1)}, u32[]{:S(2)}, u32[]{:S(2)}) collective-permute-start(f32[32,64]{1,0:T(8,128)} %get-tuple-element.33), channel_id=1, source_target_pairs={{0,4},{1,5},{2,6},{3,7},{4,0},{5,1},{6,2},{7,3},{8,12},{9,13},{10,... | collective-permute-start | bytes 24584 | tf_op jit(solution)/shard_map/ppermute | solution.py:52
  87.2 6.4 %collective-permute-start.19 = (f32[8,4,8,256]{3,2,1,0:T(8,128)S(1)}, f32[8,4,8,256]{3,2,1,0:T(8,128)S(1)}, u32[]{:S(2)}, u32[]{:S(2)}) collective-permute-start(f32[8,4,8,256]{3,2,1,0:T(8,128)S(1)} %copy-done.4), channel_id=1, source_target_pairs={{0,6},{1,25},{2,0},{3,27},{4,2},{5,29},{6,4},{7,31},{8,14},{9,1},{... | collective-permute-start | bytes 786440 | tf_op jit(solution)/shard_map/ppermute | solution.py:52
  89.2 4.5 %collective-permute-start.23 = (f32[8,4,8,256]{3,2,1,0:T(8,128)S(1)}, f32[8,4,8,256]{3,2,1,0:T(8,128)S(1)}, u32[]{:S(2)}, u32[]{:S(2)}) collective-permute-start(f32[8,4,8,256]{3,2,1,0:T(8,128)S(1)} %copy-done.4), channel_id=1, source_target_pairs={{0,1},{1,0},{2,3},{3,2},{4,5},{5,4},{6,7},{7,6},{8,9},{9,8},{10,11... | collective-permute-start | bytes 786440 | tf_op jit(solution)/shard_map/ppermute | solution.py:52
  89.2 7.7 %collective-permute-start.24 = (f32[8,4,8,256]{3,2,1,0:T(8,128)S(1)}, f32[8,4,8,256]{3,2,1,0:T(8,128)S(1)}, u32[]{:S(2)}, u32[]{:S(2)}) collective-permute-start(f32[8,4,8,256]{3,2,1,0:T(8,128)S(1)} %copy-done.5), channel_id=1, source_target_pairs={{0,1},{1,0},{2,3},{3,2},{4,5},{5,4},{6,7},{7,6},{8,9},{9,8},{10,11... | collective-permute-start | bytes 786440 | tf_op jit(solution)/shard_map/ppermute | solution.py:52
  89.7 7.9 %collective-permute-start.3 = (f32[8,4,8,256]{3,2,1,0:T(8,128)S(1)}, f32[8,4,8,256]{3,2,1,0:T(8,128)S(1)}, u32[]{:S(2)}, u32[]{:S(2)}) collective-permute-start(f32[8,4,8,256]{3,2,1,0:T(8,128)S(1)} %copy-done.2), channel_id=1, source_target_pairs={{0,2},{1,9},{2,4},{3,11},{4,6},{5,13},{6,0},{7,15},{8,10},{9,17},{... | collective-permute-start | bytes 786440 | tf_op jit(solution)/shard_map/ppermute | solution.py:52
  90.3 7.7 %collective-permute-start.6 = (f32[8,4,8,256]{3,2,1,0:T(8,128)S(1)}, f32[8,4,8,256]{3,2,1,0:T(8,128)S(1)}, u32[]{:S(2)}, u32[]{:S(2)}) collective-permute-start(f32[8,4,8,256]{3,2,1,0:T(8,128)S(1)} %copy-done.3), channel_id=1, source_target_pairs={{0,6},{1,25},{2,0},{3,27},{4,2},{5,29},{6,4},{7,31},{8,14},{9,1},{... | collective-permute-start | bytes 786440 | tf_op jit(solution)/shard_map/ppermute | solution.py:52
  93.6 7.6 %collective-permute-start.4 = (f32[8,4,8,256]{3,2,1,0:T(8,128)S(1)}, f32[8,4,8,256]{3,2,1,0:T(8,128)S(1)}, u32[]{:S(2)}, u32[]{:S(2)}) collective-permute-start(f32[8,4,8,256]{3,2,1,0:T(8,128)S(1)} %copy-done.3), channel_id=1, source_target_pairs={{0,2},{1,9},{2,4},{3,11},{4,6},{5,13},{6,0},{7,15},{8,10},{9,17},{... | collective-permute-start | bytes 786440 | tf_op jit(solution)/shard_map/ppermute | solution.py:52
  93.6 7.7 %collective-permute-start.5 = (f32[8,4,8,256]{3,2,1,0:T(8,128)S(1)}, f32[8,4,8,256]{3,2,1,0:T(8,128)S(1)}, u32[]{:S(2)}, u32[]{:S(2)}) collective-permute-start(f32[8,4,8,256]{3,2,1,0:T(8,128)S(1)} %copy-done.2), channel_id=1, source_target_pairs={{0,6},{1,25},{2,0},{3,27},{4,2},{5,29},{6,4},{7,31},{8,14},{9,1},{... | collective-permute-start | bytes 786440 | tf_op jit(solution)/shard_map/ppermute | solution.py:52
  97.6 3.8 %collective-permute-start.10 = (f32[8,4,8,256]{3,2,1,0:T(8,128)S(1)}, f32[8,4,8,256]{3,2,1,0:T(8,128)S(1)}, u32[]{:S(2)}, u32[]{:S(2)}) collective-permute-start(f32[8,4,8,256]{3,2,1,0:T(8,128)S(1)} %copy-done.3), channel_id=1, source_target_pairs={{0,1},{1,0},{2,3},{3,2},{4,5},{5,4},{6,7},{7,6},{8,9},{9,8},{10,11... | collective-permute-start | bytes 786440 | tf_op jit(solution)/shard_map/ppermute | solution.py:52
  97.6 5.0 %collective-permute-start.9 = (f32[8,4,8,256]{3,2,1,0:T(8,128)S(1)}, f32[8,4,8,256]{3,2,1,0:T(8,128)S(1)}, u32[]{:S(2)}, u32[]{:S(2)}) collective-permute-start(f32[8,4,8,256]{3,2,1,0:T(8,128)S(1)} %copy-done.2), channel_id=1, source_target_pairs={{0,1},{1,0},{2,3},{3,2},{4,5},{5,4},{6,7},{7,6},{8,9},{9,8},{10,11... | collective-permute-start | bytes 786440 | tf_op jit(solution)/shard_map/ppermute | solution.py:52
  98.1 7.7 %collective-permute-start.21 = (f32[8,4,8,256]{3,2,1,0:T(8,128)S(1)}, f32[8,4,8,256]{3,2,1,0:T(8,128)}, u32[]{:S(2)}, u32[]{:S(2)}) collective-permute-start(f32[8,4,8,256]{3,2,1,0:T(8,128)S(1)} %collective-permute-done.17.rest_2_), channel_id=1, source_target_pairs={{0,2},{1,9},{2,4},{3,11},{4,6},{5,13},{6,0},{7,15},{8,10},{9,17},{... | collective-permute-start | bytes 786440 | tf_op jit(solution)/shard_map/ppermute | solution.py:52
  101.2 6.5 %collective-permute-start.22 = (f32[8,4,8,256]{3,2,1,0:T(8,128)S(1)}, f32[8,4,8,256]{3,2,1,0:T(8,128)}, u32[]{:S(2)}, u32[]{:S(2)}) collective-permute-start(f32[8,4,8,256]{3,2,1,0:T(8,128)S(1)} %collective-permute-done.20.rest_5_), channel_id=1, source_target_pairs={{0,6},{1,25},{2,0},{3,27},{4,2},{5,29},{6,4},{7,31},{8,14},{9,1},{... | collective-permute-start | bytes 786440 | tf_op jit(solution)/shard_map/ppermute | solution.py:52
  101.3 6.3 %collective-permute-start.25 = (f32[8,4,8,256]{3,2,1,0:T(8,128)S(1)}, f32[8,4,8,256]{3,2,1,0:T(8,128)S(1)}, u32[]{:S(2)}, u32[]{:S(2)}) collective-permute-start(f32[8,4,8,256]{3,2,1,0:T(8,128)S(1)} %collective-permute-done.17.rest_2_), channel_id=1, source_target_pairs={{0,1},{1,0},{2,3},{3,2},{4,5},{5,4},{6,7},{7,6},{8,9},{9,8},{10,11... | collective-permute-start | bytes 786440 | tf_op jit(solution)/shard_map/ppermute | solution.py:52
  102.1 9.6 %collective-permute-start.26 = (f32[8,4,8,256]{3,2,1,0:T(8,128)S(1)}, f32[8,4,8,256]{3,2,1,0:T(8,128)S(1)}, u32[]{:S(2)}, u32[]{:S(2)}) collective-permute-start(f32[8,4,8,256]{3,2,1,0:T(8,128)S(1)} %collective-permute-done.18.rest_3_), channel_id=1, source_target_pairs={{0,1},{1,0},{2,3},{3,2},{4,5},{5,4},{6,7},{7,6},{8,9},{9,8},{10,11... | collective-permute-start | bytes 786440 | tf_op jit(solution)/shard_map/ppermute | solution.py:52
  103.3 9.0 %collective-permute-start.27 = (f32[8,4,8,256]{3,2,1,0:T(8,128)S(1)}, f32[8,4,8,256]{3,2,1,0:T(8,128)S(1)}, u32[]{:S(2)}, u32[]{:S(2)}) collective-permute-start(f32[8,4,8,256]{3,2,1,0:T(8,128)S(1)} %collective-permute-done.19.rest_4_), channel_id=1, source_target_pairs={{0,1},{1,0},{2,3},{3,2},{4,5},{5,4},{6,7},{7,6},{8,9},{9,8},{10,11... | collective-permute-start | bytes 786440 | tf_op jit(solution)/shard_map/ppermute | solution.py:52
  105.8 7.8 %collective-permute-start.28 = (f32[8,4,8,256]{3,2,1,0:T(8,128)S(1)}, f32[8,4,8,256]{3,2,1,0:T(8,128)S(1)}, u32[]{:S(2)}, u32[]{:S(2)}) collective-permute-start(f32[8,4,8,256]{3,2,1,0:T(8,128)S(1)} %collective-permute-done.20.rest_5_), channel_id=1, source_target_pairs={{0,1},{1,0},{2,3},{3,2},{4,5},{5,4},{6,7},{7,6},{8,9},{9,8},{10,11... | collective-permute-start | bytes 786440 | tf_op jit(solution)/shard_map/ppermute | solution.py:52
  107.7 11.0 %collective-permute-start.7 = (f32[8,4,8,256]{3,2,1,0:T(8,128)S(1)}, f32[8,4,8,256]{3,2,1,0:T(8,128)}, u32[]{:S(2)}, u32[]{:S(2)}) collective-permute-start(f32[8,4,8,256]{3,2,1,0:T(8,128)S(1)} %collective-permute-done.3.rest_2_), channel_id=1, source_target_pairs={{0,2},{1,9},{2,4},{3,11},{4,6},{5,13},{6,0},{7,15},{8,10},{9,17},{... | collective-permute-start | bytes 786440 | tf_op jit(solution)/shard_map/ppermute | solution.py:52
  108.4 10.9 %collective-permute-start.8 = (f32[8,4,8,256]{3,2,1,0:T(8,128)S(1)}, f32[8,4,8,256]{3,2,1,0:T(8,128)}, u32[]{:S(2)}, u32[]{:S(2)}) collective-permute-start(f32[8,4,8,256]{3,2,1,0:T(8,128)S(1)} %collective-permute-done.6.rest_5_), channel_id=1, source_target_pairs={{0,6},{1,25},{2,0},{3,27},{4,2},{5,29},{6,4},{7,31},{8,14},{9,1},{... | collective-permute-start | bytes 786440 | tf_op jit(solution)/shard_map/ppermute | solution.py:52
  112.3 7.1 %collective-permute-start.11 = (f32[8,4,8,256]{3,2,1,0:T(8,128)S(1)}, f32[8,4,8,256]{3,2,1,0:T(8,128)}, u32[]{:S(2)}, u32[]{:S(2)}) collective-permute-start(f32[8,4,8,256]{3,2,1,0:T(8,128)S(1)} %collective-permute-done.3.rest_2_), channel_id=1, source_target_pairs={{0,1},{1,0},{2,3},{3,2},{4,5},{5,4},{6,7},{7,6},{8,9},{9,8},{10,11... | collective-permute-start | bytes 786440 | tf_op jit(solution)/shard_map/ppermute | solution.py:52
  113.0 6.8 %collective-permute-start.29 = (f32[8,4,8,256]{3,2,1,0:T(8,128)}, f32[8,4,8,256]{3,2,1,0:T(8,128)}, u32[]{:S(2)}, u32[]{:S(2)}) collective-permute-start(f32[8,4,8,256]{3,2,1,0:T(8,128)} %collective-permute-done.21.rest_6_), channel_id=1, source_target_pairs={{0,1},{1,0},{2,3},{3,2},{4,5},{5,4},{6,7},{7,6},{8,9},{9,8},{10,11... | collective-permute-start | bytes 786440 | tf_op jit(solution)/shard_map/ppermute | solution.py:52
  114.2 5.7 %collective-permute-start.30 = (f32[8,4,8,256]{3,2,1,0:T(8,128)}, f32[8,4,8,256]{3,2,1,0:T(8,128)}, u32[]{:S(2)}, u32[]{:S(2)}) collective-permute-start(f32[8,4,8,256]{3,2,1,0:T(8,128)} %collective-permute-done.22.rest_7_), channel_id=1, source_target_pairs={{0,1},{1,0},{2,3},{3,2},{4,5},{5,4},{6,7},{7,6},{8,9},{9,8},{10,11... | collective-permute-start | bytes 786440 | tf_op jit(solution)/shard_map/ppermute | solution.py:52
  118.7 16.9 %collective-permute-start.14 = (f32[8,4,8,256]{3,2,1,0:T(8,128)S(1)}, f32[8,4,8,256]{3,2,1,0:T(8,128)S(1)}, u32[]{:S(2)}, u32[]{:S(2)}) collective-permute-start(f32[8,4,8,256]{3,2,1,0:T(8,128)S(1)} %collective-permute-done.6.rest_5_), channel_id=1, source_target_pairs={{0,1},{1,0},{2,3},{3,2},{4,5},{5,4},{6,7},{7,6},{8,9},{9,8},{10,11... | collective-permute-start | bytes 786440 | tf_op jit(solution)/shard_map/ppermute | solution.py:52
  119.3 16.3 %collective-permute-start.12 = (f32[8,4,8,256]{3,2,1,0:T(8,128)S(1)}, f32[8,4,8,256]{3,2,1,0:T(8,128)S(1)}, u32[]{:S(2)}, u32[]{:S(2)}) collective-permute-start(f32[8,4,8,256]{3,2,1,0:T(8,128)S(1)} %collective-permute-done.4.rest_3_), channel_id=1, source_target_pairs={{0,1},{1,0},{2,3},{3,2},{4,5},{5,4},{6,7},{7,6},{8,9},{9,8},{10,11... | collective-permute-start | bytes 786440 | tf_op jit(solution)/shard_map/ppermute | solution.py:52
  119.4 16.2 %collective-permute-start.13 = (f32[8,4,8,256]{3,2,1,0:T(8,128)S(1)}, f32[8,4,8,256]{3,2,1,0:T(8,128)S(1)}, u32[]{:S(2)}, u32[]{:S(2)}) collective-permute-start(f32[8,4,8,256]{3,2,1,0:T(8,128)S(1)} %collective-permute-done.5.rest_4_), channel_id=1, source_target_pairs={{0,1},{1,0},{2,3},{3,2},{4,5},{5,4},{6,7},{7,6},{8,9},{9,8},{10,11... | collective-permute-start | bytes 786440 | tf_op jit(solution)/shard_map/ppermute | solution.py:52
  119.8 15.8 %collective-permute-start.15 = (f32[8,4,8,256]{3,2,1,0:T(8,128)}, f32[8,4,8,256]{3,2,1,0:T(8,128)S(1)}, u32[]{:S(2)}, u32[]{:S(2)}) collective-permute-start(f32[8,4,8,256]{3,2,1,0:T(8,128)} %collective-permute-done.7.rest_6_), channel_id=1, source_target_pairs={{0,1},{1,0},{2,3},{3,2},{4,5},{5,4},{6,7},{7,6},{8,9},{9,8},{10,11... | collective-permute-start | bytes 786440 | tf_op jit(solution)/shard_map/ppermute | solution.py:52
  119.9 15.7 %collective-permute-start.16 = (f32[8,4,8,256]{3,2,1,0:T(8,128)}, f32[8,4,8,256]{3,2,1,0:T(8,128)S(1)}, u32[]{:S(2)}, u32[]{:S(2)}) collective-permute-start(f32[8,4,8,256]{3,2,1,0:T(8,128)} %collective-permute-done.8.rest_7_), channel_id=1, source_target_pairs={{0,1},{1,0},{2,3},{3,2},{4,5},{5,4},{6,7},{7,6},{8,9},{9,8},{10,11... | collective-permute-start | bytes 786440 | tf_op jit(solution)/shard_map/ppermute | solution.py:52
  125.8 9.8 %copy-start.24 = (f32[32,64]{1,0:T(8,128)S(1)}, f32[32,64]{1,0:T(8,128)}, u32[]{:S(2)}) copy-start(f32[32,64]{1,0:T(8,128)} %get-tuple-element.32.rest_17_) | copy-start | bytes 24580
  135.6 18.2 %copy-start.32 = (f32[8,64]{1,0:T(8,128)S(1)}, f32[8,64]{1,0:T(8,128)}, u32[]{:S(2)}) copy-start(f32[8,64]{1,0:T(8,128)} %get-tuple-element.38) | copy-start | bytes 6148
  135.7 18.2 %copy-start.33 = (s32[8,64]{1,0:T(8,128)S(1)}, s32[8,64]{1,0:T(8,128)}, u32[]{:S(2)}) copy-start(s32[8,64]{1,0:T(8,128)} %get-tuple-element.22) | copy-start | bytes 6148
  145.4 5.3 %collective-permute-start.35 = (f32[8,64]{1,0:T(8,128)S(1)}, f32[8,64]{1,0:T(8,128)S(1)}, u32[]{:S(2)}, u32[]{:S(2)}) collective-permute-start(f32[8,64]{1,0:T(8,128)S(1)} %get-tuple-element.35), channel_id=1, source_target_pairs={{0,32},{1,33},{2,34},{3,35},{4,36},{5,37},{6,38},{7,39},{8,40},{9,... | collective-permute-start | bytes 6152 | tf_op jit(solution)/shard_map/ppermute | solution.py:52
  147.1 3.7 %collective-permute-start.36 = (f32[8,64]{1,0:T(8,128)S(1)}, f32[8,64]{1,0:T(8,128)S(1)}, u32[]{:S(2)}, u32[]{:S(2)}) collective-permute-start(f32[8,64]{1,0:T(8,128)S(1)} %get-tuple-element.36), channel_id=1, source_target_pairs={{0,96},{1,97},{2,98},{3,99},{4,100},{5,101},{6,102},{7,103},{8,104... | collective-permute-start | bytes 6152 | tf_op jit(solution)/shard_map/ppermute | solution.py:52
  148.7 5.1 %collective-permute-start.37 = (f32[8,64]{1,0:T(8,128)S(1)}, f32[8,64]{1,0:T(8,128)S(1)}, u32[]{:S(2)}, u32[]{:S(2)}) collective-permute-start(f32[8,64]{1,0:T(8,128)S(1)} %get-tuple-element.37), channel_id=1, source_target_pairs={{0,64},{1,65},{2,66},{3,67},{4,68},{5,69},{6,70},{7,71},{8,72},{9,... | collective-permute-start | bytes 6152 | tf_op jit(solution)/shard_map/ppermute | solution.py:52
  (25 other events, 54.8 us)

commit v2 on v1

v2 whole, which is shorter than its diff:
```python
import functools

import jax
import jax.numpy as jnp
from jax import lax
from jax.experimental import pallas as pl
from jax.experimental.pallas import tpu as pltpu
from jax.sharding import PartitionSpec as P

AXES = ("depth", "row", "column")
F32 = jnp.float32
BF16 = jnp.bfloat16
MIB = 1 << 20


def pairs_of(core0, core1):
    out = []
    for y in range(4):
        for x in range(4):
            for z in range(4):
                for k in range(2):
                    ty, tx, tz, tk = (core1 if k else core0)(y, x, z, k)
                    out.append((y * 32 + x * 8 + z * 2 + k, (ty % 4) * 32 + (tx % 4) * 8 + (tz % 4) * 2 + tk % 2))
    return out


def along_x(n):
    return lambda y, x, z, k: (y, x + n, z, k)


def along_y(n):
    return lambda y, x, z, k: (y + n, x, z, k)


def along_z(n):
    return lambda y, x, z, k: (y, x, z + n, k)


def other_core(y, x, z, k):
    return (y, x, z, k + 1)


FIRST = {n: pairs_of(along_x(n), along_z(n)) for n in (1, -1, 2)}
SECOND = {n: pairs_of(along_z(n), along_x(n)) for n in (1, -1, 2)}
ALONG_X = {n: pairs_of(along_x(n), along_x(n)) for n in (1, -1, 2)}
ALONG_Y = {n: pairs_of(along_y(n), along_y(n)) for n in (1, -1, 2)}
Z_ACROSS = pairs_of(along_z(2), along_z(2))
SWAP = pairs_of(other_core, other_core)


def send(value, pairs):
    return lax.ppermute(value, AXES, pairs)


def spread(parts, line):
    return (parts[0], send(parts[1], line[1]), send(parts[2], line[-1]), send(parts[3], line[2]))


def smem():
    return pl.BlockSpec(memory_space=pltpu.SMEM)


def vmem():
    return pl.BlockSpec(memory_space=pltpu.VMEM)


def anywhere():
    return pl.BlockSpec(memory_space=pl.ANY)


def in_vmem(value):
    return pltpu.with_memory_space_constraint(value, pltpu.VMEM)


def in_hbm(value):
    return pltpu.with_memory_space_constraint(value, pltpu.HBM)


def grant(mib):
    return pltpu.CompilerParams(vmem_limit_bytes=mib * MIB)


def small_cost():
    return pl.CostEstimate(flops=1, bytes_accessed=1, transcendentals=0)


CELLS = 4


def relayout_body(amp_ref, out_ref, turned):
    pairs, slots, cells = amp_ref.shape
    groups = cells // CELLS
    for t in range(slots):
        turned[t] = amp_ref[:, t, :].T
    for t in range(slots):
        pieces = [turned[t, pl.ds(j, groups, stride=CELLS), :] for j in range(CELLS)]
        out_ref[:, t, :] = jnp.concatenate(pieces, axis=1)


def relayout(amp):
    pairs, slots, cells = amp.shape
    return pl.pallas_call(
        relayout_body,
        out_shape=jax.ShapeDtypeStruct((cells // CELLS, slots, CELLS * pairs), F32),
        in_specs=[vmem()],
        out_specs=vmem(),
        scratch_shapes=[pltpu.VMEM((slots, cells, pairs), F32)],
        compiler_params=grant(8),
        cost_estimate=small_cost(),
    )(amp)


def stack_body(place, b0, b1, b2, b3, after, out):
    own = jnp.where(place[3] == 0, place[1], place[2])
    for source, shift in ((b0, 0), (b1, 3), (b2, 1), (b3, 2)):
        out[:, pl.ds(lax.rem(own + shift, 4), 1)] = source[...][:, None]


def stack(place, blocks, after):
    groups, slots, lanes = blocks[0].shape
    return pl.pallas_call(
        stack_body,
        out_shape=jax.ShapeDtypeStruct((groups, 4, slots, lanes), F32),
        in_specs=[smem()] + [vmem()] * 4 + [anywhere()],
        out_specs=vmem(),
        compiler_params=grant(8),
        cost_estimate=small_cost(),
    )(place, *blocks, after)


CHUNKS = (32, 32)


def pack_body(base, place, p0, p1, p2, p3, *rest):
    out = rest[-1]
    count = out.shape[0]
    x, z, core = place[1], place[2], place[3]
    for piece, shift in ((p0, 0), (p1, 3), (p2, 1), (p3, 2)):
        first = jnp.where(core == 0, lax.rem(z + shift, 4), lax.rem(x + shift, 4) * 4)
        for i in range(4):
            out[:, pl.ds(first + i * jnp.where(core == 0, 4, 1), 1)] = piece[base : base + count, i : i + 1]


def pack(place, pieces, base, count, after):
    _, _, slots, lanes = pieces[0].shape
    return pl.pallas_call(
        functools.partial(pack_body, base),
        out_shape=jax.ShapeDtypeStruct((count, 16, slots, lanes), F32),
        in_specs=[smem()] + [vmem()] * 4 + [anywhere()] * len(after),
        out_specs=vmem(),
        compiler_params=grant(12),
        cost_estimate=small_cost(),
    )(place, *pieces, *after)


def dot_nt(a, b):
    return lax.dot_general(a, b, (((1,), (1,)), ((), ())), preferred_element_type=F32)


def split(value):
    high = value.astype(BF16)
    return high, (value - high.astype(F32)).astype(BF16)


DEPTH_BLOCK = 1280


def cycle_body(depth, place, amp_ref, int_ref, choice_ref, after, o0, o1, o2, o3, acc, by_row):
    step = pl.program_id(0)
    window, width, block = int_ref.shape
    pairs, rows, _ = amp_ref.shape

    @pl.when(step == 0)
    def _():
        acc[...] = jnp.zeros_like(acc)

    left = depth - step * block
    amp = amp_ref[...].reshape(pairs * rows, block)
    ints = int_ref[...].reshape(window * width, block)
    inside = lax.broadcasted_iota(jnp.int32, amp.shape, 1) < left
    high, low = split(jnp.where(inside, amp, 0.0))
    inside = lax.broadcasted_iota(jnp.int32, ints.shape, 1) < left
    int_high, int_low = split(jnp.where(inside, ints, 0.0))
    acc[...] += dot_nt(high, int_high) + dot_nt(high, int_low) + dot_nt(low, int_high)

    @pl.when(step == pl.num_programs(0) - 1)
    def _():
        total = jnp.zeros((pairs * rows, width), F32)
        for j in range(window):
            total = total + choice_ref[:, j : j + 1] * acc[:, j * width : (j + 1) * width]
        by_row[...] = total
        own = pairs // 4
        for out, shift in ((o0, 0), (o1, 1), (o2, 3), (o3, 2)):
            at = lax.rem(place[0] + shift, 4) * own * rows
            for a in range(rows):
                out[a] = by_row[pl.ds(at + a, own, stride=rows), :]


def cycle(place, amp, ints, choice, after):
    pairs, rows, depth = amp.shape
    window, width, _ = ints.shape
    part = jax.ShapeDtypeStruct((rows, pairs // 4, width), F32)
    whole = pl.BlockSpec(part.shape, lambda i: (0, 0, 0))
    return pl.pallas_call(
        functools.partial(cycle_body, depth),
        grid=(pl.cdiv(depth, DEPTH_BLOCK),),
        out_shape=(part,) * 4,
        in_specs=[
            smem(),
            pl.BlockSpec((pairs, rows, DEPTH_BLOCK), lambda i: (0, 0, i)),
            pl.BlockSpec((window, width, DEPTH_BLOCK), lambda i: (0, 0, i)),
            pl.BlockSpec((pairs * rows, window), lambda i: (0, 0)),
            anywhere(),
        ],
        out_specs=(whole,) * 4,
        scratch_shapes=[
            pltpu.VMEM((pairs * rows, window * width), F32),
            pltpu.VMEM((pairs * rows, width), F32),
        ],
        compiler_params=grant(24),
        cost_estimate=small_cost(),
    )(place, in_hbm(amp), in_hbm(ints), choice, after)


def rows_body(place, a0, a1, a2, a3, *rest):
    o0, o1, o2, o3, held = rest[-5:]
    held[...] = a0[...] + a1[...] + a2[...] + a3[...]
    for out, shift in ((o0, 0), (o1, 1), (o2, 3), (o3, 2)):
        out[...] = held[pl.ds(lax.rem(place[1] + shift, 4) * 2, 2)]


def rows(place, parts, after):
    count, own, width = parts[0].shape
    return pl.pallas_call(
        rows_body,
        out_shape=(jax.ShapeDtypeStruct((count // 4, own, width), F32),) * 4,
        in_specs=[smem()] + [vmem()] * 4 + [anywhere()] * len(after),
        out_specs=(vmem(),) * 4,
        scratch_shapes=[pltpu.VMEM((count, own, width), F32)],
        compiler_params=grant(8),
        cost_estimate=small_cost(),
    )(place, *parts, *after)


def halves_body(place, a0, a1, a2, a3, *rest):
    keep, away = rest[-2:]
    half = lax.div(place[2], 2)
    total = a0[...] + a1[...] + a2[...] + a3[...]
    keep[...] = jnp.where(half == 0, total[0], total[1])
    away[...] = jnp.where(half == 0, total[1], total[0])


def halves(place, parts, after):
    one = jax.ShapeDtypeStruct(parts[0].shape[1:], F32)
    return pl.pallas_call(
        halves_body,
        out_shape=(one, one),
        in_specs=[smem()] + [vmem()] * 4 + [anywhere()] * len(after),
        out_specs=(vmem(), vmem()),
        compiler_params=grant(8),
        cost_estimate=small_cost(),
    )(place, *parts, *after)


def labels_body(place, vir, occ, allowed, pair_list, occ_e, vir_e, vir_tile, bound, denom, live):
    y, x, z, core = place[0], place[1], place[2], place[3]
    row = x * 2 + lax.div(z, 2)
    column = lax.rem(z, 2) * 2 + core
    irreps = allowed.shape[0]
    total = vir.shape[0]
    pair_irrep = jnp.bitwise_xor(occ[pair_list[0, 0]], occ[pair_list[1, 0]])
    a_orb = row * 128
    ga = vir[a_orb]
    gb = jnp.bitwise_xor(ga, pair_irrep)
    tile = vir_tile[...]
    counts = [jnp.sum((tile == g).astype(jnp.int32)) for g in range(irreps)]
    starts = [jnp.int32(0)]
    for g in range(irreps - 1):
        starts.append(starts[g] + counts[g])
    count_b = jnp.int32(0)
    start_b = jnp.int32(0)
    groups, lanes = bound.shape
    cell = (
        y * (groups * CELLS)
        + lax.broadcasted_iota(jnp.int32, bound.shape, 0) * CELLS
        + lax.div(lax.broadcasted_iota(jnp.int32, bound.shape, 1), lanes // CELLS)
    )
    limit = jnp.zeros(bound.shape, jnp.int32)
    for g in range(irreps):
        count_b = jnp.where(gb == g, counts[g], count_b)
        start_b = jnp.where(gb == g, starts[g], start_b)
        partner = jnp.bitwise_xor(pair_irrep, g)
        reach = jnp.int32(0)
        for h in range(irreps):
            reach = jnp.where(partner == h, counts[h], reach)
        reach = reach * allowed[ga, gb, g]
        limit = jnp.where((cell >= starts[g]) & (cell < starts[g] + counts[g]), reach, limit)
    bound[...] = limit
    own, width = denom.shape
    slot = column * width + lax.broadcasted_iota(jnp.int32, (own, width), 1)
    line = lax.broadcasted_iota(jnp.int32, (own, width), 0)
    first = start_b + column * width

    def put(s, acc):
        orb = first + s
        value = jnp.where(orb < total, vir_e[jnp.minimum(orb, total - 1)], 0.0)
        return jnp.where(slot == column * width + s, value, acc)

    eps_b = lax.fori_loop(0, width, put, jnp.zeros((own, width), F32))
    eps_ij = jnp.zeros((own, width), F32)
    for p in range(own):
        i, j = pair_list[0, y * own + p], pair_list[1, y * own + p]
        eps_ij = jnp.where(line == p, occ_e[i] + occ_e[j], eps_ij)
    denom[...] = eps_ij - vir_e[a_orb] - eps_b
    live[...] = (slot < count_b).astype(jnp.int32)


def labels(place, vir, occ, allowed, pair_list, occ_e, vir_e, width, own, pairs):
    total = vir.shape[0]
    return pl.pallas_call(
        labels_body,
        out_shape=(
            jax.ShapeDtypeStruct((total // 4 // CELLS, CELLS * pairs), jnp.int32),
            jax.ShapeDtypeStruct((own, width), F32),
            jax.ShapeDtypeStruct((own, width), jnp.int32),
        ),
        in_specs=[smem()] * 7 + [vmem()],
        out_specs=(vmem(),) * 3,
        compiler_params=grant(8),
        cost_estimate=small_cost(),
    )(place, vir, occ, allowed, pair_list.T, occ_e, vir_e, vir.reshape(8, total // 8))


READY = 4
SLOTS = 3
PARTS = 4


def ready_body(slab, after, out, token, held, sems):
    token[...] = jnp.zeros_like(token)
    width, cells, slots = slab.shape
    steps = cells // (8 * READY)
    share = width // PARTS

    def copies(s):
        return [
            pltpu.make_async_copy(
                slab.at[pl.ds(n * share, share), pl.ds(s * READY * 8, READY * 8), :],
                held.at[s % SLOTS, pl.ds(n * share, share)],
                sems.at[s % SLOTS, n],
            )
            for n in range(PARTS)
        ]

    for s in range(SLOTS - 1):
        for c in copies(s):
            c.start()
    for s in range(steps):
        if s + SLOTS - 1 < steps:
            for c in copies(s + SLOTS - 1):
                c.start()
        for c in copies(s):
            c.wait()
        for g in range(READY):
            block = held[s % SLOTS, :, 8 * g : 8 * g + 8, :].reshape(width // 2, 2, 8, slots)
            even, odd = block[:, 0], block[:, 1]
            first = lax.broadcasted_iota(jnp.int32, even.shape, 1) < CELLS
            lower_cells = jnp.where(first, even, pltpu.roll(odd, CELLS, 1)).reshape(width * CELLS, slots)
            upper_cells = jnp.where(first, pltpu.roll(even, CELLS, 1), odd).reshape(width * CELLS, slots)
            for i, rows in enumerate((lower_cells, upper_cells)):
                at = (s * READY + g) * 2 + i
                high, low = split(rows)
                out[at, pl.ds(0, width * CELLS)] = high
                out[at, pl.ds(width * CELLS, width * CELLS)] = low


def ready(slab, after):
    width, cells, slots = slab.shape
    return pl.pallas_call(
        ready_body,
        out_shape=(
            jax.ShapeDtypeStruct((cells // CELLS, 2 * CELLS * width, slots), BF16),
            jax.ShapeDtypeStruct((8, 128), F32),
        ),
        in_specs=[anywhere(), anywhere()],
        out_specs=(vmem(), vmem()),
        scratch_shapes=[
            pltpu.VMEM((SLOTS, width, READY * 8, slots), F32),
            pltpu.SemaphoreType.DMA((SLOTS, PARTS)),
        ],
        compiler_params=grant(28),
        cost_estimate=small_cost(),
    )(slab, after)


STEP = 8


def ladder_body(last, base, place, bound, slab, mine, other, before, after, *rest):
    if last:
        o0, o1, o2, o3, amps, acc, folded, final = rest
    else:
        out, amps, acc, folded, final = rest
    y, core = place[0], place[3]
    _, rows, slots = slab.shape
    lanes = bound.shape[1]
    width = rows // (2 * CELLS)
    pairs = lanes // CELLS
    t_of = lax.broadcasted_iota(jnp.int32, (slots, lanes), 0)
    for s in range(mine.shape[0] // STEP):
        left, right = [], []
        for g in range(STEP):
            amps[g, :, pl.ds(core, 1)] = mine[s * STEP + g][:, None]
            amps[g, :, pl.ds(1 - core, 1)] = other[s * STEP + g][:, None]
            at = base + s * STEP + g
            edge = bound[at : at + 1, :]
            high, low = split(jnp.where(t_of < edge, amps[g].reshape(slots, lanes), 0.0))
            left.append(slab[at])
            right.append(jnp.concatenate([high, low], axis=1))
        part = jnp.dot(jnp.concatenate(left, axis=1), jnp.concatenate(right, axis=0), preferred_element_type=F32)
        if s == 0:
            acc[...] = part
        else:
            acc[...] += part
    half = rows // 2
    folded[...] = (acc[:half, :lanes] + acc[:half, lanes:]) + (acc[half:, :lanes] + acc[half:, lanes:])
    total = jnp.zeros((width, pairs), F32)
    for j in range(CELLS):
        total = total + folded[pl.ds(j, width, stride=CELLS), :][:, j * pairs : (j + 1) * pairs]
    total = total.T
    if not last:
        out[...] = total if base == 0 else total + before[...]
        return
    if base:
        total = total + before[...]
    final[...] = total
    own = pairs // 4
    for o, shift in ((o0, 0), (o1, 1), (o2, 3), (o3, 2)):
        o[...] = final[pl.ds(pl.multiple_of(lax.rem(y + shift, 4) * own, 8), own), :]


def ladder(place, bound, slab, mine, other, base, before, after, last):
    _, rows, slots = slab.shape
    lanes = bound.shape[1]
    pairs = lanes // CELLS
    width = rows // (2 * CELLS)
    if last:
        out_shape = (jax.ShapeDtypeStruct((pairs // 4, width), F32),) * 4
        out_specs = (vmem(),) * 4
    else:
        out_shape = jax.ShapeDtypeStruct((pairs, width), F32)
        out_specs = vmem()
    return pl.pallas_call(
        functools.partial(ladder_body, last, base),
        out_shape=out_shape,
        in_specs=[smem()] + [vmem()] * 5 + [anywhere()],
        out_specs=out_specs,
        scratch_shapes=[
            pltpu.VMEM((STEP, slots // 16, 2, 8, lanes), F32),
            pltpu.VMEM((rows, 2 * lanes), F32),
            pltpu.VMEM((rows // 2, lanes), F32),
            pltpu.VMEM((pairs, width), F32),
        ],
        compiler_params=grant(12),
        cost_estimate=small_cost(),
    )(place, bound, in_vmem(slab), mine, other, before, after)


def on_device(vir, occ, allowed, pair_list, occ_e, vir_e, ladder_amp, int_slab, cycle_amp, cycle_int):
    row, column = lax.axis_index("row"), lax.axis_index("column")
    place = jnp.stack(
        [lax.axis_index("depth"), row // 2, (row % 2) * 2 + column // 2, column % 2]
    ).astype(jnp.int32)
    pairs = ladder_amp.shape[0]
    width = int_slab.shape[1]
    own = pairs // 4

    mine = relayout(jnp.transpose(ladder_amp, (0, 2, 1)))
    bound, denom, live = labels(place, vir, occ, allowed, pair_list, occ_e, vir_e, width, own, pairs)
    line = stack(place, [mine] + [send(mine, FIRST[n]) for n in (1, -1, 2)], bound)
    pieces = [line] + [send(line, SECOND[n]) for n in (1, -1, 2)]

    choice = (pair_list[:, 1:] == jnp.arange(cycle_int.shape[1], dtype=jnp.int32)).astype(F32)
    choice = jnp.repeat(choice, cycle_amp.shape[1], axis=0)
    parts = cycle(place, cycle_amp, jnp.transpose(cycle_int, (1, 2, 0)), choice, line)
    slab, token = ready(in_hbm(int_slab.reshape(int_slab.shape[1:])), parts[0])

    parts = rows(place, spread(parts, ALONG_Y), (token,))
    base, sums, last_packed, keep = 0, bound, parts[0], parts[0]
    for i, count in enumerate(CHUNKS):
        packed = pack(place, pieces, base, count, (last_packed,))
        other = send(packed, SWAP)
        if i == 0:
            parts = spread(parts, ALONG_X)
        sums = ladder(place, bound, slab, packed, other, base, sums, keep, i == len(CHUNKS) - 1)
        if i == 0:
            keep, away = halves(place, parts, (sums,))
            got = send(away, Z_ACROSS)
        base += count
        last_packed = packed
    s0, s1, s2, s3 = spread(sums, ALONG_Y)
    total = (s0 + s1) + (s2 + s3) + (keep + got)
    return jnp.where(live > 0, total / denom, jnp.float32(0.0))[None]


def solution(mesh):
    return jax.shard_map(
        on_device,
        mesh=mesh,
        in_specs=(
            P(),
            P(),
            P(),
            P(),
            P(),
            P(),
            P(None, "depth", ("row", "column")),
            P("row", "column", "depth", None),
            P(None, None, ("depth", "row")),
            P(("depth", "row"), None, "column"),
        ),
        out_specs=P("row", "depth", "column"),
        check_vma=False,
    )
```

time: 155 us -> 69.3 us (0.45)
  Pallas kernels: 71.2 us -> 25.9 us
  waiting for transfers between devices: 23.3 us -> 8.1 us
  local copies, waits for them, and re-layouts: 20 us -> 5.13 us
  starting transfers between devices: 38.3 us -> 28.9 us
    pallas_call x7 -> x11, Pallas kernels: 71.2 us -> 25.9 us  [the longest x2 6.89 us: ladder(): pl.pallas_call(functools.partial(ladder_body, last, base), out_shape=out_...]
    ppermute x38 -> x18, waiting for transfers between devices: 23.3 us -> 8.1 us  [send(): return lax.ppermute(value, AXES, pairs)]
    unnamed x71 -> x14, local copies, waits for them, and re-layouts: 18.6 us -> 5.12 us
    ppermute x38 -> x18, starting transfers between devices: 38.3 us -> 28.9 us  [send(): return lax.ppermute(value, AXES, pairs)]
  transfers between devices with their start and end apart: 38 -> 18, of which waited for: 11 -> 6; matrix products, arithmetic and copies ran while one was open for 2% -> 0% of each run, Pallas kernels for 17% -> 30%
where the time goes in v2:
time: 69.3 us; the launch traced here: 68.9 us
  starting transfers between devices  28.9 us (42%)
  Pallas kernels  25.9 us (37%)
  waiting for transfers between devices  8.1 us (12%)
  local copies, waits for them, and re-layouts  5.13 us (7%)
  other arithmetic  0.75 us (1%)
    ppermute x18, starting transfers between devices, send(): return lax.ppermute(value, AXES, pairs)  28.9 us
    ppermute x18, waiting for transfers between devices, send(): return lax.ppermute(value, AXES, pairs)  8.1 us
    pallas_call x2, Pallas kernels, ladder(): pl.pallas_call(functools.partial(ladder_body, last, base), out_shape=out_...  6.89 us
    pallas_call x1, Pallas kernels, ready(): pl.pallas_call(ready_body, out_shape=(jax.ShapeDtypeStruct((cells // CELL...  6.77 us
    pallas_call x1, Pallas kernels, cycle(): pl.pallas_call(functools.partial(cycle_body, depth), grid=(pl.cdiv(depth,...  6.15 us
    unnamed x14, local copies, waits for them, and re-layouts  5.12 us
    pallas_call x1, Pallas kernels, labels(): pl.pallas_call(labels_body, out_shape=(jax.ShapeDtypeStruct((total // 4 /...  2.07 us
    pallas_call x2, Pallas kernels, pack(): pl.pallas_call(functools.partial(pack_body, base), out_shape=jax.ShapeDty...  1.66 us
  transfers between devices with their start and end apart: 18, of which 6 were waited for; matrix products, arithmetic and copies ran while one was open for 0% of the time, Pallas kernels for 30%

profile of v2, /device:TPU:0, one launch (start us, length us, event | category | flops | bytes accessed | tf_op | source)
XLA Modules:
  0.0 68.9 jit_solution(17738165745160435886)
XLA Ops:
  0.0 0.9 %copy-done = f32[32,256,8]{1,2,0:T(8,128)S(1)} copy-done((f32[32,256,8]{1,2,0:T(8,128)S(1)}, f32[32,256,8]{1,2,0:T(8,128)}, u32[]{:S(2)}) %copy-start) | copy-done | bytes 262168
  1.0 0.6 shard_map.101.b0
  1.5 3.2 %collective-permute-start.2 = (f32[64,8,128]{2,1,0:T(8,128)S(1)}, f32[64,8,128]{2,1,0:T(8,128)S(1)}, u32[]{:S(2)}, u32[]{:S(2)}) collective-permute-start(f32[64,8,128]{2,1,0:T(8,128)S(1)} %shard_map.101.b0), channel_id=1, source_target_pairs={{0,16},{1,5},{2,18},{3,7},{4,20},{5,1},{6,22},{7,3},{8,24},{9,13},... | collective-permute-start | bytes 786440 | tf_op jit(solution)/shard_map/ppermute | solution.py:52
  4.7 1.1 %collective-permute-start.1 = (f32[64,8,128]{2,1,0:T(8,128)S(1)}, f32[64,8,128]{2,1,0:T(8,128)S(1)}, u32[]{:S(2)}, u32[]{:S(2)}) collective-permute-start(f32[64,8,128]{2,1,0:T(8,128)S(1)} %shard_map.101.b0), channel_id=1, source_target_pairs={{0,24},{1,7},{2,26},{3,1},{4,28},{5,3},{6,30},{7,5},{8,0},{9,15},{... | collective-permute-start | bytes 786440 | tf_op jit(solution)/shard_map/ppermute | solution.py:52
  5.9 0.9 %collective-permute-start = (f32[64,8,128]{2,1,0:T(8,128)S(1)}, f32[64,8,128]{2,1,0:T(8,128)S(1)}, u32[]{:S(2)}, u32[]{:S(2)}) collective-permute-start(f32[64,8,128]{2,1,0:T(8,128)S(1)} %shard_map.101.b0), channel_id=1, source_target_pairs={{0,8},{1,3},{2,10},{3,5},{4,12},{5,7},{6,14},{7,1},{8,16},{9,11},{... | collective-permute-start | bytes 786440 | tf_op jit(solution)/shard_map/ppermute | solution.py:52
  6.8 0.1 pad_add_fusion.place
  6.8 0.8 %copy-done.1 = s32[8,8,8]{2,1,0:T(8,128)S(1)} copy-done((s32[8,8,8]{2,1,0:T(8,128)S(1)}, s32[8,8,8]{2,1,0:T(8,128)}, u32[]{:S(2)}) %copy-start.1) | copy-done | bytes 2072
  7.6 0.7 copy-done.2
  8.3 0.7 copy-done.3
  9.0 0.7 copy-done.4
  9.7 0.7 copy-done.5
  10.3 0.7 copy-done.6
  11.0 2.1 %shard_map.100 = (s32[64,128]{1,0:T(8,128)S(1)}, f32[8,64]{1,0:T(8,128)S(1)}, s32[8,64]{1,0:T(8,128)S(1)}) custom-call(s32[4]{0:T(128)S(1)} %pad_add_fusion.place, s32[1024]{0:T(1024)S(1)} %copy-done.2, s32[150]{0:T(256)S(1)} %copy-done.4, s32[8,8,8]{2,1,0:T(8,128)S(1)} %copy-done.1, s32[2,32]{1,0:T(2,128)S(1)} %bitcast.17, f32[150]{0:T(256)S(1)} %copy-done.5, ...), custom_call_target="tpu_custom_call" | custom-call | flops 1 | bytes 1 | tf_op jit(solution)/shard_map/pallas_call | solution.py:320
  13.1 0.0 collective-permute-done.1.b2
  13.1 0.3 collective-permute-done.b1
  13.5 0.7 shard_map.102.after.p0
  14.1 4.0 %collective-permute-start.5 = (f32[64,4,8,128]{3,2,1,0:T(8,128)S(1)}, f32[64,4,8,128]{3,2,1,0:T(8,128)S(1)}, u32[]{:S(2)}, u32[]{:S(2)}) collective-permute-start(f32[64,4,8,128]{3,2,1,0:T(8,128)S(1)} %shard_map.102.after.p0), channel_id=1, source_target_pairs={{0,4},{1,17},{2,6},{3,19},{4,0},{5,21},{6,2},{7,23},{8,12},{9,25},... | collective-permute-start | bytes 3145736 | tf_op jit(solution)/shard_map/ppermute | solution.py:52
  18.1 0.7 %collective-permute-start.4 = (f32[64,4,8,128]{3,2,1,0:T(8,128)S(1)}, f32[64,4,8,128]{3,2,1,0:T(8,128)S(1)}, u32[]{:S(2)}, u32[]{:S(2)}) collective-permute-start(f32[64,4,8,128]{3,2,1,0:T(8,128)S(1)} %shard_map.102.after.p0), channel_id=1, source_target_pairs={{0,6},{1,25},{2,0},{3,27},{4,2},{5,29},{6,4},{7,31},{8,14},{9,1},{... | collective-permute-start | bytes 3145736 | tf_op jit(solution)/shard_map/ppermute | solution.py:52
  18.8 1.3 %collective-permute-start.3 = (f32[64,4,8,128]{3,2,1,0:T(8,128)S(1)}, f32[64,4,8,128]{3,2,1,0:T(8,128)S(1)}, u32[]{:S(2)}, u32[]{:S(2)}) collective-permute-start(f32[64,4,8,128]{3,2,1,0:T(8,128)S(1)} %shard_map.102.after.p0), channel_id=1, source_target_pairs={{0,2},{1,9},{2,4},{3,11},{4,6},{5,13},{6,0},{7,15},{8,10},{9,17},{... | collective-permute-start | bytes 3145736 | tf_op jit(solution)/shard_map/ppermute | solution.py:52
  20.1 0.1 fusion
  20.2 6.1 %shard_map.103 = (f32[8,8,64]{2,1,0:T(8,128)S(1)}, f32[8,8,64]{2,1,0:T(8,128)S(1)}, f32[8,8,64]{2,1,0:T(8,128)S(1)}, f32[8,8,64]{2,1,0:T(8,128)S(1)}) custom-call(s32[4]{0:T(128)S(1)} %pad_add_fusion.place, f32[32,8,4800]{2,1,0:T(8,128)} %amp_ref.1, f32[4,64,4800]{2,1,0:T(8,128)} %bitcast.19, f32[256,4]{1,0:T(8,128)S(1)} %broadcast_bitcast_fusion.choice_ref, ...), custom_call_target="tpu_custom_call" | custom-call | flops 1 | bytes 1 | tf_op jit(solution)/shard_map/pallas_call | solution.py:204
  26.4 1.6 %collective-permute-start.6 = (f32[8,8,64]{2,1,0:T(8,128)S(1)}, f32[8,8,64]{2,1,0:T(8,128)S(1)}, u32[]{:S(2)}, u32[]{:S(2)}) collective-permute-start(f32[8,8,64]{2,1,0:T(8,128)S(1)} %get-tuple-element.28), channel_id=1, source_target_pairs={{0,32},{1,33},{2,34},{3,35},{4,36},{5,37},{6,38},{7,39},{8,40},{9,... | collective-permute-start | bytes 49160 | tf_op jit(solution)/shard_map/ppermute | solution.py:52
  28.0 1.7 %collective-permute-start.7 = (f32[8,8,64]{2,1,0:T(8,128)S(1)}, f32[8,8,64]{2,1,0:T(8,128)S(1)}, u32[]{:S(2)}, u32[]{:S(2)}) collective-permute-start(f32[8,8,64]{2,1,0:T(8,128)S(1)} %get-tuple-element.29), channel_id=1, source_target_pairs={{0,96},{1,97},{2,98},{3,99},{4,100},{5,101},{6,102},{7,103},{8,104... | collective-permute-start | bytes 49160 | tf_op jit(solution)/shard_map/ppermute | solution.py:52
  29.7 1.9 %collective-permute-done.6.a1 = f32[8,8,64]{2,1,0:T(8,128)S(1)} collective-permute-done((f32[8,8,64]{2,1,0:T(8,128)S(1)}, f32[8,8,64]{2,1,0:T(8,128)S(1)}, u32[]{:S(2)}, u32[]{:S(2)}) %collective-permute-start.6) | collective-permute-done | bytes 16416 | tf_op jit(solution)/shard_map/ppermute | solution.py:52
  31.6 2.0 %collective-permute-start.8 = (f32[8,8,64]{2,1,0:T(8,128)S(1)}, f32[8,8,64]{2,1,0:T(8,128)S(1)}, u32[]{:S(2)}, u32[]{:S(2)}) collective-permute-start(f32[8,8,64]{2,1,0:T(8,128)S(1)} %get-tuple-element.30), channel_id=1, source_target_pairs={{0,64},{1,65},{2,66},{3,67},{4,68},{5,69},{6,70},{7,71},{8,72},{9,... | collective-permute-start | bytes 49160 | tf_op jit(solution)/shard_map/ppermute | solution.py:52
  33.6 6.8 %shard_map.104 = (bf16[64,512,256]{2,1,0:T(8,128)(2,1)S(1)}, f32[8,128]{1,0:T(8,128)S(1)}) custom-call(f32[64,256,256]{2,1,0:T(8,128)} %bitcast.18, f32[8,8,64]{2,1,0:T(8,128)S(1)} %get-tuple-element.26.after.a0), custom_call_target="tpu_custom_call" | custom-call | flops 1 | bytes 1 | tf_op jit(solution)/shard_map/pallas_call | solution.py:379
  40.3 0.0 collective-permute-done.7.a2
  40.4 0.6 shard_map.105
  40.9 2.2 %collective-permute-done.4.p2 = f32[64,4,8,128]{3,2,1,0:T(8,128)S(1)} collective-permute-done((f32[64,4,8,128]{3,2,1,0:T(8,128)S(1)}, f32[64,4,8,128]{3,2,1,0:T(8,128)S(1)}, u32[]{:S(2)}, u32[]{:S(2)}) %collective-permute-start.4) | collective-permute-done | bytes 1048608 | tf_op jit(solution)/shard_map/ppermute | solution.py:52
  43.2 0.8 %shard_map.106.rest_0_.mine = f32[32,16,8,128]{3,2,1,0:T(8,128)S(1)} custom-call(s32[4]{0:T(128)S(1)} %pad_add_fusion.place, f32[64,4,8,128]{3,2,1,0:T(8,128)S(1)} %shard_map.102.after.p0, f32[64,4,8,128]{3,2,1,0:T(8,128)S(1)} %collective-permute-done.3.p1, f32[64,4,8,128]{3,2,1,0:T(8,128)S(1)} %collective-permute-done.4.p2, ...), custom_call_target="tpu_custom_call" | custom-call | flops 1 | bytes 1 | tf_op jit(solution)/shard_map/pallas_call | solution.py:146
  44.0 0.1 collective-permute-start.10
  44.1 0.8 %shard_map.107.mine = f32[32,16,8,128]{3,2,1,0:T(8,128)S(1)} custom-call(s32[4]{0:T(128)S(1)} %pad_add_fusion.place, f32[64,4,8,128]{3,2,1,0:T(8,128)S(1)} %shard_map.102.after.p0, f32[64,4,8,128]{3,2,1,0:T(8,128)S(1)} %collective-permute-done.3.p1, f32[64,4,8,128]{3,2,1,0:T(8,128)S(1)} %collective-permute-done.4.p2, ...), custom_call_target="tpu_custom_call" | custom-call | flops 1 | bytes 1 | tf_op jit(solution)/shard_map/pallas_call | solution.py:146
  44.9 0.6 collective-permute-start.9
  45.5 0.5 collective-permute-start.11
  46.0 2.8 %collective-permute-start.12 = (f32[2,8,64]{2,1,0:T(8,128)S(1)}, f32[2,8,64]{2,1,0:T(8,128)S(1)}, u32[]{:S(2)}, u32[]{:S(2)}) collective-permute-start(f32[2,8,64]{2,1,0:T(8,128)S(1)} %get-tuple-element.34), channel_id=1, source_target_pairs={{0,24},{1,25},{2,26},{3,27},{4,28},{5,29},{6,30},{7,31},{8,0},{9,1... | collective-permute-start | bytes 12296 | tf_op jit(solution)/shard_map/ppermute | solution.py:52
  48.7 0.8 %collective-permute-start.13 = (f32[2,8,64]{2,1,0:T(8,128)S(1)}, f32[2,8,64]{2,1,0:T(8,128)S(1)}, u32[]{:S(2)}, u32[]{:S(2)}) collective-permute-start(f32[2,8,64]{2,1,0:T(8,128)S(1)} %get-tuple-element.35), channel_id=1, source_target_pairs={{0,16},{1,17},{2,18},{3,19},{4,20},{5,21},{6,22},{7,23},{8,24},{9,... | collective-permute-start | bytes 12296 | tf_op jit(solution)/shard_map/ppermute | solution.py:52
  49.5 3.4 %shard_map.108.rest_0_.before = f32[32,64]{1,0:T(8,128)S(1)} custom-call(s32[4]{0:T(128)S(1)} %pad_add_fusion.place, s32[64,128]{1,0:T(8,128)S(1)} %get-tuple-element.25.after.bound.before, bf16[64,512,256]{2,1,0:T(8,128)(2,1)S(1)} %get-tuple-element.27.slab, f32[32,16,8,128]{3,2,1,0:T(8,128)S(1)} %shard_map.106.rest_0_.mine, ...), custom_call_target="tpu_custom_call" | custom-call | flops 1 | bytes 1 | tf_op jit(solution)/shard_map/pallas_call | solution.py:453
  52.9 0.0 collective-permute-done.12.a2
  53.0 0.9 %collective-permute-done.13.a3 = f32[2,8,64]{2,1,0:T(8,128)S(1)} collective-permute-done((f32[2,8,64]{2,1,0:T(8,128)S(1)}, f32[2,8,64]{2,1,0:T(8,128)S(1)}, u32[]{:S(2)}, u32[]{:S(2)}) %collective-permute-start.13) | collective-permute-done | bytes 4128 | tf_op jit(solution)/shard_map/ppermute | solution.py:52
  53.9 0.5 shard_map.109
  54.5 3.4 %shard_map.110 = (f32[8,64]{1,0:T(8,128)S(1)}, f32[8,64]{1,0:T(8,128)S(1)}, f32[8,64]{1,0:T(8,128)S(1)}, f32[8,64]{1,0:T(8,128)S(1)}) custom-call(s32[4]{0:T(128)S(1)} %pad_add_fusion.place, s32[64,128]{1,0:T(8,128)S(1)} %get-tuple-element.25.after.bound.before, bf16[64,512,256]{2,1,0:T(8,128)(2,1)S(1)} %get-tuple-element.27.slab, ...), custom_call_target="tpu_custom_call" | custom-call | flops 1 | bytes 1 | tf_op jit(solution)/shard_map/pallas_call | solution.py:453
  57.9 1.6 %collective-permute-start.14 = (f32[8,64]{1,0:T(8,128)S(1)}, f32[8,64]{1,0:T(8,128)S(1)}, u32[]{:S(2)}, u32[]{:S(2)}) collective-permute-start(f32[8,64]{1,0:T(8,128)S(1)} %get-tuple-element.38), channel_id=1, source_target_pairs={{0,32},{1,33},{2,34},{3,35},{4,36},{5,37},{6,38},{7,39},{8,40},{9,... | collective-permute-start | bytes 6152 | tf_op jit(solution)/shard_map/ppermute | solution.py:52
  59.6 1.7 %collective-permute-start.15 = (f32[8,64]{1,0:T(8,128)S(1)}, f32[8,64]{1,0:T(8,128)S(1)}, u32[]{:S(2)}, u32[]{:S(2)}) collective-permute-start(f32[8,64]{1,0:T(8,128)S(1)} %get-tuple-element.39), channel_id=1, source_target_pairs={{0,96},{1,97},{2,98},{3,99},{4,100},{5,101},{6,102},{7,103},{8,104... | collective-permute-start | bytes 6152 | tf_op jit(solution)/shard_map/ppermute | solution.py:52
  61.2 2.0 %collective-permute-start.16 = (f32[8,64]{1,0:T(8,128)S(1)}, f32[8,64]{1,0:T(8,128)S(1)}, u32[]{:S(2)}, u32[]{:S(2)}) collective-permute-start(f32[8,64]{1,0:T(8,128)S(1)} %get-tuple-element.40), channel_id=1, source_target_pairs={{0,64},{1,65},{2,66},{3,67},{4,68},{5,69},{6,70},{7,71},{8,72},{9,... | collective-permute-start | bytes 6152 | tf_op jit(solution)/shard_map/ppermute | solution.py:52
  63.2 2.5 %collective-permute-start.17 = (f32[8,64]{1,0:T(8,128)S(1)}, f32[8,64]{1,0:T(8,128)S(1)}, u32[]{:S(2)}, u32[]{:S(2)}) collective-permute-start(f32[8,64]{1,0:T(8,128)S(1)} %get-tuple-element.41), channel_id=1, source_target_pairs={{0,4},{1,5},{2,6},{3,7},{4,0},{5,1},{6,2},{7,3},{8,12},{9,13},{10,... | collective-permute-start | bytes 6152 | tf_op jit(solution)/shard_map/ppermute | solution.py:52
  65.7 0.7 collective-permute-done.16
  66.3 2.0 %collective-permute-done.17 = f32[8,64]{1,0:T(8,128)S(1)} collective-permute-done((f32[8,64]{1,0:T(8,128)S(1)}, f32[8,64]{1,0:T(8,128)S(1)}, u32[]{:S(2)}, u32[]{:S(2)}) %collective-permute-start.17) | collective-permute-done | bytes 2080 | tf_op jit(solution)/shard_map/ppermute | solution.py:52
  68.3 0.6 select_bitcast_fusion
  (18 shorter events, 0.1 us)
Async XLA Ops:
  0.0 0.9 %copy-start = (f32[32,256,8]{1,2,0:T(8,128)S(1)}, f32[32,256,8]{1,2,0:T(8,128)}, u32[]{:S(2)}) copy-start(f32[32,256,8]{1,2,0:T(8,128)} %param.16) | copy-start | bytes 786436
  1.5 11.5 %collective-permute-start.2 = (f32[64,8,128]{2,1,0:T(8,128)S(1)}, f32[64,8,128]{2,1,0:T(8,128)S(1)}, u32[]{:S(2)}, u32[]{:S(2)}) collective-permute-start(f32[64,8,128]{2,1,0:T(8,128)S(1)} %shard_map.101.b0), channel_id=1, source_target_pairs={{0,16},{1,5},{2,18},{3,7},{4,20},{5,1},{6,22},{7,3},{8,24},{9,13},... | collective-permute-start | bytes 786440 | tf_op jit(solution)/shard_map/ppermute | solution.py:52
  4.7 8.4 %collective-permute-start.1 = (f32[64,8,128]{2,1,0:T(8,128)S(1)}, f32[64,8,128]{2,1,0:T(8,128)S(1)}, u32[]{:S(2)}, u32[]{:S(2)}) collective-permute-start(f32[64,8,128]{2,1,0:T(8,128)S(1)} %shard_map.101.b0), channel_id=1, source_target_pairs={{0,24},{1,7},{2,26},{3,1},{4,28},{5,3},{6,30},{7,5},{8,0},{9,15},{... | collective-permute-start | bytes 786440 | tf_op jit(solution)/shard_map/ppermute | solution.py:52
  5.9 7.6 %collective-permute-start = (f32[64,8,128]{2,1,0:T(8,128)S(1)}, f32[64,8,128]{2,1,0:T(8,128)S(1)}, u32[]{:S(2)}, u32[]{:S(2)}) collective-permute-start(f32[64,8,128]{2,1,0:T(8,128)S(1)} %shard_map.101.b0), channel_id=1, source_target_pairs={{0,8},{1,3},{2,10},{3,5},{4,12},{5,7},{6,14},{7,1},{8,16},{9,11},{... | collective-permute-start | bytes 786440 | tf_op jit(solution)/shard_map/ppermute | solution.py:52
  6.8 0.8 %copy-start.1 = (s32[8,8,8]{2,1,0:T(8,128)S(1)}, s32[8,8,8]{2,1,0:T(8,128)}, u32[]{:S(2)}) copy-start(s32[8,8,8]{2,1,0:T(8,128)} %allowed.1) | copy-start | bytes 6148
  7.6 0.7 copy-start.2
  8.3 0.7 copy-start.3
  9.0 0.7 copy-start.4
  9.7 0.7 copy-start.5
  10.3 0.7 copy-start.6
  14.1 26.8 %collective-permute-start.5 = (f32[64,4,8,128]{3,2,1,0:T(8,128)S(1)}, f32[64,4,8,128]{3,2,1,0:T(8,128)S(1)}, u32[]{:S(2)}, u32[]{:S(2)}) collective-permute-start(f32[64,4,8,128]{3,2,1,0:T(8,128)S(1)} %shard_map.102.after.p0), channel_id=1, source_target_pairs={{0,4},{1,17},{2,6},{3,19},{4,0},{5,21},{6,2},{7,23},{8,12},{9,25},... | collective-permute-start | bytes 3145736 | tf_op jit(solution)/shard_map/ppermute | solution.py:52
  18.1 25.1 %collective-permute-start.4 = (f32[64,4,8,128]{3,2,1,0:T(8,128)S(1)}, f32[64,4,8,128]{3,2,1,0:T(8,128)S(1)}, u32[]{:S(2)}, u32[]{:S(2)}) collective-permute-start(f32[64,4,8,128]{3,2,1,0:T(8,128)S(1)} %shard_map.102.after.p0), channel_id=1, source_target_pairs={{0,6},{1,25},{2,0},{3,27},{4,2},{5,29},{6,4},{7,31},{8,14},{9,1},{... | collective-permute-start | bytes 3145736 | tf_op jit(solution)/shard_map/ppermute | solution.py:52
  18.8 24.4 %collective-permute-start.3 = (f32[64,4,8,128]{3,2,1,0:T(8,128)S(1)}, f32[64,4,8,128]{3,2,1,0:T(8,128)S(1)}, u32[]{:S(2)}, u32[]{:S(2)}) collective-permute-start(f32[64,4,8,128]{3,2,1,0:T(8,128)S(1)} %shard_map.102.after.p0), channel_id=1, source_target_pairs={{0,2},{1,9},{2,4},{3,11},{4,6},{5,13},{6,0},{7,15},{8,10},{9,17},{... | collective-permute-start | bytes 3145736 | tf_op jit(solution)/shard_map/ppermute | solution.py:52
  26.4 5.2 %collective-permute-start.6 = (f32[8,8,64]{2,1,0:T(8,128)S(1)}, f32[8,8,64]{2,1,0:T(8,128)S(1)}, u32[]{:S(2)}, u32[]{:S(2)}) collective-permute-start(f32[8,8,64]{2,1,0:T(8,128)S(1)} %get-tuple-element.28), channel_id=1, source_target_pairs={{0,32},{1,33},{2,34},{3,35},{4,36},{5,37},{6,38},{7,39},{8,40},{9,... | collective-permute-start | bytes 49160 | tf_op jit(solution)/shard_map/ppermute | solution.py:52
  28.0 12.3 %collective-permute-start.7 = (f32[8,8,64]{2,1,0:T(8,128)S(1)}, f32[8,8,64]{2,1,0:T(8,128)S(1)}, u32[]{:S(2)}, u32[]{:S(2)}) collective-permute-start(f32[8,8,64]{2,1,0:T(8,128)S(1)} %get-tuple-element.29), channel_id=1, source_target_pairs={{0,96},{1,97},{2,98},{3,99},{4,100},{5,101},{6,102},{7,103},{8,104... | collective-permute-start | bytes 49160 | tf_op jit(solution)/shard_map/ppermute | solution.py:52
  31.6 8.8 %collective-permute-start.8 = (f32[8,8,64]{2,1,0:T(8,128)S(1)}, f32[8,8,64]{2,1,0:T(8,128)S(1)}, u32[]{:S(2)}, u32[]{:S(2)}) collective-permute-start(f32[8,8,64]{2,1,0:T(8,128)S(1)} %get-tuple-element.30), channel_id=1, source_target_pairs={{0,64},{1,65},{2,66},{3,67},{4,68},{5,69},{6,70},{7,71},{8,72},{9,... | collective-permute-start | bytes 49160 | tf_op jit(solution)/shard_map/ppermute | solution.py:52
  44.0 5.5 %collective-permute-start.10 = (f32[32,16,8,128]{3,2,1,0:T(8,128)S(1)}, f32[32,16,8,128]{3,2,1,0:T(8,128)S(1)}, u32[]{:S(2)}, u32[]{:S(2)}) collective-permute-start(f32[32,16,8,128]{3,2,1,0:T(8,128)S(1)} %shard_map.106.rest_0_.mine), channel_id=1, source_target_pairs={{0,1},{1,0},{2,3},{3,2},{4,5},{5,4},{6,7},{7,6},{8,9},{9,8},{10,11... | collective-permute-start | bytes 6291464 | tf_op jit(solution)/shard_map/ppermute | solution.py:52
  44.9 9.5 %collective-permute-start.9 = (f32[32,16,8,128]{3,2,1,0:T(8,128)S(1)}, f32[32,16,8,128]{3,2,1,0:T(8,128)S(1)}, u32[]{:S(2)}, u32[]{:S(2)}) collective-permute-start(f32[32,16,8,128]{3,2,1,0:T(8,128)S(1)} %shard_map.107.mine), channel_id=1, source_target_pairs={{0,1},{1,0},{2,3},{3,2},{4,5},{5,4},{6,7},{7,6},{8,9},{9,8},{10,11... | collective-permute-start | bytes 6291464 | tf_op jit(solution)/shard_map/ppermute | solution.py:52
  45.5 7.4 %collective-permute-start.11 = (f32[2,8,64]{2,1,0:T(8,128)S(1)}, f32[2,8,64]{2,1,0:T(8,128)S(1)}, u32[]{:S(2)}, u32[]{:S(2)}) collective-permute-start(f32[2,8,64]{2,1,0:T(8,128)S(1)} %get-tuple-element.33), channel_id=1, source_target_pairs={{0,8},{1,9},{2,10},{3,11},{4,12},{5,13},{6,14},{7,15},{8,16},{9,17... | collective-permute-start | bytes 12296 | tf_op jit(solution)/shard_map/ppermute | solution.py:52
  46.0 7.0 %collective-permute-start.12 = (f32[2,8,64]{2,1,0:T(8,128)S(1)}, f32[2,8,64]{2,1,0:T(8,128)S(1)}, u32[]{:S(2)}, u32[]{:S(2)}) collective-permute-start(f32[2,8,64]{2,1,0:T(8,128)S(1)} %get-tuple-element.34), channel_id=1, source_target_pairs={{0,24},{1,25},{2,26},{3,27},{4,28},{5,29},{6,30},{7,31},{8,0},{9,1... | collective-permute-start | bytes 12296 | tf_op jit(solution)/shard_map/ppermute | solution.py:52
  48.7 5.2 %collective-permute-start.13 = (f32[2,8,64]{2,1,0:T(8,128)S(1)}, f32[2,8,64]{2,1,0:T(8,128)S(1)}, u32[]{:S(2)}, u32[]{:S(2)}) collective-permute-start(f32[2,8,64]{2,1,0:T(8,128)S(1)} %get-tuple-element.35), channel_id=1, source_target_pairs={{0,16},{1,17},{2,18},{3,19},{4,20},{5,21},{6,22},{7,23},{8,24},{9,... | collective-permute-start | bytes 12296 | tf_op jit(solution)/shard_map/ppermute | solution.py:52
  57.9 7.8 %collective-permute-start.14 = (f32[8,64]{1,0:T(8,128)S(1)}, f32[8,64]{1,0:T(8,128)S(1)}, u32[]{:S(2)}, u32[]{:S(2)}) collective-permute-start(f32[8,64]{1,0:T(8,128)S(1)} %get-tuple-element.38), channel_id=1, source_target_pairs={{0,32},{1,33},{2,34},{3,35},{4,36},{5,37},{6,38},{7,39},{8,40},{9,... | collective-permute-start | bytes 6152 | tf_op jit(solution)/shard_map/ppermute | solution.py:52
  59.6 6.1 %collective-permute-start.15 = (f32[8,64]{1,0:T(8,128)S(1)}, f32[8,64]{1,0:T(8,128)S(1)}, u32[]{:S(2)}, u32[]{:S(2)}) collective-permute-start(f32[8,64]{1,0:T(8,128)S(1)} %get-tuple-element.39), channel_id=1, source_target_pairs={{0,96},{1,97},{2,98},{3,99},{4,100},{5,101},{6,102},{7,103},{8,104... | collective-permute-start | bytes 6152 | tf_op jit(solution)/shard_map/ppermute | solution.py:52
  61.2 5.1 %collective-permute-start.16 = (f32[8,64]{1,0:T(8,128)S(1)}, f32[8,64]{1,0:T(8,128)S(1)}, u32[]{:S(2)}, u32[]{:S(2)}) collective-permute-start(f32[8,64]{1,0:T(8,128)S(1)} %get-tuple-element.40), channel_id=1, source_target_pairs={{0,64},{1,65},{2,66},{3,67},{4,68},{5,69},{6,70},{7,71},{8,72},{9,... | collective-permute-start | bytes 6152 | tf_op jit(solution)/shard_map/ppermute | solution.py:52
  63.2 5.1 %collective-permute-start.17 = (f32[8,64]{1,0:T(8,128)S(1)}, f32[8,64]{1,0:T(8,128)S(1)}, u32[]{:S(2)}, u32[]{:S(2)}) collective-permute-start(f32[8,64]{1,0:T(8,128)S(1)} %get-tuple-element.41), channel_id=1, source_target_pairs={{0,4},{1,5},{2,6},{3,7},{4,0},{5,1},{6,2},{7,3},{8,12},{9,13},{10,... | collective-permute-start | bytes 6152 | tf_op jit(solution)/shard_map/ppermute | solution.py:52

commit v3 on v2

--- a/solution.py
+++ b/solution.py
@@ -131,23 +131,26 @@
 CHUNKS = (32, 32)
 
 
-def pack_body(base, place, p0, p1, p2, p3, *rest):
-    out = rest[-1]
-    count = out.shape[0]
+def pack_body(place, p0, p1, p2, p3, *rest):
+    out = rest[-len(CHUNKS) :]
     x, z, core = place[1], place[2], place[3]
-    for piece, shift in ((p0, 0), (p1, 3), (p2, 1), (p3, 2)):
-        first = jnp.where(core == 0, lax.rem(z + shift, 4), lax.rem(x + shift, 4) * 4)
-        for i in range(4):
-            out[:, pl.ds(first + i * jnp.where(core == 0, 4, 1), 1)] = piece[base : base + count, i : i + 1]
-
-
-def pack(place, pieces, base, count, after):
+    base = 0
+    for o in out:
+        count = o.shape[0]
+        for piece, shift in ((p0, 0), (p1, 3), (p2, 1), (p3, 2)):
+            first = jnp.where(core == 0, lax.rem(z + shift, 4), lax.rem(x + shift, 4) * 4)
+            for i in range(4):
+                o[:, pl.ds(first + i * jnp.where(core == 0, 4, 1), 1)] = piece[base : base + count, i : i + 1]
+        base += count
+
+
+def pack(place, pieces, after):
     _, _, slots, lanes = pieces[0].shape
     return pl.pallas_call(
-        functools.partial(pack_body, base),
-        out_shape=jax.ShapeDtypeStruct((count, 16, slots, lanes), F32),
+        pack_body,
+        out_shape=tuple(jax.ShapeDtypeStruct((n, 16, slots, lanes), F32) for n in CHUNKS),
         in_specs=[smem()] + [vmem()] * 4 + [anywhere()] * len(after),
-        out_specs=vmem(),
+        out_specs=(vmem(),) * len(CHUNKS),
         compiler_params=grant(12),
         cost_estimate=small_cost(),
     )(place, *pieces, *after)
@@ -165,7 +168,7 @@
 DEPTH_BLOCK = 1280
 
 
-def cycle_body(depth, place, amp_ref, int_ref, choice_ref, after, o0, o1, o2, o3, acc, by_row):
+def cycle_body(depth, place, amp_ref, int_ref, choice_ref, o0, o1, o2, o3, acc, by_row):
     step = pl.program_id(0)
     window, width, block = int_ref.shape
     pairs, rows, _ = amp_ref.shape
@@ -196,7 +199,7 @@
                 out[a] = by_row[pl.ds(at + a, own, stride=rows), :]
 
 
-def cycle(place, amp, ints, choice, after):
+def cycle(place, amp, ints, choice):
     pairs, rows, depth = amp.shape
     window, width, _ = ints.shape
     part = jax.ShapeDtypeStruct((rows, pairs // 4, width), F32)
@@ -210,7 +213,6 @@
             pl.BlockSpec((pairs, rows, DEPTH_BLOCK), lambda i: (0, 0, i)),
             pl.BlockSpec((window, width, DEPTH_BLOCK), lambda i: (0, 0, i)),
             pl.BlockSpec((pairs * rows, window), lambda i: (0, 0)),
-            anywhere(),
         ],
         out_specs=(whole,) * 4,
         scratch_shapes=[
@@ -219,50 +221,50 @@
         ],
         compiler_params=grant(24),
         cost_estimate=small_cost(),
-    )(place, in_hbm(amp), in_hbm(ints), choice, after)
-
-
-def rows_body(place, a0, a1, a2, a3, *rest):
-    o0, o1, o2, o3, held = rest[-5:]
+    )(place, in_hbm(amp), in_hbm(ints), choice)
+
+
+def by_half_body(place, a0, a1, a2, a3, after, keep, away, held):
     held[...] = a0[...] + a1[...] + a2[...] + a3[...]
+    half = lax.div(place[2], 2)
+    for x in range(4):
+        keep[pl.ds(x, 1)] = held[pl.ds(2 * x + half, 1)]
+        away[pl.ds(x, 1)] = held[pl.ds(2 * x + 1 - half, 1)]
+
+
+def by_half(place, parts, after):
+    count, own, width = parts[0].shape
+    return pl.pallas_call(
+        by_half_body,
+        out_shape=(jax.ShapeDtypeStruct((count // 2, own, width), F32),) * 2,
+        in_specs=[smem()] + [vmem()] * 4 + [anywhere()],
+        out_specs=(vmem(),) * 2,
+        scratch_shapes=[pltpu.VMEM((count, own, width), F32)],
+        compiler_params=grant(8),
+        cost_estimate=small_cost(),
+    )(place, *parts, after)
+
+
+def by_row_body(place, keep, got, after, o0, o1, o2, o3, held):
+    held[...] = keep[...] + got[...]
     for out, shift in ((o0, 0), (o1, 1), (o2, 3), (o3, 2)):
-        out[...] = held[pl.ds(lax.rem(place[1] + shift, 4) * 2, 2)]
-
-
-def rows(place, parts, after):
-    count, own, width = parts[0].shape
-    return pl.pallas_call(
-        rows_body,
-        out_shape=(jax.ShapeDtypeStruct((count // 4, own, width), F32),) * 4,
-        in_specs=[smem()] + [vmem()] * 4 + [anywhere()] * len(after),
+        out[...] = held[lax.rem(place[1] + shift, 4)]
+
+
+def by_row(place, keep, got, after):
+    count, own, width = keep.shape
+    return pl.pallas_call(
+        by_row_body,
+        out_shape=(jax.ShapeDtypeStruct((own, width), F32),) * 4,
+        in_specs=[smem()] + [vmem()] * 2 + [anywhere()],
         out_specs=(vmem(),) * 4,
         scratch_shapes=[pltpu.VMEM((count, own, width), F32)],
         compiler_params=grant(8),
         cost_estimate=small_cost(),
-    )(place, *parts, *after)
-
-
-def halves_body(place, a0, a1, a2, a3, *rest):
-    keep, away = rest[-2:]
-    half = lax.div(place[2], 2)
-    total = a0[...] + a1[...] + a2[...] + a3[...]
-    keep[...] = jnp.where(half == 0, total[0], total[1])
-    away[...] = jnp.where(half == 0, total[1], total[0])
-
-
-def halves(place, parts, after):
-    one = jax.ShapeDtypeStruct(parts[0].shape[1:], F32)
-    return pl.pallas_call(
-        halves_body,
-        out_shape=(one, one),
-        in_specs=[smem()] + [vmem()] * 4 + [anywhere()] * len(after),
-        out_specs=(vmem(), vmem()),
-        compiler_params=grant(8),
-        cost_estimate=small_cost(),
-    )(place, *parts, *after)
-
-
-def labels_body(place, vir, occ, allowed, pair_list, occ_e, vir_e, vir_tile, bound, denom, live):
+    )(place, keep, got, after)
+
+
+def labels_body(place, vir, occ, allowed, pair_list, occ_e, vir_e, vir_tile, after, bound, denom, live):
     y, x, z, core = place[0], place[1], place[2], place[3]
     row = x * 2 + lax.div(z, 2)
     column = lax.rem(z, 2) * 2 + core
@@ -315,7 +317,7 @@
     live[...] = (slot < count_b).astype(jnp.int32)
 
 
-def labels(place, vir, occ, allowed, pair_list, occ_e, vir_e, width, own, pairs):
+def labels(place, vir, occ, allowed, pair_list, occ_e, vir_e, width, own, pairs, after):
     total = vir.shape[0]
     return pl.pallas_call(
         labels_body,
@@ -324,11 +326,11 @@
             jax.ShapeDtypeStruct((own, width), F32),
             jax.ShapeDtypeStruct((own, width), jnp.int32),
         ),
-        in_specs=[smem()] * 7 + [vmem()],
+        in_specs=[smem()] * 7 + [vmem(), anywhere()],
         out_specs=(vmem(),) * 3,
         compiler_params=grant(8),
         cost_estimate=small_cost(),
-    )(place, vir, occ, allowed, pair_list.T, occ_e, vir_e, vir.reshape(8, total // 8))
+    )(place, *(in_hbm(v) for v in (vir, occ, allowed, pair_list.T, occ_e, vir_e)), vir.reshape(8, total // 8), after)
 
 
 READY = 4
@@ -476,30 +478,26 @@
     own = pairs // 4
 
     mine = relayout(jnp.transpose(ladder_amp, (0, 2, 1)))
-    bound, denom, live = labels(place, vir, occ, allowed, pair_list, occ_e, vir_e, width, own, pairs)
-    line = stack(place, [mine] + [send(mine, FIRST[n]) for n in (1, -1, 2)], bound)
-    pieces = [line] + [send(line, SECOND[n]) for n in (1, -1, 2)]
-
+    blocks = [mine] + [send(mine, FIRST[n]) for n in (1, -1, 2)]
     choice = (pair_list[:, 1:] == jnp.arange(cycle_int.shape[1], dtype=jnp.int32)).astype(F32)
     choice = jnp.repeat(choice, cycle_amp.shape[1], axis=0)
-    parts = cycle(place, cycle_amp, jnp.transpose(cycle_int, (1, 2, 0)), choice, line)
-    slab, token = ready(in_hbm(int_slab.reshape(int_slab.shape[1:])), parts[0])
-
-    parts = rows(place, spread(parts, ALONG_Y), (token,))
-    base, sums, last_packed, keep = 0, bound, parts[0], parts[0]
+    parts = cycle(place, cycle_amp, jnp.transpose(cycle_int, (1, 2, 0)), choice)
+    line = stack(place, blocks, parts[0])
+    pieces = [line] + [send(line, SECOND[n]) for n in (1, -1, 2)]
+    bound, denom, live = labels(place, vir, occ, allowed, pair_list, occ_e, vir_e, width, own, pairs, line)
+    keep, away = by_half(place, spread(parts, ALONG_Y), line)
+    got = send(away, Z_ACROSS)
+    slab, token = ready(in_hbm(int_slab.reshape(int_slab.shape[1:])), keep)
+
+    chunks = pack(place, pieces, (token, got, bound))
+    others = [send(v, SWAP) for v in chunks]
+    parts = spread(by_row(place, keep, got, chunks[0]), ALONG_X)
+    base, sums = 0, bound
     for i, count in enumerate(CHUNKS):
-        packed = pack(place, pieces, base, count, (last_packed,))
-        other = send(packed, SWAP)
-        if i == 0:
-            parts = spread(parts, ALONG_X)
-        sums = ladder(place, bound, slab, packed, other, base, sums, keep, i == len(CHUNKS) - 1)
-        if i == 0:
-            keep, away = halves(place, parts, (sums,))
-            got = send(away, Z_ACROSS)
+        sums = ladder(place, bound, slab, chunks[i], others[i], base, sums, parts[0], i == len(CHUNKS) - 1)
         base += count
-        last_packed = packed
     s0, s1, s2, s3 = spread(sums, ALONG_Y)
-    total = (s0 + s1) + (s2 + s3) + (keep + got)
+    total = (s0 + s1) + (s2 + s3) + (parts[0] + parts[1]) + (parts[2] + parts[3])
     return jnp.where(live > 0, total / denom, jnp.float32(0.0))[None]
 
 

time: 69.3 us -> 66.1 us (0.954)
  local copies, waits for them, and re-layouts: 5.13 us -> 1.64 us
  waiting for transfers between devices: 8.1 us -> 10.4 us
  starting transfers between devices: 28.9 us -> 27.3 us
    unnamed x14 -> x2, local copies, waits for them, and re-layouts: 5.12 us -> 0.95 us
    ppermute x18, waiting for transfers between devices: 8.1 us -> 10.4 us  [send(): return lax.ppermute(value, AXES, pairs)]
    ppermute x18, starting transfers between devices: 28.9 us -> 27.3 us  [send(): return lax.ppermute(value, AXES, pairs)]
    pallas_call x4 -> x3, Pallas kernels: 2.77 us -> 2.24 us  [the longest x1 1.13 us: pack(): pl.pallas_call(pack_body, out_shape=tuple((jax.ShapeDtypeStruct((n, 16, s...]
  transfers between devices with their start and end apart: 18 -> 18, of which waited for: 6 -> 5; matrix products, arithmetic and copies ran while one was open for 0% -> 1% of each run, Pallas kernels for 30% -> 35%
where the time goes in v3:
time: 66.1 us; the launch traced here: 65.8 us
  starting transfers between devices  27.3 us (41%)
  Pallas kernels  25.6 us (39%)
  waiting for transfers between devices  10.4 us (16%)
  local copies, waits for them, and re-layouts  1.64 us (2%)
  other arithmetic  0.75 us (1%)
    ppermute x18, starting transfers between devices, send(): return lax.ppermute(value, AXES, pairs)  27.3 us
    ppermute x18, waiting for transfers between devices, send(): return lax.ppermute(value, AXES, pairs)  10.4 us
    pallas_call x2, Pallas kernels, ladder(): pl.pallas_call(functools.partial(ladder_body, last, base), out_shape=out_...  6.91 us
    pallas_call x1, Pallas kernels, ready(): pl.pallas_call(ready_body, out_shape=(jax.ShapeDtypeStruct((cells // CELL...  6.77 us
    pallas_call x1, Pallas kernels, cycle(): pl.pallas_call(functools.partial(cycle_body, depth), grid=(pl.cdiv(depth,...  6.15 us
    pallas_call x1, Pallas kernels, labels(): pl.pallas_call(labels_body, out_shape=(jax.ShapeDtypeStruct((total // 4 /...  2.21 us
  transfers between devices with their start and end apart: 18, of which 5 were waited for; matrix products, arithmetic and copies ran while one was open for 1% of the time, Pallas kernels for 35%

profile of v3, /device:TPU:0, one launch (start us, length us, event | category | flops | bytes accessed | tf_op | source)
XLA Modules:
  0.0 65.8 jit_solution(18351057239342030812)
XLA Ops:
  0.0 0.9 %copy-done = f32[32,256,8]{1,2,0:T(8,128)S(1)} copy-done((f32[32,256,8]{1,2,0:T(8,128)S(1)}, f32[32,256,8]{1,2,0:T(8,128)}, u32[]{:S(2)}) %copy-start) | copy-done | bytes 262168
  1.0 0.6 shard_map.100.b0
  1.5 3.2 %collective-permute-start.2 = (f32[64,8,128]{2,1,0:T(8,128)S(1)}, f32[64,8,128]{2,1,0:T(8,128)S(1)}, u32[]{:S(2)}, u32[]{:S(2)}) collective-permute-start(f32[64,8,128]{2,1,0:T(8,128)S(1)} %shard_map.100.b0), channel_id=1, source_target_pairs={{0,16},{1,5},{2,18},{3,7},{4,20},{5,1},{6,22},{7,3},{8,24},{9,13},... | collective-permute-start | bytes 786440 | tf_op jit(solution)/shard_map/ppermute | solution.py:52
  4.7 1.1 %collective-permute-start.1 = (f32[64,8,128]{2,1,0:T(8,128)S(1)}, f32[64,8,128]{2,1,0:T(8,128)S(1)}, u32[]{:S(2)}, u32[]{:S(2)}) collective-permute-start(f32[64,8,128]{2,1,0:T(8,128)S(1)} %shard_map.100.b0), channel_id=1, source_target_pairs={{0,24},{1,7},{2,26},{3,1},{4,28},{5,3},{6,30},{7,5},{8,0},{9,15},{... | collective-permute-start | bytes 786440 | tf_op jit(solution)/shard_map/ppermute | solution.py:52
  5.9 0.9 %collective-permute-start = (f32[64,8,128]{2,1,0:T(8,128)S(1)}, f32[64,8,128]{2,1,0:T(8,128)S(1)}, u32[]{:S(2)}, u32[]{:S(2)}) collective-permute-start(f32[64,8,128]{2,1,0:T(8,128)S(1)} %shard_map.100.b0), channel_id=1, source_target_pairs={{0,8},{1,3},{2,10},{3,5},{4,12},{5,7},{6,14},{7,1},{8,16},{9,11},{... | collective-permute-start | bytes 786440 | tf_op jit(solution)/shard_map/ppermute | solution.py:52
  6.8 0.7 %slice_bitcast_fusion = s32[32]{0:T(128)S(1)} fusion(s32[32,2]{0,1:T(2,128)} %param.13), kind=kLoop, calls=%fused_computation.5 | loop fusion | bytes 256 | tf_op jit(solution)/shard_map/eq | solution.py:482
  7.4 0.1 fusion
  7.5 0.1 pad_add_fusion.place
  7.6 6.1 %shard_map.101 = (f32[8,8,64]{2,1,0:T(8,128)S(1)}, f32[8,8,64]{2,1,0:T(8,128)S(1)}, f32[8,8,64]{2,1,0:T(8,128)S(1)}, f32[8,8,64]{2,1,0:T(8,128)S(1)}) custom-call(s32[4]{0:T(128)S(1)} %pad_add_fusion.place, f32[32,8,4800]{2,1,0:T(8,128)} %amp_ref.1, f32[4,64,4800]{2,1,0:T(8,128)} %bitcast.17, f32[256,4]{1,0:T(8,128)S(1)} %broadcast_bitcast_fusion.choice_ref), custom_call_target="tpu_custom_call" | custom-call | flops 1 | bytes 1 | tf_op jit(solution)/shard_map/pallas_call | solution.py:207
  13.8 0.0 collective-permute-done.2.b3
  13.8 0.0 collective-permute-done.1.b2
  13.8 0.0 collective-permute-done.b1
  13.8 0.7 %shard_map.102.after.p0 = f32[64,4,8,128]{3,2,1,0:T(8,128)S(1)} custom-call(s32[4]{0:T(128)S(1)} %pad_add_fusion.place, f32[64,8,128]{2,1,0:T(8,128)S(1)} %shard_map.100.b0, f32[64,8,128]{2,1,0:T(8,128)S(1)} %collective-permute-done.b1, f32[64,8,128]{2,1,0:T(8,128)S(1)} %collective-permute-done.1.b2, f32[64,8,128]{2,1,0:T(8,128)S(1)} %collective-permute-done.2.b3, ...), custom_call_target="tpu_custom_call" | custom-call | flops 1 | bytes 1 | tf_op jit(solution)/shard_map/pallas_call | solution.py:121
  14.5 4.0 %collective-permute-start.8 = (f32[64,4,8,128]{3,2,1,0:T(8,128)S(1)}, f32[64,4,8,128]{3,2,1,0:T(8,128)S(1)}, u32[]{:S(2)}, u32[]{:S(2)}) collective-permute-start(f32[64,4,8,128]{3,2,1,0:T(8,128)S(1)} %shard_map.102.after.p0), channel_id=1, source_target_pairs={{0,4},{1,17},{2,6},{3,19},{4,0},{5,21},{6,2},{7,23},{8,12},{9,25},... | collective-permute-start | bytes 3145736 | tf_op jit(solution)/shard_map/ppermute | solution.py:52
  18.4 0.7 %collective-permute-start.7 = (f32[64,4,8,128]{3,2,1,0:T(8,128)S(1)}, f32[64,4,8,128]{3,2,1,0:T(8,128)S(1)}, u32[]{:S(2)}, u32[]{:S(2)}) collective-permute-start(f32[64,4,8,128]{3,2,1,0:T(8,128)S(1)} %shard_map.102.after.p0), channel_id=1, source_target_pairs={{0,6},{1,25},{2,0},{3,27},{4,2},{5,29},{6,4},{7,31},{8,14},{9,1},{... | collective-permute-start | bytes 3145736 | tf_op jit(solution)/shard_map/ppermute | solution.py:52
  19.2 1.3 %collective-permute-start.6 = (f32[64,4,8,128]{3,2,1,0:T(8,128)S(1)}, f32[64,4,8,128]{3,2,1,0:T(8,128)S(1)}, u32[]{:S(2)}, u32[]{:S(2)}) collective-permute-start(f32[64,4,8,128]{3,2,1,0:T(8,128)S(1)} %shard_map.102.after.p0), channel_id=1, source_target_pairs={{0,2},{1,9},{2,4},{3,11},{4,6},{5,13},{6,0},{7,15},{8,10},{9,17},{... | collective-permute-start | bytes 3145736 | tf_op jit(solution)/shard_map/ppermute | solution.py:52
  20.5 1.6 %collective-permute-start.3 = (f32[8,8,64]{2,1,0:T(8,128)S(1)}, f32[8,8,64]{2,1,0:T(8,128)S(1)}, u32[]{:S(2)}, u32[]{:S(2)}) collective-permute-start(f32[8,8,64]{2,1,0:T(8,128)S(1)} %get-tuple-element.29), channel_id=1, source_target_pairs={{0,32},{1,33},{2,34},{3,35},{4,36},{5,37},{6,38},{7,39},{8,40},{9,... | collective-permute-start | bytes 49160 | tf_op jit(solution)/shard_map/ppermute | solution.py:52
  22.1 1.7 %collective-permute-start.4 = (f32[8,8,64]{2,1,0:T(8,128)S(1)}, f32[8,8,64]{2,1,0:T(8,128)S(1)}, u32[]{:S(2)}, u32[]{:S(2)}) collective-permute-start(f32[8,8,64]{2,1,0:T(8,128)S(1)} %get-tuple-element.30), channel_id=1, source_target_pairs={{0,96},{1,97},{2,98},{3,99},{4,100},{5,101},{6,102},{7,103},{8,104... | collective-permute-start | bytes 49160 | tf_op jit(solution)/shard_map/ppermute | solution.py:52
  23.7 1.9 %collective-permute-done.3.a1 = f32[8,8,64]{2,1,0:T(8,128)S(1)} collective-permute-done((f32[8,8,64]{2,1,0:T(8,128)S(1)}, f32[8,8,64]{2,1,0:T(8,128)S(1)}, u32[]{:S(2)}, u32[]{:S(2)}) %collective-permute-start.3) | collective-permute-done | bytes 16416 | tf_op jit(solution)/shard_map/ppermute | solution.py:52
  25.6 2.0 %collective-permute-start.5 = (f32[8,8,64]{2,1,0:T(8,128)S(1)}, f32[8,8,64]{2,1,0:T(8,128)S(1)}, u32[]{:S(2)}, u32[]{:S(2)}) collective-permute-start(f32[8,8,64]{2,1,0:T(8,128)S(1)} %get-tuple-element.31), channel_id=1, source_target_pairs={{0,64},{1,65},{2,66},{3,67},{4,68},{5,69},{6,70},{7,71},{8,72},{9,... | collective-permute-start | bytes 49160 | tf_op jit(solution)/shard_map/ppermute | solution.py:52
  27.6 0.0 collective-permute-done.4.a2
  27.6 3.4 %collective-permute-done.5.a3 = f32[8,8,64]{2,1,0:T(8,128)S(1)} collective-permute-done((f32[8,8,64]{2,1,0:T(8,128)S(1)}, f32[8,8,64]{2,1,0:T(8,128)S(1)}, u32[]{:S(2)}, u32[]{:S(2)}) %collective-permute-start.5) | collective-permute-done | bytes 16416 | tf_op jit(solution)/shard_map/ppermute | solution.py:52
  31.0 0.6 shard_map.104
  31.6 1.1 %collective-permute-start.9 = (f32[4,8,64]{2,1,0:T(8,128)S(1)}, f32[4,8,64]{2,1,0:T(8,128)S(1)}, u32[]{:S(2)}, u32[]{:S(2)}) collective-permute-start(f32[4,8,64]{2,1,0:T(8,128)S(1)} %get-tuple-element.35), channel_id=1, source_target_pairs={{0,4},{1,5},{2,6},{3,7},{4,0},{5,1},{6,2},{7,3},{8,12},{9,13},{10,... | collective-permute-start | bytes 24584 | tf_op jit(solution)/shard_map/ppermute | solution.py:52
  32.7 6.8 %shard_map.105 = (bf16[64,512,256]{2,1,0:T(8,128)(2,1)S(1)}, f32[8,128]{1,0:T(8,128)S(1)}) custom-call(f32[64,256,256]{2,1,0:T(8,128)} %bitcast.16, f32[4,8,64]{2,1,0:T(8,128)S(1)} %get-tuple-element.32.after.keep), custom_call_target="tpu_custom_call" | custom-call | flops 1 | bytes 1 | tf_op jit(solution)/shard_map/pallas_call | solution.py:381
  39.5 2.2 %shard_map.103 = (s32[64,128]{1,0:T(8,128)S(1)}, f32[8,64]{1,0:T(8,128)S(1)}, s32[8,64]{1,0:T(8,128)S(1)}) custom-call(s32[4]{0:T(128)S(1)} %pad_add_fusion.place, s32[1024]{0:T(1024)} %vir.1, s32[150]{0:T(256)} %occ.1, s32[8,8,8]{2,1,0:T(8,128)} %allowed.1, s32[2,32]{1,0:T(2,128)} %bitcast.19, f32[150]{0:T(256)} %occ_e.1, f32[1024]{0:T(1024)} %vir_e.1, ...), custom_call_target="tpu_custom_call" | custom-call | flops 1 | bytes 1 | tf_op jit(solution)/shard_map/pallas_call | solution.py:322
  41.7 1.1 %collective-permute-done.9.rest_1_.got = f32[4,8,64]{2,1,0:T(8,128)S(1)} collective-permute-done((f32[4,8,64]{2,1,0:T(8,128)S(1)}, f32[4,8,64]{2,1,0:T(8,128)S(1)}, u32[]{:S(2)}, u32[]{:S(2)}) %collective-permute-start.9) | collective-permute-done | bytes 8224 | tf_op jit(solution)/shard_map/ppermute | solution.py:52
  42.9 0.0 collective-permute-done.8.p3
  42.9 0.8 %collective-permute-done.7.p2 = f32[64,4,8,128]{3,2,1,0:T(8,128)S(1)} collective-permute-done((f32[64,4,8,128]{3,2,1,0:T(8,128)S(1)}, f32[64,4,8,128]{3,2,1,0:T(8,128)S(1)}, u32[]{:S(2)}, u32[]{:S(2)}) %collective-permute-start.7) | collective-permute-done | bytes 1048608 | tf_op jit(solution)/shard_map/ppermute | solution.py:52
  43.7 0.0 collective-permute-done.6.p1
  43.7 1.1 %shard_map.106 = (f32[32,16,8,128]{3,2,1,0:T(8,128)S(1)}, f32[32,16,8,128]{3,2,1,0:T(8,128)S(1)}) custom-call(s32[4]{0:T(128)S(1)} %pad_add_fusion.place, f32[64,4,8,128]{3,2,1,0:T(8,128)S(1)} %shard_map.102.after.p0, f32[64,4,8,128]{3,2,1,0:T(8,128)S(1)} %collective-permute-done.6.p1, f32[64,4,8,128]{3,2,1,0:T(8,128)S(1)} %collective-permute-done.7.p2, ...), custom_call_target="tpu_custom_call" | custom-call | flops 1 | bytes 1 | tf_op jit(solution)/shard_map/pallas_call | solution.py:149
  44.8 0.1 collective-permute-start.11
  44.9 0.5 collective-permute-start.10
  45.4 0.6 shard_map.107
  46.0 0.7 %collective-permute-start.15 = (f32[8,64]{1,0:T(8,128)S(1)}, f32[8,64]{1,0:T(8,128)S(1)}, u32[]{:S(2)}, u32[]{:S(2)}) collective-permute-start(f32[8,64]{1,0:T(8,128)S(1)} %get-tuple-element.43), channel_id=1, source_target_pairs={{0,8},{1,9},{2,10},{3,11},{4,12},{5,13},{6,14},{7,15},{8,16},{9,17... | collective-permute-start | bytes 6152 | tf_op jit(solution)/shard_map/ppermute | solution.py:52
  46.6 2.6 %collective-permute-start.16 = (f32[8,64]{1,0:T(8,128)S(1)}, f32[8,64]{1,0:T(8,128)S(1)}, u32[]{:S(2)}, u32[]{:S(2)}) collective-permute-start(f32[8,64]{1,0:T(8,128)S(1)} %get-tuple-element.44), channel_id=1, source_target_pairs={{0,24},{1,25},{2,26},{3,27},{4,28},{5,29},{6,30},{7,31},{8,0},{9,1... | collective-permute-start | bytes 6152 | tf_op jit(solution)/shard_map/ppermute | solution.py:52
  49.3 0.6 collective-permute-start.17
  49.9 3.4 %shard_map.108.before = f32[32,64]{1,0:T(8,128)S(1)} custom-call(s32[4]{0:T(128)S(1)} %pad_add_fusion.place, s32[64,128]{1,0:T(8,128)S(1)} %get-tuple-element.28.rest_2_.bound.before, bf16[64,512,256]{2,1,0:T(8,128)(2,1)S(1)} %get-tuple-element.33.slab, f32[32,16,8,128]{3,2,1,0:T(8,128)S(1)} %get-tuple-element.37.after.mine, ...), custom_call_target="tpu_custom_call" | custom-call | flops 1 | bytes 1 | tf_op jit(solution)/shard_map/pallas_call | solution.py:455
  53.3 0.0 collective-permute-done.10.other
  53.3 3.5 %shard_map.109 = (f32[8,64]{1,0:T(8,128)S(1)}, f32[8,64]{1,0:T(8,128)S(1)}, f32[8,64]{1,0:T(8,128)S(1)}, f32[8,64]{1,0:T(8,128)S(1)}) custom-call(s32[4]{0:T(128)S(1)} %pad_add_fusion.place, s32[64,128]{1,0:T(8,128)S(1)} %get-tuple-element.28.rest_2_.bound.before, bf16[64,512,256]{2,1,0:T(8,128)(2,1)S(1)} %get-tuple-element.33.slab, ...), custom_call_target="tpu_custom_call" | custom-call | flops 1 | bytes 1 | tf_op jit(solution)/shard_map/pallas_call | solution.py:455
  56.8 1.6 %collective-permute-start.12 = (f32[8,64]{1,0:T(8,128)S(1)}, f32[8,64]{1,0:T(8,128)S(1)}, u32[]{:S(2)}, u32[]{:S(2)}) collective-permute-start(f32[8,64]{1,0:T(8,128)S(1)} %get-tuple-element.40), channel_id=1, source_target_pairs={{0,32},{1,33},{2,34},{3,35},{4,36},{5,37},{6,38},{7,39},{8,40},{9,... | collective-permute-start | bytes 6152 | tf_op jit(solution)/shard_map/ppermute | solution.py:52
  58.4 1.7 %collective-permute-start.13 = (f32[8,64]{1,0:T(8,128)S(1)}, f32[8,64]{1,0:T(8,128)S(1)}, u32[]{:S(2)}, u32[]{:S(2)}) collective-permute-start(f32[8,64]{1,0:T(8,128)S(1)} %get-tuple-element.41), channel_id=1, source_target_pairs={{0,96},{1,97},{2,98},{3,99},{4,100},{5,101},{6,102},{7,103},{8,104... | collective-permute-start | bytes 6152 | tf_op jit(solution)/shard_map/ppermute | solution.py:52
  60.1 0.0 collective-permute-done.15
  60.1 2.0 %collective-permute-start.14 = (f32[8,64]{1,0:T(8,128)S(1)}, f32[8,64]{1,0:T(8,128)S(1)}, u32[]{:S(2)}, u32[]{:S(2)}) collective-permute-start(f32[8,64]{1,0:T(8,128)S(1)} %get-tuple-element.42), channel_id=1, source_target_pairs={{0,64},{1,65},{2,66},{3,67},{4,68},{5,69},{6,70},{7,71},{8,72},{9,... | collective-permute-start | bytes 6152 | tf_op jit(solution)/shard_map/ppermute | solution.py:52
  62.1 0.0 collective-permute-done.16
  62.1 0.0 collective-permute-done.13
  62.1 3.1 %collective-permute-done.14 = f32[8,64]{1,0:T(8,128)S(1)} collective-permute-done((f32[8,64]{1,0:T(8,128)S(1)}, f32[8,64]{1,0:T(8,128)S(1)}, u32[]{:S(2)}, u32[]{:S(2)}) %collective-permute-start.14) | collective-permute-done | bytes 2080 | tf_op jit(solution)/shard_map/ppermute | solution.py:52
  65.2 0.6 select_bitcast_fusion
  (5 shorter events, 0.0 us)
Async XLA Ops:
  0.0 0.9 %copy-start = (f32[32,256,8]{1,2,0:T(8,128)S(1)}, f32[32,256,8]{1,2,0:T(8,128)}, u32[]{:S(2)}) copy-start(f32[32,256,8]{1,2,0:T(8,128)} %param.16) | copy-start | bytes 786436
  1.5 12.2 %collective-permute-start.2 = (f32[64,8,128]{2,1,0:T(8,128)S(1)}, f32[64,8,128]{2,1,0:T(8,128)S(1)}, u32[]{:S(2)}, u32[]{:S(2)}) collective-permute-start(f32[64,8,128]{2,1,0:T(8,128)S(1)} %shard_map.100.b0), channel_id=1, source_target_pairs={{0,16},{1,5},{2,18},{3,7},{4,20},{5,1},{6,22},{7,3},{8,24},{9,13},... | collective-permute-start | bytes 786440 | tf_op jit(solution)/shard_map/ppermute | solution.py:52
  4.7 9.0 %collective-permute-start.1 = (f32[64,8,128]{2,1,0:T(8,128)S(1)}, f32[64,8,128]{2,1,0:T(8,128)S(1)}, u32[]{:S(2)}, u32[]{:S(2)}) collective-permute-start(f32[64,8,128]{2,1,0:T(8,128)S(1)} %shard_map.100.b0), channel_id=1, source_target_pairs={{0,24},{1,7},{2,26},{3,1},{4,28},{5,3},{6,30},{7,5},{8,0},{9,15},{... | collective-permute-start | bytes 786440 | tf_op jit(solution)/shard_map/ppermute | solution.py:52
  5.9 7.9 %collective-permute-start = (f32[64,8,128]{2,1,0:T(8,128)S(1)}, f32[64,8,128]{2,1,0:T(8,128)S(1)}, u32[]{:S(2)}, u32[]{:S(2)}) collective-permute-start(f32[64,8,128]{2,1,0:T(8,128)S(1)} %shard_map.100.b0), channel_id=1, source_target_pairs={{0,8},{1,3},{2,10},{3,5},{4,12},{5,7},{6,14},{7,1},{8,16},{9,11},{... | collective-permute-start | bytes 786440 | tf_op jit(solution)/shard_map/ppermute | solution.py:52
  14.5 28.4 %collective-permute-start.8 = (f32[64,4,8,128]{3,2,1,0:T(8,128)S(1)}, f32[64,4,8,128]{3,2,1,0:T(8,128)S(1)}, u32[]{:S(2)}, u32[]{:S(2)}) collective-permute-start(f32[64,4,8,128]{3,2,1,0:T(8,128)S(1)} %shard_map.102.after.p0), channel_id=1, source_target_pairs={{0,4},{1,17},{2,6},{3,19},{4,0},{5,21},{6,2},{7,23},{8,12},{9,25},... | collective-permute-start | bytes 3145736 | tf_op jit(solution)/shard_map/ppermute | solution.py:52
  18.4 25.2 %collective-permute-start.7 = (f32[64,4,8,128]{3,2,1,0:T(8,128)S(1)}, f32[64,4,8,128]{3,2,1,0:T(8,128)S(1)}, u32[]{:S(2)}, u32[]{:S(2)}) collective-permute-start(f32[64,4,8,128]{3,2,1,0:T(8,128)S(1)} %shard_map.102.after.p0), channel_id=1, source_target_pairs={{0,6},{1,25},{2,0},{3,27},{4,2},{5,29},{6,4},{7,31},{8,14},{9,1},{... | collective-permute-start | bytes 3145736 | tf_op jit(solution)/shard_map/ppermute | solution.py:52
  19.2 24.5 %collective-permute-start.6 = (f32[64,4,8,128]{3,2,1,0:T(8,128)S(1)}, f32[64,4,8,128]{3,2,1,0:T(8,128)S(1)}, u32[]{:S(2)}, u32[]{:S(2)}) collective-permute-start(f32[64,4,8,128]{3,2,1,0:T(8,128)S(1)} %shard_map.102.after.p0), channel_id=1, source_target_pairs={{0,2},{1,9},{2,4},{3,11},{4,6},{5,13},{6,0},{7,15},{8,10},{9,17},{... | collective-permute-start | bytes 3145736 | tf_op jit(solution)/shard_map/ppermute | solution.py:52
  20.5 5.1 %collective-permute-start.3 = (f32[8,8,64]{2,1,0:T(8,128)S(1)}, f32[8,8,64]{2,1,0:T(8,128)S(1)}, u32[]{:S(2)}, u32[]{:S(2)}) collective-permute-start(f32[8,8,64]{2,1,0:T(8,128)S(1)} %get-tuple-element.29), channel_id=1, source_target_pairs={{0,32},{1,33},{2,34},{3,35},{4,36},{5,37},{6,38},{7,39},{8,40},{9,... | collective-permute-start | bytes 49160 | tf_op jit(solution)/shard_map/ppermute | solution.py:52
  22.1 5.5 %collective-permute-start.4 = (f32[8,8,64]{2,1,0:T(8,128)S(1)}, f32[8,8,64]{2,1,0:T(8,128)S(1)}, u32[]{:S(2)}, u32[]{:S(2)}) collective-permute-start(f32[8,8,64]{2,1,0:T(8,128)S(1)} %get-tuple-element.30), channel_id=1, source_target_pairs={{0,96},{1,97},{2,98},{3,99},{4,100},{5,101},{6,102},{7,103},{8,104... | collective-permute-start | bytes 49160 | tf_op jit(solution)/shard_map/ppermute | solution.py:52
  25.6 5.4 %collective-permute-start.5 = (f32[8,8,64]{2,1,0:T(8,128)S(1)}, f32[8,8,64]{2,1,0:T(8,128)S(1)}, u32[]{:S(2)}, u32[]{:S(2)}) collective-permute-start(f32[8,8,64]{2,1,0:T(8,128)S(1)} %get-tuple-element.31), channel_id=1, source_target_pairs={{0,64},{1,65},{2,66},{3,67},{4,68},{5,69},{6,70},{7,71},{8,72},{9,... | collective-permute-start | bytes 49160 | tf_op jit(solution)/shard_map/ppermute | solution.py:52
  31.6 11.3 %collective-permute-start.9 = (f32[4,8,64]{2,1,0:T(8,128)S(1)}, f32[4,8,64]{2,1,0:T(8,128)S(1)}, u32[]{:S(2)}, u32[]{:S(2)}) collective-permute-start(f32[4,8,64]{2,1,0:T(8,128)S(1)} %get-tuple-element.35), channel_id=1, source_target_pairs={{0,4},{1,5},{2,6},{3,7},{4,0},{5,1},{6,2},{7,3},{8,12},{9,13},{10,... | collective-permute-start | bytes 24584 | tf_op jit(solution)/shard_map/ppermute | solution.py:52
  44.8 5.0 %collective-permute-start.11 = (f32[32,16,8,128]{3,2,1,0:T(8,128)S(1)}, f32[32,16,8,128]{3,2,1,0:T(8,128)S(1)}, u32[]{:S(2)}, u32[]{:S(2)}) collective-permute-start(f32[32,16,8,128]{3,2,1,0:T(8,128)S(1)} %get-tuple-element.37.after.mine), channel_id=1, source_target_pairs={{0,1},{1,0},{2,3},{3,2},{4,5},{5,4},{6,7},{7,6},{8,9},{9,8},{10,11... | collective-permute-start | bytes 6291464 | tf_op jit(solution)/shard_map/ppermute | solution.py:52
  44.9 8.4 %collective-permute-start.10 = (f32[32,16,8,128]{3,2,1,0:T(8,128)S(1)}, f32[32,16,8,128]{3,2,1,0:T(8,128)S(1)}, u32[]{:S(2)}, u32[]{:S(2)}) collective-permute-start(f32[32,16,8,128]{3,2,1,0:T(8,128)S(1)} %get-tuple-element.36.mine), channel_id=1, source_target_pairs={{0,1},{1,0},{2,3},{3,2},{4,5},{5,4},{6,7},{7,6},{8,9},{9,8},{10,11... | collective-permute-start | bytes 6291464 | tf_op jit(solution)/shard_map/ppermute | solution.py:52
  46.0 14.1 %collective-permute-start.15 = (f32[8,64]{1,0:T(8,128)S(1)}, f32[8,64]{1,0:T(8,128)S(1)}, u32[]{:S(2)}, u32[]{:S(2)}) collective-permute-start(f32[8,64]{1,0:T(8,128)S(1)} %get-tuple-element.43), channel_id=1, source_target_pairs={{0,8},{1,9},{2,10},{3,11},{4,12},{5,13},{6,14},{7,15},{8,16},{9,17... | collective-permute-start | bytes 6152 | tf_op jit(solution)/shard_map/ppermute | solution.py:52
  46.6 15.4 %collective-permute-start.16 = (f32[8,64]{1,0:T(8,128)S(1)}, f32[8,64]{1,0:T(8,128)S(1)}, u32[]{:S(2)}, u32[]{:S(2)}) collective-permute-start(f32[8,64]{1,0:T(8,128)S(1)} %get-tuple-element.44), channel_id=1, source_target_pairs={{0,24},{1,25},{2,26},{3,27},{4,28},{5,29},{6,30},{7,31},{8,0},{9,1... | collective-permute-start | bytes 6152 | tf_op jit(solution)/shard_map/ppermute | solution.py:52
  49.3 12.8 %collective-permute-start.17 = (f32[8,64]{1,0:T(8,128)S(1)}, f32[8,64]{1,0:T(8,128)S(1)}, u32[]{:S(2)}, u32[]{:S(2)}) collective-permute-start(f32[8,64]{1,0:T(8,128)S(1)} %get-tuple-element.45), channel_id=1, source_target_pairs={{0,16},{1,17},{2,18},{3,19},{4,20},{5,21},{6,22},{7,23},{8,24},{9,... | collective-permute-start | bytes 6152 | tf_op jit(solution)/shard_map/ppermute | solution.py:52
  56.8 5.3 %collective-permute-start.12 = (f32[8,64]{1,0:T(8,128)S(1)}, f32[8,64]{1,0:T(8,128)S(1)}, u32[]{:S(2)}, u32[]{:S(2)}) collective-permute-start(f32[8,64]{1,0:T(8,128)S(1)} %get-tuple-element.40), channel_id=1, source_target_pairs={{0,32},{1,33},{2,34},{3,35},{4,36},{5,37},{6,38},{7,39},{8,40},{9,... | collective-permute-start | bytes 6152 | tf_op jit(solution)/shard_map/ppermute | solution.py:52
  58.4 3.7 %collective-permute-start.13 = (f32[8,64]{1,0:T(8,128)S(1)}, f32[8,64]{1,0:T(8,128)S(1)}, u32[]{:S(2)}, u32[]{:S(2)}) collective-permute-start(f32[8,64]{1,0:T(8,128)S(1)} %get-tuple-element.41), channel_id=1, source_target_pairs={{0,96},{1,97},{2,98},{3,99},{4,100},{5,101},{6,102},{7,103},{8,104... | collective-permute-start | bytes 6152 | tf_op jit(solution)/shard_map/ppermute | solution.py:52
  60.1 5.1 %collective-permute-start.14 = (f32[8,64]{1,0:T(8,128)S(1)}, f32[8,64]{1,0:T(8,128)S(1)}, u32[]{:S(2)}, u32[]{:S(2)}) collective-permute-start(f32[8,64]{1,0:T(8,128)S(1)} %get-tuple-element.42), channel_id=1, source_target_pairs={{0,64},{1,65},{2,66},{3,67},{4,68},{5,69},{6,70},{7,71},{8,72},{9,... | collective-permute-start | bytes 6152 | tf_op jit(solution)/shard_map/ppermute | solution.py:52

commit v4 on v3

--- a/solution.py
+++ b/solution.py
@@ -107,53 +107,51 @@
         scratch_shapes=[pltpu.VMEM((slots, cells, pairs), F32)],
         compiler_params=grant(8),
         cost_estimate=small_cost(),
-    )(amp)
-
-
-def stack_body(place, b0, b1, b2, b3, after, out):
+    )(in_hbm(amp))
+
+
+CHUNKS = (32, 32)
+
+
+def stack_body(place, b0, b1, b2, b3, after, *out):
     own = jnp.where(place[3] == 0, place[1], place[2])
-    for source, shift in ((b0, 0), (b1, 3), (b2, 1), (b3, 2)):
-        out[:, pl.ds(lax.rem(own + shift, 4), 1)] = source[...][:, None]
+    base = 0
+    for q in out:
+        count = q.shape[0]
+        for source, shift in ((b0, 0), (b1, 3), (b2, 1), (b3, 2)):
+            q[:, pl.ds(lax.rem(own + shift, 4), 1)] = source[base : base + count][:, None]
+        base += count
 
 
 def stack(place, blocks, after):
-    groups, slots, lanes = blocks[0].shape
+    _, slots, lanes = blocks[0].shape
     return pl.pallas_call(
         stack_body,
-        out_shape=jax.ShapeDtypeStruct((groups, 4, slots, lanes), F32),
+        out_shape=tuple(jax.ShapeDtypeStruct((n, 4, slots, lanes), F32) for n in CHUNKS),
         in_specs=[smem()] + [vmem()] * 4 + [anywhere()],
-        out_specs=vmem(),
+        out_specs=(vmem(),) * len(CHUNKS),
         compiler_params=grant(8),
         cost_estimate=small_cost(),
     )(place, *blocks, after)
 
 
-CHUNKS = (32, 32)
-
-
-def pack_body(place, p0, p1, p2, p3, *rest):
-    out = rest[-len(CHUNKS) :]
-    x, z, core = place[1], place[2], place[3]
-    base = 0
-    for o in out:
-        count = o.shape[0]
-        for piece, shift in ((p0, 0), (p1, 3), (p2, 1), (p3, 2)):
-            first = jnp.where(core == 0, lax.rem(z + shift, 4), lax.rem(x + shift, 4) * 4)
-            for i in range(4):
-                o[:, pl.ds(first + i * jnp.where(core == 0, 4, 1), 1)] = piece[base : base + count, i : i + 1]
-        base += count
-
-
-def pack(place, pieces, after):
-    _, _, slots, lanes = pieces[0].shape
+def pack_body(*refs):
+    out = refs[-len(CHUNKS) :]
+    for n, o in enumerate(out):
+        for i in range(4):
+            o[:, 4 * i : 4 * i + 4] = refs[4 * n + i][...]
+
+
+def pack(held, after):
+    _, _, slots, lanes = held[0][0].shape
     return pl.pallas_call(
         pack_body,
         out_shape=tuple(jax.ShapeDtypeStruct((n, 16, slots, lanes), F32) for n in CHUNKS),
-        in_specs=[smem()] + [vmem()] * 4 + [anywhere()] * len(after),
+        in_specs=[vmem()] * 4 * len(held) + [anywhere()] * len(after),
         out_specs=(vmem(),) * len(CHUNKS),
-        compiler_params=grant(12),
-        cost_estimate=small_cost(),
-    )(place, *pieces, *after)
+        compiler_params=grant(16),
+        cost_estimate=small_cost(),
+    )(*(p for pieces in held for p in pieces), *after)
 
 
 def dot_nt(a, b):
@@ -168,7 +166,7 @@
 DEPTH_BLOCK = 1280
 
 
-def cycle_body(depth, place, amp_ref, int_ref, choice_ref, o0, o1, o2, o3, acc, by_row):
+def cycle_body(depth, place, amp_ref, int_ref, choice_ref, keep, away, acc, by_row):
     step = pl.program_id(0)
     window, width, block = int_ref.shape
     pairs, rows, _ = amp_ref.shape
@@ -192,29 +190,28 @@
         for j in range(window):
             total = total + choice_ref[:, j : j + 1] * acc[:, j * width : (j + 1) * width]
         by_row[...] = total
-        own = pairs // 4
-        for out, shift in ((o0, 0), (o1, 1), (o2, 3), (o3, 2)):
-            at = lax.rem(place[0] + shift, 4) * own * rows
-            for a in range(rows):
-                out[a] = by_row[pl.ds(at + a, own, stride=rows), :]
+        half = lax.div(place[2], 2)
+        for x in range(rows // 2):
+            keep[x] = by_row[pl.ds(2 * x + half, pairs, stride=rows), :]
+            away[x] = by_row[pl.ds(2 * x + 1 - half, pairs, stride=rows), :]
 
 
 def cycle(place, amp, ints, choice):
     pairs, rows, depth = amp.shape
     window, width, _ = ints.shape
-    part = jax.ShapeDtypeStruct((rows, pairs // 4, width), F32)
+    part = jax.ShapeDtypeStruct((rows // 2, pairs, width), F32)
     whole = pl.BlockSpec(part.shape, lambda i: (0, 0, 0))
     return pl.pallas_call(
         functools.partial(cycle_body, depth),
         grid=(pl.cdiv(depth, DEPTH_BLOCK),),
-        out_shape=(part,) * 4,
+        out_shape=(part,) * 2,
         in_specs=[
             smem(),
             pl.BlockSpec((pairs, rows, DEPTH_BLOCK), lambda i: (0, 0, i)),
             pl.BlockSpec((window, width, DEPTH_BLOCK), lambda i: (0, 0, i)),
             pl.BlockSpec((pairs * rows, window), lambda i: (0, 0)),
         ],
-        out_specs=(whole,) * 4,
+        out_specs=(whole,) * 2,
         scratch_shapes=[
             pltpu.VMEM((pairs * rows, window * width), F32),
             pltpu.VMEM((pairs * rows, width), F32),
@@ -222,27 +219,6 @@
         compiler_params=grant(24),
         cost_estimate=small_cost(),
     )(place, in_hbm(amp), in_hbm(ints), choice)
-
-
-def by_half_body(place, a0, a1, a2, a3, after, keep, away, held):
-    held[...] = a0[...] + a1[...] + a2[...] + a3[...]
-    half = lax.div(place[2], 2)
-    for x in range(4):
-        keep[pl.ds(x, 1)] = held[pl.ds(2 * x + half, 1)]
-        away[pl.ds(x, 1)] = held[pl.ds(2 * x + 1 - half, 1)]
-
-
-def by_half(place, parts, after):
-    count, own, width = parts[0].shape
-    return pl.pallas_call(
-        by_half_body,
-        out_shape=(jax.ShapeDtypeStruct((count // 2, own, width), F32),) * 2,
-        in_specs=[smem()] + [vmem()] * 4 + [anywhere()],
-        out_specs=(vmem(),) * 2,
-        scratch_shapes=[pltpu.VMEM((count, own, width), F32)],
-        compiler_params=grant(8),
-        cost_estimate=small_cost(),
-    )(place, *parts, after)
 
 
 def by_row_body(place, keep, got, after, o0, o1, o2, o3, held):
@@ -264,7 +240,7 @@
     )(place, keep, got, after)
 
 
-def labels_body(place, vir, occ, allowed, pair_list, occ_e, vir_e, vir_tile, after, bound, denom, live):
+def labels(place, vir, occ, allowed, pair_list, occ_e, vir_e, vir_tile, bound, denom, live):
     y, x, z, core = place[0], place[1], place[2], place[3]
     row = x * 2 + lax.div(z, 2)
     column = lax.rem(z, 2) * 2 + core
@@ -317,29 +293,14 @@
     live[...] = (slot < count_b).astype(jnp.int32)
 
 
-def labels(place, vir, occ, allowed, pair_list, occ_e, vir_e, width, own, pairs, after):
-    total = vir.shape[0]
-    return pl.pallas_call(
-        labels_body,
-        out_shape=(
-            jax.ShapeDtypeStruct((total // 4 // CELLS, CELLS * pairs), jnp.int32),
-            jax.ShapeDtypeStruct((own, width), F32),
-            jax.ShapeDtypeStruct((own, width), jnp.int32),
-        ),
-        in_specs=[smem()] * 7 + [vmem(), anywhere()],
-        out_specs=(vmem(),) * 3,
-        compiler_params=grant(8),
-        cost_estimate=small_cost(),
-    )(place, *(in_hbm(v) for v in (vir, occ, allowed, pair_list.T, occ_e, vir_e)), vir.reshape(8, total // 8), after)
-
-
 READY = 4
 SLOTS = 3
 PARTS = 4
 
 
-def ready_body(slab, after, out, token, held, sems):
-    token[...] = jnp.zeros_like(token)
+def ready_body(*refs):
+    slab = refs[8]
+    out, bound, denom, live, held, sems = refs[-6:]
     width, cells, slots = slab.shape
     steps = cells // (8 * READY)
     share = width // PARTS
@@ -357,6 +318,7 @@
     for s in range(SLOTS - 1):
         for c in copies(s):
             c.start()
+    labels(*refs[:8], bound, denom, live)
     for s in range(steps):
         if s + SLOTS - 1 < steps:
             for c in copies(s + SLOTS - 1):
@@ -376,23 +338,25 @@
                 out[at, pl.ds(width * CELLS, width * CELLS)] = low
 
 
-def ready(slab, after):
+def ready(place, tables, vir_tile, slab, own, pairs, after):
     width, cells, slots = slab.shape
     return pl.pallas_call(
         ready_body,
         out_shape=(
             jax.ShapeDtypeStruct((cells // CELLS, 2 * CELLS * width, slots), BF16),
-            jax.ShapeDtypeStruct((8, 128), F32),
+            jax.ShapeDtypeStruct((cells // CELLS, CELLS * pairs), jnp.int32),
+            jax.ShapeDtypeStruct((own, width), F32),
+            jax.ShapeDtypeStruct((own, width), jnp.int32),
         ),
-        in_specs=[anywhere(), anywhere()],
-        out_specs=(vmem(), vmem()),
+        in_specs=[smem()] * 7 + [vmem()] + [anywhere()] * (1 + len(after)),
+        out_specs=(vmem(),) * 4,
         scratch_shapes=[
             pltpu.VMEM((SLOTS, width, READY * 8, slots), F32),
             pltpu.SemaphoreType.DMA((SLOTS, PARTS)),
         ],
         compiler_params=grant(28),
         cost_estimate=small_cost(),
-    )(slab, after)
+    )(place, *(in_hbm(v) for v in tables), vir_tile, in_hbm(slab), *after)
 
 
 STEP = 8
@@ -400,6 +364,7 @@
 
 def ladder_body(last, base, place, bound, slab, mine, other, before, after, *rest):
     if last:
+        parts, rest = rest[:4], rest[4:]
         o0, o1, o2, o3, amps, acc, folded, final = rest
     else:
         out, amps, acc, folded, final = rest
@@ -408,12 +373,19 @@
     lanes = bound.shape[1]
     width = rows // (2 * CELLS)
     pairs = lanes // CELLS
+    x, z = place[1], place[2]
+    tiles = []
+    for source, at_first in ((mine, core == 0), (other, core == 1)):
+        for n, shift in enumerate((0, 3, 1, 2)):
+            first = jnp.where(at_first, lax.rem(z + shift, 4) * 2, lax.rem(x + shift, 4) * 8 + 1)
+            for i in range(4):
+                tiles.append((source, 4 * n + i, first + i * jnp.where(at_first, 8, 2)))
     t_of = lax.broadcasted_iota(jnp.int32, (slots, lanes), 0)
     for s in range(mine.shape[0] // STEP):
         left, right = [], []
         for g in range(STEP):
-            amps[g, :, pl.ds(core, 1)] = mine[s * STEP + g][:, None]
-            amps[g, :, pl.ds(1 - core, 1)] = other[s * STEP + g][:, None]
+            for source, n, tile in tiles:
+                amps[g, tile] = source[s * STEP + g, n]
             at = base + s * STEP + g
             edge = bound[at : at + 1, :]
             high, low = split(jnp.where(t_of < edge, amps[g].reshape(slots, lanes), 0.0))
@@ -435,13 +407,14 @@
         return
     if base:
         total = total + before[...]
-    final[...] = total
+    final[...] = total + (parts[0][...] + parts[1][...]) + (parts[2][...] + parts[3][...])
     own = pairs // 4
     for o, shift in ((o0, 0), (o1, 1), (o2, 3), (o3, 2)):
         o[...] = final[pl.ds(pl.multiple_of(lax.rem(y + shift, 4) * own, 8), own), :]
 
 
-def ladder(place, bound, slab, mine, other, base, before, after, last):
+def ladder(place, bound, slab, mine, other, base, before, after, parts=()):
+    last = bool(parts)
     _, rows, slots = slab.shape
     lanes = bound.shape[1]
     pairs = lanes // CELLS
@@ -455,17 +428,17 @@
     return pl.pallas_call(
         functools.partial(ladder_body, last, base),
         out_shape=out_shape,
-        in_specs=[smem()] + [vmem()] * 5 + [anywhere()],
+        in_specs=[smem()] + [vmem()] * 5 + [anywhere()] + [vmem()] * len(parts),
         out_specs=out_specs,
         scratch_shapes=[
-            pltpu.VMEM((STEP, slots // 16, 2, 8, lanes), F32),
+            pltpu.VMEM((STEP, slots // 8, 8, lanes), F32),
             pltpu.VMEM((rows, 2 * lanes), F32),
             pltpu.VMEM((rows // 2, lanes), F32),
             pltpu.VMEM((pairs, width), F32),
         ],
         compiler_params=grant(12),
         cost_estimate=small_cost(),
-    )(place, bound, in_vmem(slab), mine, other, before, after)
+    )(place, bound, in_vmem(slab), mine, other, before, after, *parts)
 
 
 def on_device(vir, occ, allowed, pair_list, occ_e, vir_e, ladder_amp, int_slab, cycle_amp, cycle_int):
@@ -481,23 +454,31 @@
     blocks = [mine] + [send(mine, FIRST[n]) for n in (1, -1, 2)]
     choice = (pair_list[:, 1:] == jnp.arange(cycle_int.shape[1], dtype=jnp.int32)).astype(F32)
     choice = jnp.repeat(choice, cycle_amp.shape[1], axis=0)
-    parts = cycle(place, cycle_amp, jnp.transpose(cycle_int, (1, 2, 0)), choice)
-    line = stack(place, blocks, parts[0])
-    pieces = [line] + [send(line, SECOND[n]) for n in (1, -1, 2)]
-    bound, denom, live = labels(place, vir, occ, allowed, pair_list, occ_e, vir_e, width, own, pairs, line)
-    keep, away = by_half(place, spread(parts, ALONG_Y), line)
+    keep, away = cycle(place, cycle_amp, jnp.transpose(cycle_int, (1, 2, 0)), choice)
+    low, high = stack(place, blocks, keep)
+    low_below, high_above = send(low, SECOND[1]), send(high, SECOND[-1])
+    high_below, low_above = send(high, SECOND[1]), send(low, SECOND[-1])
     got = send(away, Z_ACROSS)
-    slab, token = ready(in_hbm(int_slab.reshape(int_slab.shape[1:])), keep)
-
-    chunks = pack(place, pieces, (token, got, bound))
+    slab, bound, denom, live = ready(
+        place,
+        (vir, occ, allowed, pair_list.T, occ_e, vir_e),
+        vir.reshape(8, -1),
+        int_slab.reshape(int_slab.shape[1:]),
+        own,
+        pairs,
+        (low_below, high_above),
+    )
+    held = [
+        (low, low_below, low_above, send(low_below, SECOND[1])),
+        (high, high_below, high_above, send(high_above, SECOND[-1])),
+    ]
+    chunks = pack(held, (bound, got))
     others = [send(v, SWAP) for v in chunks]
     parts = spread(by_row(place, keep, got, chunks[0]), ALONG_X)
-    base, sums = 0, bound
-    for i, count in enumerate(CHUNKS):
-        sums = ladder(place, bound, slab, chunks[i], others[i], base, sums, parts[0], i == len(CHUNKS) - 1)
-        base += count
+    sums = ladder(place, bound, slab, chunks[0], others[0], 0, bound, bound)
+    sums = ladder(place, bound, slab, chunks[1], others[1], CHUNKS[0], sums, bound, parts)
     s0, s1, s2, s3 = spread(sums, ALONG_Y)
-    total = (s0 + s1) + (s2 + s3) + (parts[0] + parts[1]) + (parts[2] + parts[3])
+    total = (s0 + s1) + (s2 + s3)
     return jnp.where(live > 0, total / denom, jnp.float32(0.0))[None]
 
 

time: 66.1 us -> 62.8 us (0.950)
  starting transfers between devices: 27.3 us -> 25.1 us
  Pallas kernels: 25.6 us -> 24.6 us
  local copies, waits for them, and re-layouts: 1.64 us -> 0.69 us
  waiting for transfers between devices: 10.4 us -> 11.2 us
    pallas_call x3 -> x1, Pallas kernels: 3.45 us -> 0.62 us  [stack(): pl.pallas_call(stack_body, out_shape=tuple((jax.ShapeDtypeStruct((n, 4, s...]
    ppermute x18, starting transfers between devices: 27.3 us -> 25.1 us  [send(): return lax.ppermute(value, AXES, pairs)]
    pallas_call x1, Pallas kernels: 6.77 us -> 8.2 us  [ready(): pl.pallas_call(ready_body, out_shape=(jax.ShapeDtypeStruct((cells // CELL...]
    unnamed x2 -> x0, local copies, waits for them, and re-layouts: 0.95 us -> none
    pallas_call x1, Pallas kernels: 0.59 us -> 1.54 us  [relayout(): pl.pallas_call(relayout_body, out_shape=jax.ShapeDtypeStruct((cells // CE...]
    pallas_call x1, Pallas kernels: 1.13 us -> 0.27 us  [pack(): pl.pallas_call(pack_body, out_shape=tuple((jax.ShapeDtypeStruct((n, 16, s...]
    ppermute x18, waiting for transfers between devices: 10.4 us -> 11.2 us  [send(): return lax.ppermute(value, AXES, pairs)]
  transfers between devices with their start and end apart: 18 -> 18, of which waited for: 5 -> 4; matrix products, arithmetic and copies ran while one was open for 1% -> 1% of each run, Pallas kernels for 35% -> 30%
where the time goes in v4:
time: 62.8 us; the launch traced here: 62.5 us
  starting transfers between devices  25.1 us (40%)
  Pallas kernels  24.6 us (39%)
  waiting for transfers between devices  11.2 us (18%)
  other arithmetic  0.75 us (1%)
  local copies, waits for them, and re-layouts  0.69 us (1%)
    ppermute x18, starting transfers between devices, send(): return lax.ppermute(value, AXES, pairs)  25.1 us
    ppermute x18, waiting for transfers between devices, send(): return lax.ppermute(value, AXES, pairs)  11.2 us
    pallas_call x1, Pallas kernels, ready(): pl.pallas_call(ready_body, out_shape=(jax.ShapeDtypeStruct((cells // CELL...  8.2 us
    pallas_call x2, Pallas kernels, ladder(): pl.pallas_call(functools.partial(ladder_body, last, base), out_shape=out_...  7.31 us
    pallas_call x1, Pallas kernels, cycle(): pl.pallas_call(functools.partial(cycle_body, depth), grid=(pl.cdiv(depth,...  6.15 us
    pallas_call x1, Pallas kernels, relayout(): pl.pallas_call(relayout_body, out_shape=jax.ShapeDtypeStruct((cells // CE...  1.54 us
  transfers between devices with their start and end apart: 18, of which 4 were waited for; matrix products, arithmetic and copies ran while one was open for 1% of the time, Pallas kernels for 30%

profile of v4, /device:TPU:0, one launch (start us, length us, event | category | flops | bytes accessed | tf_op | source)
XLA Modules:
  0.0 62.5 jit_solution(2819069679126743364)
XLA Ops:
  0.0 1.5 %shard_map.100.b0 = f32[64,8,128]{2,1,0:T(8,128)S(1)} custom-call(f32[32,8,256]{2,1,0:T(8,128)} %bitcast.17), custom_call_target="tpu_custom_call" | custom-call | flops 1 | bytes 1 | tf_op jit(solution)/shard_map/pallas_call | solution.py:102
  1.5 3.2 %collective-permute-start.2 = (f32[64,8,128]{2,1,0:T(8,128)S(1)}, f32[64,8,128]{2,1,0:T(8,128)S(1)}, u32[]{:S(2)}, u32[]{:S(2)}) collective-permute-start(f32[64,8,128]{2,1,0:T(8,128)S(1)} %shard_map.100.b0), channel_id=1, source_target_pairs={{0,16},{1,5},{2,18},{3,7},{4,20},{5,1},{6,22},{7,3},{8,24},{9,13},... | collective-permute-start | bytes 786440 | tf_op jit(solution)/shard_map/ppermute | solution.py:52
  4.7 1.1 %collective-permute-start.1 = (f32[64,8,128]{2,1,0:T(8,128)S(1)}, f32[64,8,128]{2,1,0:T(8,128)S(1)}, u32[]{:S(2)}, u32[]{:S(2)}) collective-permute-start(f32[64,8,128]{2,1,0:T(8,128)S(1)} %shard_map.100.b0), channel_id=1, source_target_pairs={{0,24},{1,7},{2,26},{3,1},{4,28},{5,3},{6,30},{7,5},{8,0},{9,15},{... | collective-permute-start | bytes 786440 | tf_op jit(solution)/shard_map/ppermute | solution.py:52
  5.9 0.9 %collective-permute-start = (f32[64,8,128]{2,1,0:T(8,128)S(1)}, f32[64,8,128]{2,1,0:T(8,128)S(1)}, u32[]{:S(2)}, u32[]{:S(2)}) collective-permute-start(f32[64,8,128]{2,1,0:T(8,128)S(1)} %shard_map.100.b0), channel_id=1, source_target_pairs={{0,8},{1,3},{2,10},{3,5},{4,12},{5,7},{6,14},{7,1},{8,16},{9,11},{... | collective-permute-start | bytes 786440 | tf_op jit(solution)/shard_map/ppermute | solution.py:52
  6.8 0.7 %slice_bitcast_fusion = s32[32]{0:T(128)S(1)} fusion(s32[32,2]{0,1:T(2,128)} %param.13), kind=kLoop, calls=%fused_computation.5 | loop fusion | bytes 256 | tf_op jit(solution)/shard_map/eq | solution.py:455
  7.4 0.1 fusion
  7.5 0.1 pad_add_fusion.place.refs_0_
  7.6 6.2 %shard_map.101 = (f32[4,32,64]{2,1,0:T(8,128)S(1)}, f32[4,32,64]{2,1,0:T(8,128)S(1)}) custom-call(s32[4]{0:T(128)S(1)} %pad_add_fusion.place.refs_0_, f32[32,8,4800]{2,1,0:T(8,128)} %amp_ref.1, f32[4,64,4800]{2,1,0:T(8,128)} %bitcast.16, f32[256,4]{1,0:T(8,128)S(1)} %broadcast_bitcast_fusion.choice_ref), custom_call_target="tpu_custom_call" | custom-call | flops 1 | bytes 1 | tf_op jit(solution)/shard_map/pallas_call | solution.py:204
  13.8 0.0 collective-permute-done.2.b3
  13.8 0.0 collective-permute-done.1.b2
  13.8 0.0 collective-permute-done.b1
  13.8 0.6 shard_map.102
  14.4 2.0 %collective-permute-start.3 = (f32[32,4,8,128]{3,2,1,0:T(8,128)S(1)}, f32[32,4,8,128]{3,2,1,0:T(8,128)S(1)}, u32[]{:S(2)}, u32[]{:S(2)}) collective-permute-start(f32[32,4,8,128]{3,2,1,0:T(8,128)S(1)} %get-tuple-element.24.refs_0_), channel_id=1, source_target_pairs={{0,2},{1,9},{2,4},{3,11},{4,6},{5,13},{6,0},{7,15},{8,10},{9,17},{... | collective-permute-start | bytes 1572872 | tf_op jit(solution)/shard_map/ppermute | solution.py:52
  16.4 2.2 %collective-permute-start.4 = (f32[32,4,8,128]{3,2,1,0:T(8,128)S(1)}, f32[32,4,8,128]{3,2,1,0:T(8,128)S(1)}, u32[]{:S(2)}, u32[]{:S(2)}) collective-permute-start(f32[32,4,8,128]{3,2,1,0:T(8,128)S(1)} %get-tuple-element.25.refs_4_), channel_id=1, source_target_pairs={{0,6},{1,25},{2,0},{3,27},{4,2},{5,29},{6,4},{7,31},{8,14},{9,1},{... | collective-permute-start | bytes 1572872 | tf_op jit(solution)/shard_map/ppermute | solution.py:52
  18.6 1.9 %collective-permute-start.5 = (f32[32,4,8,128]{3,2,1,0:T(8,128)S(1)}, f32[32,4,8,128]{3,2,1,0:T(8,128)S(1)}, u32[]{:S(2)}, u32[]{:S(2)}) collective-permute-start(f32[32,4,8,128]{3,2,1,0:T(8,128)S(1)} %get-tuple-element.24.refs_0_), channel_id=1, source_target_pairs={{0,6},{1,25},{2,0},{3,27},{4,2},{5,29},{6,4},{7,31},{8,14},{9,1},{... | collective-permute-start | bytes 1572872 | tf_op jit(solution)/shard_map/ppermute | solution.py:52
  20.6 0.1 collective-permute-start.7
  20.6 5.1 %collective-permute-done.3.refs_9_.refs_1_ = f32[32,4,8,128]{3,2,1,0:T(8,128)S(1)} collective-permute-done((f32[32,4,8,128]{3,2,1,0:T(8,128)S(1)}, f32[32,4,8,128]{3,2,1,0:T(8,128)S(1)}, u32[]{:S(2)}, u32[]{:S(2)}) %collective-permute-start.3) | collective-permute-done | bytes 524320 | tf_op jit(solution)/shard_map/ppermute | solution.py:52
  25.7 0.0 collective-permute-start.6
  25.7 0.0 collective-permute-done.4.refs_10_.refs_6_
  25.7 3.3 %collective-permute-start.8 = (f32[32,4,8,128]{3,2,1,0:T(8,128)S(1)}, f32[32,4,8,128]{3,2,1,0:T(8,128)S(1)}, u32[]{:S(2)}, u32[]{:S(2)}) collective-permute-start(f32[32,4,8,128]{3,2,1,0:T(8,128)S(1)} %collective-permute-done.4.refs_10_.refs_6_), channel_id=1, source_target_pairs={{0,6},{1,25},{2,0},{3,27},{4,2},{5,29},{6,4},{7,31},{8,14},{9,1},{... | collective-permute-start | bytes 1572872 | tf_op jit(solution)/shard_map/ppermute | solution.py:52
  29.0 0.6 collective-permute-start.9
  29.6 8.2 %shard_map.103 = (bf16[64,512,256]{2,1,0:T(8,128)(2,1)S(1)}, s32[64,128]{1,0:T(8,128)S(1)}, f32[8,64]{1,0:T(8,128)S(1)}, s32[8,64]{1,0:T(8,128)S(1)}) custom-call(s32[4]{0:T(128)S(1)} %pad_add_fusion.place.refs_0_, s32[1024]{0:T(1024)} %refs_1_.1, s32[150]{0:T(256)} %refs_2_.1, s32[8,8,8]{2,1,0:T(8,128)} %refs_3_.1, s32[2,32]{1,0:T(2,128)} %bitcast.19, ...), custom_call_target="tpu_custom_call" | custom-call | flops 1 | bytes 1 | tf_op jit(solution)/shard_map/pallas_call | solution.py:343
  37.8 2.0 %collective-permute-done.9.refs_9_.got = f32[4,32,64]{2,1,0:T(8,128)S(1)} collective-permute-done((f32[4,32,64]{2,1,0:T(8,128)S(1)}, f32[4,32,64]{2,1,0:T(8,128)S(1)}, u32[]{:S(2)}, u32[]{:S(2)}) %collective-permute-start.9) | collective-permute-done | bytes 32800 | tf_op jit(solution)/shard_map/ppermute | solution.py:52
  39.8 0.0 collective-permute-done.5.refs_2_
  39.8 0.0 collective-permute-done.7.refs_5_
  39.8 0.0 collective-permute-done.6.refs_3_
  39.8 0.0 collective-permute-done.8.refs_7_
  39.8 0.3 shard_map.104
  40.1 0.1 collective-permute-start.11
  40.2 0.5 collective-permute-start.10
  40.7 0.6 shard_map.106
  41.3 0.7 %collective-permute-start.12 = (f32[32,64]{1,0:T(8,128)S(1)}, f32[32,64]{1,0:T(8,128)S(1)}, u32[]{:S(2)}, u32[]{:S(2)}) collective-permute-start(f32[32,64]{1,0:T(8,128)S(1)} %get-tuple-element.33), channel_id=1, source_target_pairs={{0,8},{1,9},{2,10},{3,11},{4,12},{5,13},{6,14},{7,15},{8,16},{9,17... | collective-permute-start | bytes 24584 | tf_op jit(solution)/shard_map/ppermute | solution.py:52
  41.9 2.7 %collective-permute-start.13 = (f32[32,64]{1,0:T(8,128)S(1)}, f32[32,64]{1,0:T(8,128)S(1)}, u32[]{:S(2)}, u32[]{:S(2)}) collective-permute-start(f32[32,64]{1,0:T(8,128)S(1)} %get-tuple-element.34), channel_id=1, source_target_pairs={{0,24},{1,25},{2,26},{3,27},{4,28},{5,29},{6,30},{7,31},{8,0},{9,1... | collective-permute-start | bytes 24584 | tf_op jit(solution)/shard_map/ppermute | solution.py:52
  44.6 0.6 collective-permute-start.14
  45.1 0.0 collective-permute-done.11.other
  45.1 3.6 %shard_map.105.before = f32[32,64]{1,0:T(8,128)S(1)} custom-call(s32[4]{0:T(128)S(1)} %pad_add_fusion.place.refs_0_, s32[64,128]{1,0:T(8,128)S(1)} %get-tuple-element.27.refs_8_.bound.before.after, bf16[64,512,256]{2,1,0:T(8,128)(2,1)S(1)} %get-tuple-element.28.slab, f32[32,16,8,128]{3,2,1,0:T(8,128)S(1)} %get-tuple-element.31.mine.after, ...), custom_call_target="tpu_custom_call" | custom-call | flops 1 | bytes 1 | tf_op jit(solution)/shard_map/pallas_call | solution.py:428
  48.8 0.0 collective-permute-done.12.rest_1_
  48.8 0.0 collective-permute-done.13.rest_2_
  48.8 1.0 %collective-permute-done.14.rest_3_ = f32[32,64]{1,0:T(8,128)S(1)} collective-permute-done((f32[32,64]{1,0:T(8,128)S(1)}, f32[32,64]{1,0:T(8,128)S(1)}, u32[]{:S(2)}, u32[]{:S(2)}) %collective-permute-start.14) | collective-permute-done | bytes 8224 | tf_op jit(solution)/shard_map/ppermute | solution.py:52
  49.8 0.0 collective-permute-done.10.other
  49.8 3.7 %shard_map.107 = (f32[8,64]{1,0:T(8,128)S(1)}, f32[8,64]{1,0:T(8,128)S(1)}, f32[8,64]{1,0:T(8,128)S(1)}, f32[8,64]{1,0:T(8,128)S(1)}) custom-call(s32[4]{0:T(128)S(1)} %pad_add_fusion.place.refs_0_, s32[64,128]{1,0:T(8,128)S(1)} %get-tuple-element.27.refs_8_.bound.before.after, bf16[64,512,256]{2,1,0:T(8,128)(2,1)S(1)} %get-tuple-element.28.slab, ...), custom_call_target="tpu_custom_call" | custom-call | flops 1 | bytes 1 | tf_op jit(solution)/shard_map/pallas_call | solution.py:428
  53.5 1.6 %collective-permute-start.15 = (f32[8,64]{1,0:T(8,128)S(1)}, f32[8,64]{1,0:T(8,128)S(1)}, u32[]{:S(2)}, u32[]{:S(2)}) collective-permute-start(f32[8,64]{1,0:T(8,128)S(1)} %get-tuple-element.37), channel_id=1, source_target_pairs={{0,32},{1,33},{2,34},{3,35},{4,36},{5,37},{6,38},{7,39},{8,40},{9,... | collective-permute-start | bytes 6152 | tf_op jit(solution)/shard_map/ppermute | solution.py:52
  55.1 1.7 %collective-permute-start.16 = (f32[8,64]{1,0:T(8,128)S(1)}, f32[8,64]{1,0:T(8,128)S(1)}, u32[]{:S(2)}, u32[]{:S(2)}) collective-permute-start(f32[8,64]{1,0:T(8,128)S(1)} %get-tuple-element.38), channel_id=1, source_target_pairs={{0,96},{1,97},{2,98},{3,99},{4,100},{5,101},{6,102},{7,103},{8,104... | collective-permute-start | bytes 6152 | tf_op jit(solution)/shard_map/ppermute | solution.py:52
  56.8 2.0 %collective-permute-start.17 = (f32[8,64]{1,0:T(8,128)S(1)}, f32[8,64]{1,0:T(8,128)S(1)}, u32[]{:S(2)}, u32[]{:S(2)}) collective-permute-start(f32[8,64]{1,0:T(8,128)S(1)} %get-tuple-element.39), channel_id=1, source_target_pairs={{0,64},{1,65},{2,66},{3,67},{4,68},{5,69},{6,70},{7,71},{8,72},{9,... | collective-permute-start | bytes 6152 | tf_op jit(solution)/shard_map/ppermute | solution.py:52
  58.8 0.0 collective-permute-done.15
  58.8 0.0 collective-permute-done.16
  58.8 3.1 %collective-permute-done.17 = f32[8,64]{1,0:T(8,128)S(1)} collective-permute-done((f32[8,64]{1,0:T(8,128)S(1)}, f32[8,64]{1,0:T(8,128)S(1)}, u32[]{:S(2)}, u32[]{:S(2)}) %collective-permute-start.17) | collective-permute-done | bytes 2080 | tf_op jit(solution)/shard_map/ppermute | solution.py:52
  61.9 0.6 select_bitcast_fusion
  (1 shorter events, 0.0 us)
Async XLA Ops:
  1.5 12.2 %collective-permute-start.2 = (f32[64,8,128]{2,1,0:T(8,128)S(1)}, f32[64,8,128]{2,1,0:T(8,128)S(1)}, u32[]{:S(2)}, u32[]{:S(2)}) collective-permute-start(f32[64,8,128]{2,1,0:T(8,128)S(1)} %shard_map.100.b0), channel_id=1, source_target_pairs={{0,16},{1,5},{2,18},{3,7},{4,20},{5,1},{6,22},{7,3},{8,24},{9,13},... | collective-permute-start | bytes 786440 | tf_op jit(solution)/shard_map/ppermute | solution.py:52
  4.7 9.0 %collective-permute-start.1 = (f32[64,8,128]{2,1,0:T(8,128)S(1)}, f32[64,8,128]{2,1,0:T(8,128)S(1)}, u32[]{:S(2)}, u32[]{:S(2)}) collective-permute-start(f32[64,8,128]{2,1,0:T(8,128)S(1)} %shard_map.100.b0), channel_id=1, source_target_pairs={{0,24},{1,7},{2,26},{3,1},{4,28},{5,3},{6,30},{7,5},{8,0},{9,15},{... | collective-permute-start | bytes 786440 | tf_op jit(solution)/shard_map/ppermute | solution.py:52
  5.9 7.9 %collective-permute-start = (f32[64,8,128]{2,1,0:T(8,128)S(1)}, f32[64,8,128]{2,1,0:T(8,128)S(1)}, u32[]{:S(2)}, u32[]{:S(2)}) collective-permute-start(f32[64,8,128]{2,1,0:T(8,128)S(1)} %shard_map.100.b0), channel_id=1, source_target_pairs={{0,8},{1,3},{2,10},{3,5},{4,12},{5,7},{6,14},{7,1},{8,16},{9,11},{... | collective-permute-start | bytes 786440 | tf_op jit(solution)/shard_map/ppermute | solution.py:52
  14.4 11.3 %collective-permute-start.3 = (f32[32,4,8,128]{3,2,1,0:T(8,128)S(1)}, f32[32,4,8,128]{3,2,1,0:T(8,128)S(1)}, u32[]{:S(2)}, u32[]{:S(2)}) collective-permute-start(f32[32,4,8,128]{3,2,1,0:T(8,128)S(1)} %get-tuple-element.24.refs_0_), channel_id=1, source_target_pairs={{0,2},{1,9},{2,4},{3,11},{4,6},{5,13},{6,0},{7,15},{8,10},{9,17},{... | collective-permute-start | bytes 1572872 | tf_op jit(solution)/shard_map/ppermute | solution.py:52
  16.4 9.3 %collective-permute-start.4 = (f32[32,4,8,128]{3,2,1,0:T(8,128)S(1)}, f32[32,4,8,128]{3,2,1,0:T(8,128)S(1)}, u32[]{:S(2)}, u32[]{:S(2)}) collective-permute-start(f32[32,4,8,128]{3,2,1,0:T(8,128)S(1)} %get-tuple-element.25.refs_4_), channel_id=1, source_target_pairs={{0,6},{1,25},{2,0},{3,27},{4,2},{5,29},{6,4},{7,31},{8,14},{9,1},{... | collective-permute-start | bytes 1572872 | tf_op jit(solution)/shard_map/ppermute | solution.py:52
  18.6 21.2 %collective-permute-start.5 = (f32[32,4,8,128]{3,2,1,0:T(8,128)S(1)}, f32[32,4,8,128]{3,2,1,0:T(8,128)S(1)}, u32[]{:S(2)}, u32[]{:S(2)}) collective-permute-start(f32[32,4,8,128]{3,2,1,0:T(8,128)S(1)} %get-tuple-element.24.refs_0_), channel_id=1, source_target_pairs={{0,6},{1,25},{2,0},{3,27},{4,2},{5,29},{6,4},{7,31},{8,14},{9,1},{... | collective-permute-start | bytes 1572872 | tf_op jit(solution)/shard_map/ppermute | solution.py:52
  20.6 19.2 %collective-permute-start.7 = (f32[32,4,8,128]{3,2,1,0:T(8,128)S(1)}, f32[32,4,8,128]{3,2,1,0:T(8,128)S(1)}, u32[]{:S(2)}, u32[]{:S(2)}) collective-permute-start(f32[32,4,8,128]{3,2,1,0:T(8,128)S(1)} %get-tuple-element.25.refs_4_), channel_id=1, source_target_pairs={{0,2},{1,9},{2,4},{3,11},{4,6},{5,13},{6,0},{7,15},{8,10},{9,17},{... | collective-permute-start | bytes 1572872 | tf_op jit(solution)/shard_map/ppermute | solution.py:52
  25.7 14.1 %collective-permute-start.6 = (f32[32,4,8,128]{3,2,1,0:T(8,128)S(1)}, f32[32,4,8,128]{3,2,1,0:T(8,128)S(1)}, u32[]{:S(2)}, u32[]{:S(2)}) collective-permute-start(f32[32,4,8,128]{3,2,1,0:T(8,128)S(1)} %collective-permute-done.3.refs_9_.refs_1_), channel_id=1, source_target_pairs={{0,2},{1,9},{2,4},{3,11},{4,6},{5,13},{6,0},{7,15},{8,10},{9,17},{... | collective-permute-start | bytes 1572872 | tf_op jit(solution)/shard_map/ppermute | solution.py:52
  25.7 14.1 %collective-permute-start.8 = (f32[32,4,8,128]{3,2,1,0:T(8,128)S(1)}, f32[32,4,8,128]{3,2,1,0:T(8,128)S(1)}, u32[]{:S(2)}, u32[]{:S(2)}) collective-permute-start(f32[32,4,8,128]{3,2,1,0:T(8,128)S(1)} %collective-permute-done.4.refs_10_.refs_6_), channel_id=1, source_target_pairs={{0,6},{1,25},{2,0},{3,27},{4,2},{5,29},{6,4},{7,31},{8,14},{9,1},{... | collective-permute-start | bytes 1572872 | tf_op jit(solution)/shard_map/ppermute | solution.py:52
  29.0 10.8 %collective-permute-start.9 = (f32[4,32,64]{2,1,0:T(8,128)S(1)}, f32[4,32,64]{2,1,0:T(8,128)S(1)}, u32[]{:S(2)}, u32[]{:S(2)}) collective-permute-start(f32[4,32,64]{2,1,0:T(8,128)S(1)} %get-tuple-element.29), channel_id=1, source_target_pairs={{0,4},{1,5},{2,6},{3,7},{4,0},{5,1},{6,2},{7,3},{8,12},{9,13},{10,... | collective-permute-start | bytes 98312 | tf_op jit(solution)/shard_map/ppermute | solution.py:52
  40.1 5.0 %collective-permute-start.11 = (f32[32,16,8,128]{3,2,1,0:T(8,128)S(1)}, f32[32,16,8,128]{3,2,1,0:T(8,128)S(1)}, u32[]{:S(2)}, u32[]{:S(2)}) collective-permute-start(f32[32,16,8,128]{3,2,1,0:T(8,128)S(1)} %get-tuple-element.31.mine.after), channel_id=1, source_target_pairs={{0,1},{1,0},{2,3},{3,2},{4,5},{5,4},{6,7},{7,6},{8,9},{9,8},{10,11... | collective-permute-start | bytes 6291464 | tf_op jit(solution)/shard_map/ppermute | solution.py:52
  40.2 9.6 %collective-permute-start.10 = (f32[32,16,8,128]{3,2,1,0:T(8,128)S(1)}, f32[32,16,8,128]{3,2,1,0:T(8,128)S(1)}, u32[]{:S(2)}, u32[]{:S(2)}) collective-permute-start(f32[32,16,8,128]{3,2,1,0:T(8,128)S(1)} %get-tuple-element.30.mine), channel_id=1, source_target_pairs={{0,1},{1,0},{2,3},{3,2},{4,5},{5,4},{6,7},{7,6},{8,9},{9,8},{10,11... | collective-permute-start | bytes 6291464 | tf_op jit(solution)/shard_map/ppermute | solution.py:52
  41.3 7.5 %collective-permute-start.12 = (f32[32,64]{1,0:T(8,128)S(1)}, f32[32,64]{1,0:T(8,128)S(1)}, u32[]{:S(2)}, u32[]{:S(2)}) collective-permute-start(f32[32,64]{1,0:T(8,128)S(1)} %get-tuple-element.33), channel_id=1, source_target_pairs={{0,8},{1,9},{2,10},{3,11},{4,12},{5,13},{6,14},{7,15},{8,16},{9,17... | collective-permute-start | bytes 24584 | tf_op jit(solution)/shard_map/ppermute | solution.py:52
  41.9 6.9 %collective-permute-start.13 = (f32[32,64]{1,0:T(8,128)S(1)}, f32[32,64]{1,0:T(8,128)S(1)}, u32[]{:S(2)}, u32[]{:S(2)}) collective-permute-start(f32[32,64]{1,0:T(8,128)S(1)} %get-tuple-element.34), channel_id=1, source_target_pairs={{0,24},{1,25},{2,26},{3,27},{4,28},{5,29},{6,30},{7,31},{8,0},{9,1... | collective-permute-start | bytes 24584 | tf_op jit(solution)/shard_map/ppermute | solution.py:52
  44.6 5.2 %collective-permute-start.14 = (f32[32,64]{1,0:T(8,128)S(1)}, f32[32,64]{1,0:T(8,128)S(1)}, u32[]{:S(2)}, u32[]{:S(2)}) collective-permute-start(f32[32,64]{1,0:T(8,128)S(1)} %get-tuple-element.35), channel_id=1, source_target_pairs={{0,16},{1,17},{2,18},{3,19},{4,20},{5,21},{6,22},{7,23},{8,24},{9,... | collective-permute-start | bytes 24584 | tf_op jit(solution)/shard_map/ppermute | solution.py:52
  53.5 5.3 %collective-permute-start.15 = (f32[8,64]{1,0:T(8,128)S(1)}, f32[8,64]{1,0:T(8,128)S(1)}, u32[]{:S(2)}, u32[]{:S(2)}) collective-permute-start(f32[8,64]{1,0:T(8,128)S(1)} %get-tuple-element.37), channel_id=1, source_target_pairs={{0,32},{1,33},{2,34},{3,35},{4,36},{5,37},{6,38},{7,39},{8,40},{9,... | collective-permute-start | bytes 6152 | tf_op jit(solution)/shard_map/ppermute | solution.py:52
  55.1 3.7 %collective-permute-start.16 = (f32[8,64]{1,0:T(8,128)S(1)}, f32[8,64]{1,0:T(8,128)S(1)}, u32[]{:S(2)}, u32[]{:S(2)}) collective-permute-start(f32[8,64]{1,0:T(8,128)S(1)} %get-tuple-element.38), channel_id=1, source_target_pairs={{0,96},{1,97},{2,98},{3,99},{4,100},{5,101},{6,102},{7,103},{8,104... | collective-permute-start | bytes 6152 | tf_op jit(solution)/shard_map/ppermute | solution.py:52
  56.8 5.1 %collective-permute-start.17 = (f32[8,64]{1,0:T(8,128)S(1)}, f32[8,64]{1,0:T(8,128)S(1)}, u32[]{:S(2)}, u32[]{:S(2)}) collective-permute-start(f32[8,64]{1,0:T(8,128)S(1)} %get-tuple-element.39), channel_id=1, source_target_pairs={{0,64},{1,65},{2,66},{3,67},{4,68},{5,69},{6,70},{7,71},{8,72},{9,... | collective-permute-start | bytes 6152 | tf_op jit(solution)/shard_map/ppermute | solution.py:52

commit v5 on v4

--- a/solution.py
+++ b/solution.py
@@ -42,9 +42,7 @@
 
 FIRST = {n: pairs_of(along_x(n), along_z(n)) for n in (1, -1, 2)}
 SECOND = {n: pairs_of(along_z(n), along_x(n)) for n in (1, -1, 2)}
-ALONG_X = {n: pairs_of(along_x(n), along_x(n)) for n in (1, -1, 2)}
 ALONG_Y = {n: pairs_of(along_y(n), along_y(n)) for n in (1, -1, 2)}
-Z_ACROSS = pairs_of(along_z(2), along_z(2))
 SWAP = pairs_of(other_core, other_core)
 
 
@@ -113,33 +111,35 @@
 CHUNKS = (32, 32)
 
 
-def stack_body(place, b0, b1, b2, b3, after, *out):
+def stack_body(place, b0, b1, b2, b3, share, *out):
     own = jnp.where(place[3] == 0, place[1], place[2])
     base = 0
-    for q in out:
-        count = q.shape[0]
+    extra = share.shape[0] // len(CHUNKS)
+    for n, (q, count) in enumerate(zip(out, CHUNKS)):
         for source, shift in ((b0, 0), (b1, 3), (b2, 1), (b3, 2)):
-            q[:, pl.ds(lax.rem(own + shift, 4), 1)] = source[base : base + count][:, None]
+            q[0:count, pl.ds(lax.rem(own + shift, 4), 1)] = source[base : base + count][:, None]
+        q[count:] = share[n * extra : (n + 1) * extra]
         base += count
 
 
-def stack(place, blocks, after):
+def stack(place, blocks, share):
     _, slots, lanes = blocks[0].shape
+    sizes = [n + share.shape[0] // len(CHUNKS) for n in CHUNKS]
     return pl.pallas_call(
         stack_body,
-        out_shape=tuple(jax.ShapeDtypeStruct((n, 4, slots, lanes), F32) for n in CHUNKS),
-        in_specs=[smem()] + [vmem()] * 4 + [anywhere()],
+        out_shape=tuple(jax.ShapeDtypeStruct((n, 4, slots, lanes), F32) for n in sizes),
+        in_specs=[smem()] + [vmem()] * 5,
         out_specs=(vmem(),) * len(CHUNKS),
         compiler_params=grant(8),
         cost_estimate=small_cost(),
-    )(place, *blocks, after)
+    )(place, *blocks, share)
 
 
 def pack_body(*refs):
     out = refs[-len(CHUNKS) :]
     for n, o in enumerate(out):
         for i in range(4):
-            o[:, 4 * i : 4 * i + 4] = refs[4 * n + i][...]
+            o[:, 4 * i : 4 * i + 4] = refs[4 * n + i][0 : CHUNKS[n]]
 
 
 def pack(held, after):
@@ -163,10 +163,10 @@
     return high, (value - high.astype(F32)).astype(BF16)
 
 
-DEPTH_BLOCK = 1280
-
-
-def cycle_body(depth, place, amp_ref, int_ref, choice_ref, keep, away, acc, by_row):
+DEPTH_BLOCK = 2432
+
+
+def cycle_body(depth, place, amp_ref, int_ref, choice_ref, out, acc, by_row):
     step = pl.program_id(0)
     window, width, block = int_ref.shape
     pairs, rows, _ = amp_ref.shape
@@ -190,28 +190,27 @@
         for j in range(window):
             total = total + choice_ref[:, j : j + 1] * acc[:, j * width : (j + 1) * width]
         by_row[...] = total
-        half = lax.div(place[2], 2)
         for x in range(rows // 2):
-            keep[x] = by_row[pl.ds(2 * x + half, pairs, stride=rows), :]
-            away[x] = by_row[pl.ds(2 * x + 1 - half, pairs, stride=rows), :]
+            pair = [by_row[pl.ds(2 * x + h, pairs, stride=rows), :] for h in range(2)]
+            out[x] = jnp.concatenate(pair, axis=1).reshape(pairs // 8, 8, 2 * width)
 
 
 def cycle(place, amp, ints, choice):
     pairs, rows, depth = amp.shape
     window, width, _ = ints.shape
-    part = jax.ShapeDtypeStruct((rows // 2, pairs, width), F32)
-    whole = pl.BlockSpec(part.shape, lambda i: (0, 0, 0))
+    part = jax.ShapeDtypeStruct((rows // 2, pairs // 8, 8, 2 * width), F32)
+    whole = pl.BlockSpec(part.shape, lambda i: (0, 0, 0, 0))
     return pl.pallas_call(
         functools.partial(cycle_body, depth),
         grid=(pl.cdiv(depth, DEPTH_BLOCK),),
-        out_shape=(part,) * 2,
+        out_shape=part,
         in_specs=[
             smem(),
             pl.BlockSpec((pairs, rows, DEPTH_BLOCK), lambda i: (0, 0, i)),
             pl.BlockSpec((window, width, DEPTH_BLOCK), lambda i: (0, 0, i)),
             pl.BlockSpec((pairs * rows, window), lambda i: (0, 0)),
         ],
-        out_specs=(whole,) * 2,
+        out_specs=whole,
         scratch_shapes=[
             pltpu.VMEM((pairs * rows, window * width), F32),
             pltpu.VMEM((pairs * rows, width), F32),
@@ -221,23 +220,48 @@
     )(place, in_hbm(amp), in_hbm(ints), choice)
 
 
-def by_row_body(place, keep, got, after, o0, o1, o2, o3, held):
-    held[...] = keep[...] + got[...]
-    for out, shift in ((o0, 0), (o1, 1), (o2, 3), (o3, 2)):
-        out[...] = held[lax.rem(place[1] + shift, 4)]
-
-
-def by_row(place, keep, got, after):
-    count, own, width = keep.shape
-    return pl.pallas_call(
-        by_row_body,
-        out_shape=(jax.ShapeDtypeStruct((own, width), F32),) * 4,
-        in_specs=[smem()] + [vmem()] * 2 + [anywhere()],
+def shares_body(place, *refs):
+    o0, o1, o2, o3, far, near = refs[-6:]
+    x, half, core = place[1], lax.div(place[2], 2), place[3]
+    window, _, slots, lanes = far.shape
+    pairs, width = o0.shape
+    extra = window // len(CHUNKS)
+    for n, first in enumerate(CHUNKS):
+        own, below, above, across = refs[4 * n : 4 * n + 4]
+        part = slice(n * extra, (n + 1) * extra)
+        far[part] = own[first:] + across[first:]
+        near[part] = below[first:] + above[first:]
+
+    def side(value, which):
+        value = value.reshape(pairs, lanes)
+        return jnp.where(which == 0, value[:, :width], value[:, width:])
+
+    @pl.when(core == 0)
+    def _():
+        for out, shift in ((o0, 0), (o1, 1), (o2, 3), (o3, 2)):
+            out[...] = side(far[lax.rem(x + shift, 4)], half)
+
+    @pl.when(core == 1)
+    def _():
+        total = far[x] + near[x]
+        o0[...] = side(total, half)
+        o1[...] = jnp.zeros_like(o1)
+        o2[...] = jnp.zeros_like(o2)
+        o3[...] = side(total, 1 - half)
+
+
+def shares(place, held, pairs, width, after):
+    extra, _, slots, lanes = held[0][0].shape
+    extra = (extra - CHUNKS[0]) * len(CHUNKS)
+    return pl.pallas_call(
+        shares_body,
+        out_shape=(jax.ShapeDtypeStruct((pairs, width), F32),) * 4,
+        in_specs=[smem()] + [vmem()] * 4 * len(held) + [anywhere()],
         out_specs=(vmem(),) * 4,
-        scratch_shapes=[pltpu.VMEM((count, own, width), F32)],
-        compiler_params=grant(8),
-        cost_estimate=small_cost(),
-    )(place, keep, got, after)
+        scratch_shapes=[pltpu.VMEM((extra, 4, slots, lanes), F32)] * 2,
+        compiler_params=grant(16),
+        cost_estimate=small_cost(),
+    )(place, *(p for pieces in held for p in pieces), after)
 
 
 def labels(place, vir, occ, allowed, pair_list, occ_e, vir_e, vir_tile, bound, denom, live):
@@ -284,7 +308,7 @@
         value = jnp.where(orb < total, vir_e[jnp.minimum(orb, total - 1)], 0.0)
         return jnp.where(slot == column * width + s, value, acc)
 
-    eps_b = lax.fori_loop(0, width, put, jnp.zeros((own, width), F32))
+    eps_b = lax.fori_loop(0, width, put, jnp.zeros((own, width), F32), unroll=8)
     eps_ij = jnp.zeros((own, width), F32)
     for p in range(own):
         i, j = pair_list[0, y * own + p], pair_list[1, y * own + p]
@@ -294,7 +318,7 @@
 
 
 READY = 4
-SLOTS = 3
+SLOTS = 4
 PARTS = 4
 
 
@@ -454,11 +478,10 @@
     blocks = [mine] + [send(mine, FIRST[n]) for n in (1, -1, 2)]
     choice = (pair_list[:, 1:] == jnp.arange(cycle_int.shape[1], dtype=jnp.int32)).astype(F32)
     choice = jnp.repeat(choice, cycle_amp.shape[1], axis=0)
-    keep, away = cycle(place, cycle_amp, jnp.transpose(cycle_int, (1, 2, 0)), choice)
-    low, high = stack(place, blocks, keep)
+    share = cycle(place, cycle_amp, jnp.transpose(cycle_int, (1, 2, 0)), choice)
+    low, high = stack(place, blocks, share)
     low_below, high_above = send(low, SECOND[1]), send(high, SECOND[-1])
     high_below, low_above = send(high, SECOND[1]), send(low, SECOND[-1])
-    got = send(away, Z_ACROSS)
     slab, bound, denom, live = ready(
         place,
         (vir, occ, allowed, pair_list.T, occ_e, vir_e),
@@ -472,9 +495,9 @@
         (low, low_below, low_above, send(low_below, SECOND[1])),
         (high, high_below, high_above, send(high_above, SECOND[-1])),
     ]
-    chunks = pack(held, (bound, got))
+    chunks = pack(held, (bound,))
     others = [send(v, SWAP) for v in chunks]
-    parts = spread(by_row(place, keep, got, chunks[0]), ALONG_X)
+    parts = spread(shares(place, held, pairs, width, chunks[0]), FIRST)
     sums = ladder(place, bound, slab, chunks[0], others[0], 0, bound, bound)
     sums = ladder(place, bound, slab, chunks[1], others[1], CHUNKS[0], sums, bound, parts)
     s0, s1, s2, s3 = spread(sums, ALONG_Y)

time: 62.8 us -> 60.7 us (0.967)
  waiting for transfers between devices: 11.2 us -> 10.1 us
    ppermute x18 -> x17, waiting for transfers between devices: 11.2 us -> 10.1 us  [send(): return lax.ppermute(value, AXES, pairs)]
    ppermute x18 -> x17, starting transfers between devices: 25.1 us -> 24.7 us  [send(): return lax.ppermute(value, AXES, pairs)]
  transfers between devices with their start and end apart: 18 -> 17, of which waited for: 4 -> 5; matrix products, arithmetic and copies ran while one was open for 1% -> 1% of each run, Pallas kernels for 30% -> 30%
where the time goes in v5:
time: 60.7 us; the launch traced here: 60.4 us
  starting transfers between devices  24.7 us (41%)
  Pallas kernels  24.1 us (40%)
  waiting for transfers between devices  10.1 us (17%)
  other arithmetic  0.75 us (1%)
  local copies, waits for them, and re-layouts  0.69 us (1%)
    ppermute x17, starting transfers between devices, send(): return lax.ppermute(value, AXES, pairs)  24.7 us
    ppermute x17, waiting for transfers between devices, send(): return lax.ppermute(value, AXES, pairs)  10.1 us
    pallas_call x1, Pallas kernels, ready(): pl.pallas_call(ready_body, out_shape=(jax.ShapeDtypeStruct((cells // CELL...  8.05 us
    pallas_call x2, Pallas kernels, ladder(): pl.pallas_call(functools.partial(ladder_body, last, base), out_shape=out_...  7.35 us
    pallas_call x1, Pallas kernels, cycle(): pl.pallas_call(functools.partial(cycle_body, depth), grid=(pl.cdiv(depth,...  5.61 us
    pallas_call x1, Pallas kernels, relayout(): pl.pallas_call(relayout_body, out_shape=jax.ShapeDtypeStruct((cells // CE...  1.54 us
  transfers between devices with their start and end apart: 17, of which 5 were waited for; matrix products, arithmetic and copies ran while one was open for 1% of the time, Pallas kernels for 30%

profile of v5, /device:TPU:0, one launch (start us, length us, event | category | flops | bytes accessed | tf_op | source)
XLA Modules:
  0.0 60.4 jit_solution(18413661865413282489)
XLA Ops:
  0.0 1.5 %shard_map.100.b0 = f32[64,8,128]{2,1,0:T(8,128)S(1)} custom-call(f32[32,8,256]{2,1,0:T(8,128)} %bitcast.17), custom_call_target="tpu_custom_call" | custom-call | flops 1 | bytes 1 | tf_op jit(solution)/shard_map/pallas_call | solution.py:100
  1.5 3.2 %collective-permute-start.2 = (f32[64,8,128]{2,1,0:T(8,128)S(1)}, f32[64,8,128]{2,1,0:T(8,128)S(1)}, u32[]{:S(2)}, u32[]{:S(2)}) collective-permute-start(f32[64,8,128]{2,1,0:T(8,128)S(1)} %shard_map.100.b0), channel_id=1, source_target_pairs={{0,16},{1,5},{2,18},{3,7},{4,20},{5,1},{6,22},{7,3},{8,24},{9,13},... | collective-permute-start | bytes 786440 | tf_op jit(solution)/shard_map/ppermute | solution.py:50
  4.7 1.1 %collective-permute-start.1 = (f32[64,8,128]{2,1,0:T(8,128)S(1)}, f32[64,8,128]{2,1,0:T(8,128)S(1)}, u32[]{:S(2)}, u32[]{:S(2)}) collective-permute-start(f32[64,8,128]{2,1,0:T(8,128)S(1)} %shard_map.100.b0), channel_id=1, source_target_pairs={{0,24},{1,7},{2,26},{3,1},{4,28},{5,3},{6,30},{7,5},{8,0},{9,15},{... | collective-permute-start | bytes 786440 | tf_op jit(solution)/shard_map/ppermute | solution.py:50
  5.9 0.9 %collective-permute-start = (f32[64,8,128]{2,1,0:T(8,128)S(1)}, f32[64,8,128]{2,1,0:T(8,128)S(1)}, u32[]{:S(2)}, u32[]{:S(2)}) collective-permute-start(f32[64,8,128]{2,1,0:T(8,128)S(1)} %shard_map.100.b0), channel_id=1, source_target_pairs={{0,8},{1,3},{2,10},{3,5},{4,12},{5,7},{6,14},{7,1},{8,16},{9,11},{... | collective-permute-start | bytes 786440 | tf_op jit(solution)/shard_map/ppermute | solution.py:50
  6.8 0.7 %slice_bitcast_fusion = s32[32]{0:T(128)S(1)} fusion(s32[32,2]{0,1:T(2,128)} %param.13), kind=kLoop, calls=%fused_computation.5 | loop fusion | bytes 256 | tf_op jit(solution)/shard_map/eq | solution.py:479
  7.4 0.1 fusion
  7.5 0.1 pad_add_fusion.place.refs_0_
  7.6 5.6 %shard_map.101.share = f32[4,4,8,128]{3,2,1,0:T(8,128)S(1)} custom-call(s32[4]{0:T(128)S(1)} %pad_add_fusion.place.refs_0_, f32[32,8,4800]{2,1,0:T(8,128)} %amp_ref.1, f32[4,64,4800]{2,1,0:T(8,128)} %bitcast.16, f32[256,4]{1,0:T(8,128)S(1)} %broadcast_bitcast_fusion.choice_ref), custom_call_target="tpu_custom_call" | custom-call | flops 1 | bytes 1 | tf_op jit(solution)/shard_map/pallas_call | solution.py:203
  13.2 0.0 collective-permute-done.2.b3
  13.2 0.0 collective-permute-done.1.b2
  13.3 0.2 collective-permute-done.b1
  13.5 0.6 %shard_map.102 = (f32[34,4,8,128]{3,2,1,0:T(8,128)S(1)}, f32[34,4,8,128]{3,2,1,0:T(8,128)S(1)}) custom-call(s32[4]{0:T(128)S(1)} %pad_add_fusion.place.refs_0_, f32[64,8,128]{2,1,0:T(8,128)S(1)} %shard_map.100.b0, f32[64,8,128]{2,1,0:T(8,128)S(1)} %collective-permute-done.b1, f32[64,8,128]{2,1,0:T(8,128)S(1)} %collective-permute-done.1.b2, ...), custom_call_target="tpu_custom_call" | custom-call | flops 1 | bytes 1 | tf_op jit(solution)/shard_map/pallas_call | solution.py:128
  14.1 2.0 %collective-permute-start.3 = (f32[34,4,8,128]{3,2,1,0:T(8,128)S(1)}, f32[34,4,8,128]{3,2,1,0:T(8,128)S(1)}, u32[]{:S(2)}, u32[]{:S(2)}) collective-permute-start(f32[34,4,8,128]{3,2,1,0:T(8,128)S(1)} %get-tuple-element.21.refs_0_), channel_id=1, source_target_pairs={{0,2},{1,9},{2,4},{3,11},{4,6},{5,13},{6,0},{7,15},{8,10},{9,17},{... | collective-permute-start | bytes 1671176 | tf_op jit(solution)/shard_map/ppermute | solution.py:50
  16.1 2.2 %collective-permute-start.4 = (f32[34,4,8,128]{3,2,1,0:T(8,128)S(1)}, f32[34,4,8,128]{3,2,1,0:T(8,128)S(1)}, u32[]{:S(2)}, u32[]{:S(2)}) collective-permute-start(f32[34,4,8,128]{3,2,1,0:T(8,128)S(1)} %get-tuple-element.22.refs_4_), channel_id=1, source_target_pairs={{0,6},{1,25},{2,0},{3,27},{4,2},{5,29},{6,4},{7,31},{8,14},{9,1},{... | collective-permute-start | bytes 1671176 | tf_op jit(solution)/shard_map/ppermute | solution.py:50
  18.3 1.9 %collective-permute-start.5 = (f32[34,4,8,128]{3,2,1,0:T(8,128)S(1)}, f32[34,4,8,128]{3,2,1,0:T(8,128)S(1)}, u32[]{:S(2)}, u32[]{:S(2)}) collective-permute-start(f32[34,4,8,128]{3,2,1,0:T(8,128)S(1)} %get-tuple-element.21.refs_0_), channel_id=1, source_target_pairs={{0,6},{1,25},{2,0},{3,27},{4,2},{5,29},{6,4},{7,31},{8,14},{9,1},{... | collective-permute-start | bytes 1671176 | tf_op jit(solution)/shard_map/ppermute | solution.py:50
  20.2 0.1 collective-permute-start.7
  20.3 5.4 %collective-permute-done.3.refs_9_.refs_1_ = f32[34,4,8,128]{3,2,1,0:T(8,128)S(1)} collective-permute-done((f32[34,4,8,128]{3,2,1,0:T(8,128)S(1)}, f32[34,4,8,128]{3,2,1,0:T(8,128)S(1)}, u32[]{:S(2)}, u32[]{:S(2)}) %collective-permute-start.3) | collective-permute-done | bytes 557088 | tf_op jit(solution)/shard_map/ppermute | solution.py:50
  25.7 0.0 collective-permute-start.6
  25.7 0.0 collective-permute-done.4.refs_10_.refs_6_
  25.7 3.3 %collective-permute-start.8 = (f32[34,4,8,128]{3,2,1,0:T(8,128)S(1)}, f32[34,4,8,128]{3,2,1,0:T(8,128)S(1)}, u32[]{:S(2)}, u32[]{:S(2)}) collective-permute-start(f32[34,4,8,128]{3,2,1,0:T(8,128)S(1)} %collective-permute-done.4.refs_10_.refs_6_), channel_id=1, source_target_pairs={{0,6},{1,25},{2,0},{3,27},{4,2},{5,29},{6,4},{7,31},{8,14},{9,1},{... | collective-permute-start | bytes 1671176 | tf_op jit(solution)/shard_map/ppermute | solution.py:50
  29.0 8.0 %shard_map.103 = (bf16[64,512,256]{2,1,0:T(8,128)(2,1)S(1)}, s32[64,128]{1,0:T(8,128)S(1)}, f32[8,64]{1,0:T(8,128)S(1)}, s32[8,64]{1,0:T(8,128)S(1)}) custom-call(s32[4]{0:T(128)S(1)} %pad_add_fusion.place.refs_0_, s32[1024]{0:T(1024)} %refs_1_.1, s32[150]{0:T(256)} %refs_2_.1, s32[8,8,8]{2,1,0:T(8,128)} %refs_3_.1, s32[2,32]{1,0:T(2,128)} %bitcast.19, ...), custom_call_target="tpu_custom_call" | custom-call | flops 1 | bytes 1 | tf_op jit(solution)/shard_map/pallas_call | solution.py:367
  37.1 0.0 collective-permute-done.5.refs_2_
  37.1 0.0 collective-permute-done.7.refs_5_
  37.1 0.5 collective-permute-done.6.refs_3_
  37.6 0.0 collective-permute-done.8.refs_7_
  37.6 0.3 shard_map.104
  37.9 0.1 collective-permute-start.10
  38.0 0.5 collective-permute-start.9
  38.5 0.6 %shard_map.106 = (f32[32,64]{1,0:T(8,128)S(1)}, f32[32,64]{1,0:T(8,128)S(1)}, f32[32,64]{1,0:T(8,128)S(1)}, f32[32,64]{1,0:T(8,128)S(1)}) custom-call(s32[4]{0:T(128)S(1)} %pad_add_fusion.place.refs_0_, f32[34,4,8,128]{3,2,1,0:T(8,128)S(1)} %get-tuple-element.21.refs_0_, f32[34,4,8,128]{3,2,1,0:T(8,128)S(1)} %collective-permute-done.3.refs_9_.refs_1_, ...), custom_call_target="tpu_custom_call" | custom-call | flops 1 | bytes 1 | tf_op jit(solution)/shard_map/pallas_call | solution.py:256
  39.2 0.5 collective-permute-start.11
  39.7 2.8 %collective-permute-start.12 = (f32[32,64]{1,0:T(8,128)S(1)}, f32[32,64]{1,0:T(8,128)S(1)}, u32[]{:S(2)}, u32[]{:S(2)}) collective-permute-start(f32[32,64]{1,0:T(8,128)S(1)} %get-tuple-element.30), channel_id=1, source_target_pairs={{0,24},{1,7},{2,26},{3,1},{4,28},{5,3},{6,30},{7,5},{8,0},{9,15},{... | collective-permute-start | bytes 24584 | tf_op jit(solution)/shard_map/ppermute | solution.py:50
  42.5 0.8 %collective-permute-start.13 = (f32[32,64]{1,0:T(8,128)S(1)}, f32[32,64]{1,0:T(8,128)S(1)}, u32[]{:S(2)}, u32[]{:S(2)}) collective-permute-start(f32[32,64]{1,0:T(8,128)S(1)} %get-tuple-element.31), channel_id=1, source_target_pairs={{0,16},{1,5},{2,18},{3,7},{4,20},{5,1},{6,22},{7,3},{8,24},{9,13},... | collective-permute-start | bytes 24584 | tf_op jit(solution)/shard_map/ppermute | solution.py:50
  43.2 0.0 collective-permute-done.10.other
  43.2 3.7 %shard_map.105.before = f32[32,64]{1,0:T(8,128)S(1)} custom-call(s32[4]{0:T(128)S(1)} %pad_add_fusion.place.refs_0_, s32[64,128]{1,0:T(8,128)S(1)} %get-tuple-element.24.refs_8_.bound.before.after, bf16[64,512,256]{2,1,0:T(8,128)(2,1)S(1)} %get-tuple-element.25.slab, f32[32,16,8,128]{3,2,1,0:T(8,128)S(1)} %get-tuple-element.27.mine.refs_8_, ...), custom_call_target="tpu_custom_call" | custom-call | flops 1 | bytes 1 | tf_op jit(solution)/shard_map/pallas_call | solution.py:452
  46.9 0.0 collective-permute-done.11.rest_1_
  46.9 0.0 collective-permute-done.12.rest_2_
  46.9 0.8 %collective-permute-done.13.rest_3_ = f32[32,64]{1,0:T(8,128)S(1)} collective-permute-done((f32[32,64]{1,0:T(8,128)S(1)}, f32[32,64]{1,0:T(8,128)S(1)}, u32[]{:S(2)}, u32[]{:S(2)}) %collective-permute-start.13) | collective-permute-done | bytes 8224 | tf_op jit(solution)/shard_map/ppermute | solution.py:50
  47.7 0.0 collective-permute-done.9.other
  47.7 3.7 %shard_map.107 = (f32[8,64]{1,0:T(8,128)S(1)}, f32[8,64]{1,0:T(8,128)S(1)}, f32[8,64]{1,0:T(8,128)S(1)}, f32[8,64]{1,0:T(8,128)S(1)}) custom-call(s32[4]{0:T(128)S(1)} %pad_add_fusion.place.refs_0_, s32[64,128]{1,0:T(8,128)S(1)} %get-tuple-element.24.refs_8_.bound.before.after, bf16[64,512,256]{2,1,0:T(8,128)(2,1)S(1)} %get-tuple-element.25.slab, ...), custom_call_target="tpu_custom_call" | custom-call | flops 1 | bytes 1 | tf_op jit(solution)/shard_map/pallas_call | solution.py:452
  51.4 1.6 %collective-permute-start.14 = (f32[8,64]{1,0:T(8,128)S(1)}, f32[8,64]{1,0:T(8,128)S(1)}, u32[]{:S(2)}, u32[]{:S(2)}) collective-permute-start(f32[8,64]{1,0:T(8,128)S(1)} %get-tuple-element.33), channel_id=1, source_target_pairs={{0,32},{1,33},{2,34},{3,35},{4,36},{5,37},{6,38},{7,39},{8,40},{9,... | collective-permute-start | bytes 6152 | tf_op jit(solution)/shard_map/ppermute | solution.py:50
  53.0 1.7 %collective-permute-start.15 = (f32[8,64]{1,0:T(8,128)S(1)}, f32[8,64]{1,0:T(8,128)S(1)}, u32[]{:S(2)}, u32[]{:S(2)}) collective-permute-start(f32[8,64]{1,0:T(8,128)S(1)} %get-tuple-element.34), channel_id=1, source_target_pairs={{0,96},{1,97},{2,98},{3,99},{4,100},{5,101},{6,102},{7,103},{8,104... | collective-permute-start | bytes 6152 | tf_op jit(solution)/shard_map/ppermute | solution.py:50
  54.7 2.0 %collective-permute-start.16 = (f32[8,64]{1,0:T(8,128)S(1)}, f32[8,64]{1,0:T(8,128)S(1)}, u32[]{:S(2)}, u32[]{:S(2)}) collective-permute-start(f32[8,64]{1,0:T(8,128)S(1)} %get-tuple-element.35), channel_id=1, source_target_pairs={{0,64},{1,65},{2,66},{3,67},{4,68},{5,69},{6,70},{7,71},{8,72},{9,... | collective-permute-start | bytes 6152 | tf_op jit(solution)/shard_map/ppermute | solution.py:50
  56.7 0.0 collective-permute-done.14
  56.7 0.0 collective-permute-done.15
  56.7 3.1 %collective-permute-done.16 = f32[8,64]{1,0:T(8,128)S(1)} collective-permute-done((f32[8,64]{1,0:T(8,128)S(1)}, f32[8,64]{1,0:T(8,128)S(1)}, u32[]{:S(2)}, u32[]{:S(2)}) %collective-permute-start.16) | collective-permute-done | bytes 2080 | tf_op jit(solution)/shard_map/ppermute | solution.py:50
  59.8 0.6 select_bitcast_fusion
  (1 shorter events, 0.0 us)
Async XLA Ops:
  1.5 11.7 %collective-permute-start.2 = (f32[64,8,128]{2,1,0:T(8,128)S(1)}, f32[64,8,128]{2,1,0:T(8,128)S(1)}, u32[]{:S(2)}, u32[]{:S(2)}) collective-permute-start(f32[64,8,128]{2,1,0:T(8,128)S(1)} %shard_map.100.b0), channel_id=1, source_target_pairs={{0,16},{1,5},{2,18},{3,7},{4,20},{5,1},{6,22},{7,3},{8,24},{9,13},... | collective-permute-start | bytes 786440 | tf_op jit(solution)/shard_map/ppermute | solution.py:50
  4.7 8.5 %collective-permute-start.1 = (f32[64,8,128]{2,1,0:T(8,128)S(1)}, f32[64,8,128]{2,1,0:T(8,128)S(1)}, u32[]{:S(2)}, u32[]{:S(2)}) collective-permute-start(f32[64,8,128]{2,1,0:T(8,128)S(1)} %shard_map.100.b0), channel_id=1, source_target_pairs={{0,24},{1,7},{2,26},{3,1},{4,28},{5,3},{6,30},{7,5},{8,0},{9,15},{... | collective-permute-start | bytes 786440 | tf_op jit(solution)/shard_map/ppermute | solution.py:50
  5.9 7.6 %collective-permute-start = (f32[64,8,128]{2,1,0:T(8,128)S(1)}, f32[64,8,128]{2,1,0:T(8,128)S(1)}, u32[]{:S(2)}, u32[]{:S(2)}) collective-permute-start(f32[64,8,128]{2,1,0:T(8,128)S(1)} %shard_map.100.b0), channel_id=1, source_target_pairs={{0,8},{1,3},{2,10},{3,5},{4,12},{5,7},{6,14},{7,1},{8,16},{9,11},{... | collective-permute-start | bytes 786440 | tf_op jit(solution)/shard_map/ppermute | solution.py:50
  14.1 11.6 %collective-permute-start.3 = (f32[34,4,8,128]{3,2,1,0:T(8,128)S(1)}, f32[34,4,8,128]{3,2,1,0:T(8,128)S(1)}, u32[]{:S(2)}, u32[]{:S(2)}) collective-permute-start(f32[34,4,8,128]{3,2,1,0:T(8,128)S(1)} %get-tuple-element.21.refs_0_), channel_id=1, source_target_pairs={{0,2},{1,9},{2,4},{3,11},{4,6},{5,13},{6,0},{7,15},{8,10},{9,17},{... | collective-permute-start | bytes 1671176 | tf_op jit(solution)/shard_map/ppermute | solution.py:50
  16.1 9.6 %collective-permute-start.4 = (f32[34,4,8,128]{3,2,1,0:T(8,128)S(1)}, f32[34,4,8,128]{3,2,1,0:T(8,128)S(1)}, u32[]{:S(2)}, u32[]{:S(2)}) collective-permute-start(f32[34,4,8,128]{3,2,1,0:T(8,128)S(1)} %get-tuple-element.22.refs_4_), channel_id=1, source_target_pairs={{0,6},{1,25},{2,0},{3,27},{4,2},{5,29},{6,4},{7,31},{8,14},{9,1},{... | collective-permute-start | bytes 1671176 | tf_op jit(solution)/shard_map/ppermute | solution.py:50
  18.3 18.8 %collective-permute-start.5 = (f32[34,4,8,128]{3,2,1,0:T(8,128)S(1)}, f32[34,4,8,128]{3,2,1,0:T(8,128)S(1)}, u32[]{:S(2)}, u32[]{:S(2)}) collective-permute-start(f32[34,4,8,128]{3,2,1,0:T(8,128)S(1)} %get-tuple-element.21.refs_0_), channel_id=1, source_target_pairs={{0,6},{1,25},{2,0},{3,27},{4,2},{5,29},{6,4},{7,31},{8,14},{9,1},{... | collective-permute-start | bytes 1671176 | tf_op jit(solution)/shard_map/ppermute | solution.py:50
  20.2 16.9 %collective-permute-start.7 = (f32[34,4,8,128]{3,2,1,0:T(8,128)S(1)}, f32[34,4,8,128]{3,2,1,0:T(8,128)S(1)}, u32[]{:S(2)}, u32[]{:S(2)}) collective-permute-start(f32[34,4,8,128]{3,2,1,0:T(8,128)S(1)} %get-tuple-element.22.refs_4_), channel_id=1, source_target_pairs={{0,2},{1,9},{2,4},{3,11},{4,6},{5,13},{6,0},{7,15},{8,10},{9,17},{... | collective-permute-start | bytes 1671176 | tf_op jit(solution)/shard_map/ppermute | solution.py:50
  25.7 11.9 %collective-permute-start.6 = (f32[34,4,8,128]{3,2,1,0:T(8,128)S(1)}, f32[34,4,8,128]{3,2,1,0:T(8,128)S(1)}, u32[]{:S(2)}, u32[]{:S(2)}) collective-permute-start(f32[34,4,8,128]{3,2,1,0:T(8,128)S(1)} %collective-permute-done.3.refs_9_.refs_1_), channel_id=1, source_target_pairs={{0,2},{1,9},{2,4},{3,11},{4,6},{5,13},{6,0},{7,15},{8,10},{9,17},{... | collective-permute-start | bytes 1671176 | tf_op jit(solution)/shard_map/ppermute | solution.py:50
  25.7 11.9 %collective-permute-start.8 = (f32[34,4,8,128]{3,2,1,0:T(8,128)S(1)}, f32[34,4,8,128]{3,2,1,0:T(8,128)S(1)}, u32[]{:S(2)}, u32[]{:S(2)}) collective-permute-start(f32[34,4,8,128]{3,2,1,0:T(8,128)S(1)} %collective-permute-done.4.refs_10_.refs_6_), channel_id=1, source_target_pairs={{0,6},{1,25},{2,0},{3,27},{4,2},{5,29},{6,4},{7,31},{8,14},{9,1},{... | collective-permute-start | bytes 1671176 | tf_op jit(solution)/shard_map/ppermute | solution.py:50
  37.9 5.3 %collective-permute-start.10 = (f32[32,16,8,128]{3,2,1,0:T(8,128)S(1)}, f32[32,16,8,128]{3,2,1,0:T(8,128)S(1)}, u32[]{:S(2)}, u32[]{:S(2)}) collective-permute-start(f32[32,16,8,128]{3,2,1,0:T(8,128)S(1)} %get-tuple-element.27.mine.refs_8_), channel_id=1, source_target_pairs={{0,1},{1,0},{2,3},{3,2},{4,5},{5,4},{6,7},{7,6},{8,9},{9,8},{10,11... | collective-permute-start | bytes 6291464 | tf_op jit(solution)/shard_map/ppermute | solution.py:50
  38.0 9.7 %collective-permute-start.9 = (f32[32,16,8,128]{3,2,1,0:T(8,128)S(1)}, f32[32,16,8,128]{3,2,1,0:T(8,128)S(1)}, u32[]{:S(2)}, u32[]{:S(2)}) collective-permute-start(f32[32,16,8,128]{3,2,1,0:T(8,128)S(1)} %get-tuple-element.26.mine), channel_id=1, source_target_pairs={{0,1},{1,0},{2,3},{3,2},{4,5},{5,4},{6,7},{7,6},{8,9},{9,8},{10,11... | collective-permute-start | bytes 6291464 | tf_op jit(solution)/shard_map/ppermute | solution.py:50
  39.2 7.7 %collective-permute-start.11 = (f32[32,64]{1,0:T(8,128)S(1)}, f32[32,64]{1,0:T(8,128)S(1)}, u32[]{:S(2)}, u32[]{:S(2)}) collective-permute-start(f32[32,64]{1,0:T(8,128)S(1)} %get-tuple-element.29), channel_id=1, source_target_pairs={{0,8},{1,3},{2,10},{3,5},{4,12},{5,7},{6,14},{7,1},{8,16},{9,11},{... | collective-permute-start | bytes 24584 | tf_op jit(solution)/shard_map/ppermute | solution.py:50
  39.7 7.2 %collective-permute-start.12 = (f32[32,64]{1,0:T(8,128)S(1)}, f32[32,64]{1,0:T(8,128)S(1)}, u32[]{:S(2)}, u32[]{:S(2)}) collective-permute-start(f32[32,64]{1,0:T(8,128)S(1)} %get-tuple-element.30), channel_id=1, source_target_pairs={{0,24},{1,7},{2,26},{3,1},{4,28},{5,3},{6,30},{7,5},{8,0},{9,15},{... | collective-permute-start | bytes 24584 | tf_op jit(solution)/shard_map/ppermute | solution.py:50
  42.5 5.2 %collective-permute-start.13 = (f32[32,64]{1,0:T(8,128)S(1)}, f32[32,64]{1,0:T(8,128)S(1)}, u32[]{:S(2)}, u32[]{:S(2)}) collective-permute-start(f32[32,64]{1,0:T(8,128)S(1)} %get-tuple-element.31), channel_id=1, source_target_pairs={{0,16},{1,5},{2,18},{3,7},{4,20},{5,1},{6,22},{7,3},{8,24},{9,13},... | collective-permute-start | bytes 24584 | tf_op jit(solution)/shard_map/ppermute | solution.py:50
  51.4 5.3 %collective-permute-start.14 = (f32[8,64]{1,0:T(8,128)S(1)}, f32[8,64]{1,0:T(8,128)S(1)}, u32[]{:S(2)}, u32[]{:S(2)}) collective-permute-start(f32[8,64]{1,0:T(8,128)S(1)} %get-tuple-element.33), channel_id=1, source_target_pairs={{0,32},{1,33},{2,34},{3,35},{4,36},{5,37},{6,38},{7,39},{8,40},{9,... | collective-permute-start | bytes 6152 | tf_op jit(solution)/shard_map/ppermute | solution.py:50
  53.0 3.7 %collective-permute-start.15 = (f32[8,64]{1,0:T(8,128)S(1)}, f32[8,64]{1,0:T(8,128)S(1)}, u32[]{:S(2)}, u32[]{:S(2)}) collective-permute-start(f32[8,64]{1,0:T(8,128)S(1)} %get-tuple-element.34), channel_id=1, source_target_pairs={{0,96},{1,97},{2,98},{3,99},{4,100},{5,101},{6,102},{7,103},{8,104... | collective-permute-start | bytes 6152 | tf_op jit(solution)/shard_map/ppermute | solution.py:50
  54.7 5.1 %collective-permute-start.16 = (f32[8,64]{1,0:T(8,128)S(1)}, f32[8,64]{1,0:T(8,128)S(1)}, u32[]{:S(2)}, u32[]{:S(2)}) collective-permute-start(f32[8,64]{1,0:T(8,128)S(1)} %get-tuple-element.35), channel_id=1, source_target_pairs={{0,64},{1,65},{2,66},{3,67},{4,68},{5,69},{6,70},{7,71},{8,72},{9,... | collective-permute-start | bytes 6152 | tf_op jit(solution)/shard_map/ppermute | solution.py:50

commit v6 on v5

--- a/solution.py
+++ b/solution.py
@@ -135,23 +135,26 @@
     )(place, *blocks, share)
 
 
-def pack_body(*refs):
-    out = refs[-len(CHUNKS) :]
-    for n, o in enumerate(out):
+def pack_body(place, *refs):
+    for n, o in enumerate(refs[-8:-6]):
         for i in range(4):
             o[:, 4 * i : 4 * i + 4] = refs[4 * n + i][0 : CHUNKS[n]]
-
-
-def pack(held, after):
-    _, _, slots, lanes = held[0][0].shape
+    shares_body(place, *refs[:8], *refs[-6:])
+
+
+def pack(place, held, pairs, width, after):
+    extra, _, slots, lanes = held[0][0].shape
+    extra = (extra - CHUNKS[0]) * len(CHUNKS)
     return pl.pallas_call(
         pack_body,
-        out_shape=tuple(jax.ShapeDtypeStruct((n, 16, slots, lanes), F32) for n in CHUNKS),
-        in_specs=[vmem()] * 4 * len(held) + [anywhere()] * len(after),
-        out_specs=(vmem(),) * len(CHUNKS),
+        out_shape=tuple(jax.ShapeDtypeStruct((n, 16, slots, lanes), F32) for n in CHUNKS)
+        + (jax.ShapeDtypeStruct((pairs, width), F32),) * 4,
+        in_specs=[smem()] + [vmem()] * 4 * len(held) + [anywhere()] * len(after),
+        out_specs=(vmem(),) * (len(CHUNKS) + 4),
+        scratch_shapes=[pltpu.VMEM((extra, 4, slots, lanes), F32)] * 2,
         compiler_params=grant(16),
         cost_estimate=small_cost(),
-    )(*(p for pieces in held for p in pieces), *after)
+    )(place, *(p for pieces in held for p in pieces), *after)
 
 
 def dot_nt(a, b):
@@ -248,20 +251,6 @@
         o1[...] = jnp.zeros_like(o1)
         o2[...] = jnp.zeros_like(o2)
         o3[...] = side(total, 1 - half)
-
-
-def shares(place, held, pairs, width, after):
-    extra, _, slots, lanes = held[0][0].shape
-    extra = (extra - CHUNKS[0]) * len(CHUNKS)
-    return pl.pallas_call(
-        shares_body,
-        out_shape=(jax.ShapeDtypeStruct((pairs, width), F32),) * 4,
-        in_specs=[smem()] + [vmem()] * 4 * len(held) + [anywhere()],
-        out_specs=(vmem(),) * 4,
-        scratch_shapes=[pltpu.VMEM((extra, 4, slots, lanes), F32)] * 2,
-        compiler_params=grant(16),
-        cost_estimate=small_cost(),
-    )(place, *(p for pieces in held for p in pieces), after)
 
 
 def labels(place, vir, occ, allowed, pair_list, occ_e, vir_e, vir_tile, bound, denom, live):
@@ -383,7 +372,7 @@
     )(place, *(in_hbm(v) for v in tables), vir_tile, in_hbm(slab), *after)
 
 
-STEP = 8
+STEP = 16
 
 
 def ladder_body(last, base, place, bound, slab, mine, other, before, after, *rest):
@@ -495,9 +484,9 @@
         (low, low_below, low_above, send(low_below, SECOND[1])),
         (high, high_below, high_above, send(high_above, SECOND[-1])),
     ]
-    chunks = pack(held, (bound,))
+    *chunks, p0, p1, p2, p3 = pack(place, held, pairs, width, (bound,))
     others = [send(v, SWAP) for v in chunks]
-    parts = spread(shares(place, held, pairs, width, chunks[0]), FIRST)
+    parts = spread((p0, p1, p2, p3), FIRST)
     sums = ladder(place, bound, slab, chunks[0], others[0], 0, bound, bound)
     sums = ladder(place, bound, slab, chunks[1], others[1], CHUNKS[0], sums, bound, parts)
     s0, s1, s2, s3 = spread(sums, ALONG_Y)

time: 60.7 us -> 60.6 us (level)
    pallas_call x1, Pallas kernels: 0.27 us -> 0.91 us  [pack(): pl.pallas_call(pack_body, out_shape=tuple((jax.ShapeDtypeStruct((n, 16, s...]
    pallas_call x1 -> x0, Pallas kernels: 0.64 us -> none  [shares(): pl.pallas_call(shares_body, out_shape=(jax.ShapeDtypeStruct((pairs, width...]
  transfers between devices with their start and end apart: 17 -> 17, of which waited for: 5 -> 5; matrix products, arithmetic and copies ran while one was open for 1% -> 1% of each run, Pallas kernels for 30% -> 29%
where the time goes in v6:
time: 60.6 us; the launch traced here: 60.4 us
  starting transfers between devices  24.6 us (41%)
  Pallas kernels  24.1 us (40%)
  waiting for transfers between devices  10.1 us (17%)
  other arithmetic  0.75 us (1%)
  local copies, waits for them, and re-layouts  0.69 us (1%)
    ppermute x17, starting transfers between devices, send(): return lax.ppermute(value, AXES, pairs)  24.6 us
    ppermute x17, waiting for transfers between devices, send(): return lax.ppermute(value, AXES, pairs)  10.1 us
    pallas_call x1, Pallas kernels, ready(): pl.pallas_call(ready_body, out_shape=(jax.ShapeDtypeStruct((cells // CELL...  8.05 us
    pallas_call x2, Pallas kernels, ladder(): pl.pallas_call(functools.partial(ladder_body, last, base), out_shape=out_...  7.36 us
    pallas_call x1, Pallas kernels, cycle(): pl.pallas_call(functools.partial(cycle_body, depth), grid=(pl.cdiv(depth,...  5.61 us
    pallas_call x1, Pallas kernels, relayout(): pl.pallas_call(relayout_body, out_shape=jax.ShapeDtypeStruct((cells // CE...  1.54 us
  transfers between devices with their start and end apart: 17, of which 5 were waited for; matrix products, arithmetic and copies ran while one was open for 1% of the time, Pallas kernels for 29%

profile of v6, /device:TPU:0, one launch (start us, length us, event | category | flops | bytes accessed | tf_op | source)
XLA Modules:
  0.0 60.4 jit_solution(12543124487708943424)
XLA Ops:
  0.0 1.5 %shard_map.100.b0 = f32[64,8,128]{2,1,0:T(8,128)S(1)} custom-call(f32[32,8,256]{2,1,0:T(8,128)} %bitcast.17), custom_call_target="tpu_custom_call" | custom-call | flops 1 | bytes 1 | tf_op jit(solution)/shard_map/pallas_call | solution.py:100
  1.5 3.2 %collective-permute-start.2 = (f32[64,8,128]{2,1,0:T(8,128)S(1)}, f32[64,8,128]{2,1,0:T(8,128)S(1)}, u32[]{:S(2)}, u32[]{:S(2)}) collective-permute-start(f32[64,8,128]{2,1,0:T(8,128)S(1)} %shard_map.100.b0), channel_id=1, source_target_pairs={{0,16},{1,5},{2,18},{3,7},{4,20},{5,1},{6,22},{7,3},{8,24},{9,13},... | collective-permute-start | bytes 786440 | tf_op jit(solution)/shard_map/ppermute | solution.py:50
  4.7 1.1 %collective-permute-start.1 = (f32[64,8,128]{2,1,0:T(8,128)S(1)}, f32[64,8,128]{2,1,0:T(8,128)S(1)}, u32[]{:S(2)}, u32[]{:S(2)}) collective-permute-start(f32[64,8,128]{2,1,0:T(8,128)S(1)} %shard_map.100.b0), channel_id=1, source_target_pairs={{0,24},{1,7},{2,26},{3,1},{4,28},{5,3},{6,30},{7,5},{8,0},{9,15},{... | collective-permute-start | bytes 786440 | tf_op jit(solution)/shard_map/ppermute | solution.py:50
  5.9 0.9 %collective-permute-start = (f32[64,8,128]{2,1,0:T(8,128)S(1)}, f32[64,8,128]{2,1,0:T(8,128)S(1)}, u32[]{:S(2)}, u32[]{:S(2)}) collective-permute-start(f32[64,8,128]{2,1,0:T(8,128)S(1)} %shard_map.100.b0), channel_id=1, source_target_pairs={{0,8},{1,3},{2,10},{3,5},{4,12},{5,7},{6,14},{7,1},{8,16},{9,11},{... | collective-permute-start | bytes 786440 | tf_op jit(solution)/shard_map/ppermute | solution.py:50
  6.8 0.7 %slice_bitcast_fusion = s32[32]{0:T(128)S(1)} fusion(s32[32,2]{0,1:T(2,128)} %param.13), kind=kLoop, calls=%fused_computation.5 | loop fusion | bytes 256 | tf_op jit(solution)/shard_map/eq | solution.py:468
  7.4 0.1 fusion
  7.5 0.1 pad_add_fusion.place.refs_0_
  7.6 5.6 %shard_map.101.share = f32[4,4,8,128]{3,2,1,0:T(8,128)S(1)} custom-call(s32[4]{0:T(128)S(1)} %pad_add_fusion.place.refs_0_, f32[32,8,4800]{2,1,0:T(8,128)} %amp_ref.1, f32[4,64,4800]{2,1,0:T(8,128)} %bitcast.16, f32[256,4]{1,0:T(8,128)S(1)} %broadcast_bitcast_fusion.choice_ref), custom_call_target="tpu_custom_call" | custom-call | flops 1 | bytes 1 | tf_op jit(solution)/shard_map/pallas_call | solution.py:206
  13.2 0.0 collective-permute-done.2.b3
  13.2 0.0 collective-permute-done.1.b2
  13.3 0.2 collective-permute-done.b1
  13.5 0.6 %shard_map.102 = (f32[34,4,8,128]{3,2,1,0:T(8,128)S(1)}, f32[34,4,8,128]{3,2,1,0:T(8,128)S(1)}) custom-call(s32[4]{0:T(128)S(1)} %pad_add_fusion.place.refs_0_, f32[64,8,128]{2,1,0:T(8,128)S(1)} %shard_map.100.b0, f32[64,8,128]{2,1,0:T(8,128)S(1)} %collective-permute-done.b1, f32[64,8,128]{2,1,0:T(8,128)S(1)} %collective-permute-done.1.b2, ...), custom_call_target="tpu_custom_call" | custom-call | flops 1 | bytes 1 | tf_op jit(solution)/shard_map/pallas_call | solution.py:128
  14.1 2.0 %collective-permute-start.3 = (f32[34,4,8,128]{3,2,1,0:T(8,128)S(1)}, f32[34,4,8,128]{3,2,1,0:T(8,128)S(1)}, u32[]{:S(2)}, u32[]{:S(2)}) collective-permute-start(f32[34,4,8,128]{3,2,1,0:T(8,128)S(1)} %get-tuple-element.21.refs_0_), channel_id=1, source_target_pairs={{0,2},{1,9},{2,4},{3,11},{4,6},{5,13},{6,0},{7,15},{8,10},{9,17},{... | collective-permute-start | bytes 1671176 | tf_op jit(solution)/shard_map/ppermute | solution.py:50
  16.1 2.2 %collective-permute-start.4 = (f32[34,4,8,128]{3,2,1,0:T(8,128)S(1)}, f32[34,4,8,128]{3,2,1,0:T(8,128)S(1)}, u32[]{:S(2)}, u32[]{:S(2)}) collective-permute-start(f32[34,4,8,128]{3,2,1,0:T(8,128)S(1)} %get-tuple-element.22.refs_4_), channel_id=1, source_target_pairs={{0,6},{1,25},{2,0},{3,27},{4,2},{5,29},{6,4},{7,31},{8,14},{9,1},{... | collective-permute-start | bytes 1671176 | tf_op jit(solution)/shard_map/ppermute | solution.py:50
  18.3 1.9 %collective-permute-start.5 = (f32[34,4,8,128]{3,2,1,0:T(8,128)S(1)}, f32[34,4,8,128]{3,2,1,0:T(8,128)S(1)}, u32[]{:S(2)}, u32[]{:S(2)}) collective-permute-start(f32[34,4,8,128]{3,2,1,0:T(8,128)S(1)} %get-tuple-element.21.refs_0_), channel_id=1, source_target_pairs={{0,6},{1,25},{2,0},{3,27},{4,2},{5,29},{6,4},{7,31},{8,14},{9,1},{... | collective-permute-start | bytes 1671176 | tf_op jit(solution)/shard_map/ppermute | solution.py:50
  20.2 0.1 collective-permute-start.7
  20.3 5.4 %collective-permute-done.3.refs_9_.refs_1_ = f32[34,4,8,128]{3,2,1,0:T(8,128)S(1)} collective-permute-done((f32[34,4,8,128]{3,2,1,0:T(8,128)S(1)}, f32[34,4,8,128]{3,2,1,0:T(8,128)S(1)}, u32[]{:S(2)}, u32[]{:S(2)}) %collective-permute-start.3) | collective-permute-done | bytes 557088 | tf_op jit(solution)/shard_map/ppermute | solution.py:50
  25.7 0.0 collective-permute-start.6
  25.7 0.0 collective-permute-done.4.refs_10_.refs_6_
  25.7 3.3 %collective-permute-start.8 = (f32[34,4,8,128]{3,2,1,0:T(8,128)S(1)}, f32[34,4,8,128]{3,2,1,0:T(8,128)S(1)}, u32[]{:S(2)}, u32[]{:S(2)}) collective-permute-start(f32[34,4,8,128]{3,2,1,0:T(8,128)S(1)} %collective-permute-done.4.refs_10_.refs_6_), channel_id=1, source_target_pairs={{0,6},{1,25},{2,0},{3,27},{4,2},{5,29},{6,4},{7,31},{8,14},{9,1},{... | collective-permute-start | bytes 1671176 | tf_op jit(solution)/shard_map/ppermute | solution.py:50
  29.0 8.0 %shard_map.103 = (bf16[64,512,256]{2,1,0:T(8,128)(2,1)S(1)}, s32[64,128]{1,0:T(8,128)S(1)}, f32[8,64]{1,0:T(8,128)S(1)}, s32[8,64]{1,0:T(8,128)S(1)}) custom-call(s32[4]{0:T(128)S(1)} %pad_add_fusion.place.refs_0_, s32[1024]{0:T(1024)} %refs_1_.1, s32[150]{0:T(256)} %refs_2_.1, s32[8,8,8]{2,1,0:T(8,128)} %refs_3_.1, s32[2,32]{1,0:T(2,128)} %bitcast.19, ...), custom_call_target="tpu_custom_call" | custom-call | flops 1 | bytes 1 | tf_op jit(solution)/shard_map/pallas_call | solution.py:356
  37.1 0.0 collective-permute-done.5.refs_2_
  37.1 0.0 collective-permute-done.7.refs_5_
  37.1 0.5 collective-permute-done.6.refs_3_
  37.6 0.0 collective-permute-done.8.refs_7_
  37.6 0.9 %shard_map.104 = (f32[32,16,8,128]{3,2,1,0:T(8,128)S(1)}, f32[32,16,8,128]{3,2,1,0:T(8,128)S(1)}, f32[32,64]{1,0:T(8,128)S(1)}, f32[32,64]{1,0:T(8,128)S(1)}, f3...) custom-call(s32[4]{0:T(128)S(1)} %pad_add_fusion.place.refs_0_, f32[34,4,8,128]{3,2,1,0:T(8,128)S(1)} %get-tuple-element.21.refs_0_, ...), custom_call_target="tpu_custom_call" | custom-call | flops 1 | bytes 1 | tf_op jit(solution)/shard_map/pallas_call | solution.py:148
  38.6 0.1 collective-permute-start.10
  38.7 0.5 collective-permute-start.9
  39.2 0.5 collective-permute-start.11
  39.6 2.8 %collective-permute-start.12 = (f32[32,64]{1,0:T(8,128)S(1)}, f32[32,64]{1,0:T(8,128)S(1)}, u32[]{:S(2)}, u32[]{:S(2)}) collective-permute-start(f32[32,64]{1,0:T(8,128)S(1)} %get-tuple-element.30), channel_id=1, source_target_pairs={{0,24},{1,7},{2,26},{3,1},{4,28},{5,3},{6,30},{7,5},{8,0},{9,15},{... | collective-permute-start | bytes 24584 | tf_op jit(solution)/shard_map/ppermute | solution.py:50
  42.4 0.8 %collective-permute-start.13 = (f32[32,64]{1,0:T(8,128)S(1)}, f32[32,64]{1,0:T(8,128)S(1)}, u32[]{:S(2)}, u32[]{:S(2)}) collective-permute-start(f32[32,64]{1,0:T(8,128)S(1)} %get-tuple-element.31), channel_id=1, source_target_pairs={{0,16},{1,5},{2,18},{3,7},{4,20},{5,1},{6,22},{7,3},{8,24},{9,13},... | collective-permute-start | bytes 24584 | tf_op jit(solution)/shard_map/ppermute | solution.py:50
  43.1 0.0 collective-permute-done.10.other
  43.1 3.7 %shard_map.105.before = f32[32,64]{1,0:T(8,128)S(1)} custom-call(s32[4]{0:T(128)S(1)} %pad_add_fusion.place.refs_0_, s32[64,128]{1,0:T(8,128)S(1)} %get-tuple-element.24.refs_8_.bound.before.after, bf16[64,512,256]{2,1,0:T(8,128)(2,1)S(1)} %get-tuple-element.25.slab, f32[32,16,8,128]{3,2,1,0:T(8,128)S(1)} %get-tuple-element.27.mine, ...), custom_call_target="tpu_custom_call" | custom-call | flops 1 | bytes 1 | tf_op jit(solution)/shard_map/pallas_call | solution.py:441
  46.8 0.0 collective-permute-done.11.rest_1_
  46.8 0.0 collective-permute-done.12.rest_2_
  46.8 0.8 %collective-permute-done.13.rest_3_ = f32[32,64]{1,0:T(8,128)S(1)} collective-permute-done((f32[32,64]{1,0:T(8,128)S(1)}, f32[32,64]{1,0:T(8,128)S(1)}, u32[]{:S(2)}, u32[]{:S(2)}) %collective-permute-start.13) | collective-permute-done | bytes 8224 | tf_op jit(solution)/shard_map/ppermute | solution.py:50
  47.6 0.0 collective-permute-done.9.other
  47.6 3.7 %shard_map.106 = (f32[8,64]{1,0:T(8,128)S(1)}, f32[8,64]{1,0:T(8,128)S(1)}, f32[8,64]{1,0:T(8,128)S(1)}, f32[8,64]{1,0:T(8,128)S(1)}) custom-call(s32[4]{0:T(128)S(1)} %pad_add_fusion.place.refs_0_, s32[64,128]{1,0:T(8,128)S(1)} %get-tuple-element.24.refs_8_.bound.before.after, bf16[64,512,256]{2,1,0:T(8,128)(2,1)S(1)} %get-tuple-element.25.slab, ...), custom_call_target="tpu_custom_call" | custom-call | flops 1 | bytes 1 | tf_op jit(solution)/shard_map/pallas_call | solution.py:441
  51.3 1.6 %collective-permute-start.14 = (f32[8,64]{1,0:T(8,128)S(1)}, f32[8,64]{1,0:T(8,128)S(1)}, u32[]{:S(2)}, u32[]{:S(2)}) collective-permute-start(f32[8,64]{1,0:T(8,128)S(1)} %get-tuple-element.33), channel_id=1, source_target_pairs={{0,32},{1,33},{2,34},{3,35},{4,36},{5,37},{6,38},{7,39},{8,40},{9,... | collective-permute-start | bytes 6152 | tf_op jit(solution)/shard_map/ppermute | solution.py:50
  53.0 1.7 %collective-permute-start.15 = (f32[8,64]{1,0:T(8,128)S(1)}, f32[8,64]{1,0:T(8,128)S(1)}, u32[]{:S(2)}, u32[]{:S(2)}) collective-permute-start(f32[8,64]{1,0:T(8,128)S(1)} %get-tuple-element.34), channel_id=1, source_target_pairs={{0,96},{1,97},{2,98},{3,99},{4,100},{5,101},{6,102},{7,103},{8,104... | collective-permute-start | bytes 6152 | tf_op jit(solution)/shard_map/ppermute | solution.py:50
  54.6 2.0 %collective-permute-start.16 = (f32[8,64]{1,0:T(8,128)S(1)}, f32[8,64]{1,0:T(8,128)S(1)}, u32[]{:S(2)}, u32[]{:S(2)}) collective-permute-start(f32[8,64]{1,0:T(8,128)S(1)} %get-tuple-element.35), channel_id=1, source_target_pairs={{0,64},{1,65},{2,66},{3,67},{4,68},{5,69},{6,70},{7,71},{8,72},{9,... | collective-permute-start | bytes 6152 | tf_op jit(solution)/shard_map/ppermute | solution.py:50
  56.6 0.0 collective-permute-done.14
  56.6 0.0 collective-permute-done.15
  56.6 3.1 %collective-permute-done.16 = f32[8,64]{1,0:T(8,128)S(1)} collective-permute-done((f32[8,64]{1,0:T(8,128)S(1)}, f32[8,64]{1,0:T(8,128)S(1)}, u32[]{:S(2)}, u32[]{:S(2)}) %collective-permute-start.16) | collective-permute-done | bytes 2080 | tf_op jit(solution)/shard_map/ppermute | solution.py:50
  59.7 0.6 select_bitcast_fusion
  (1 shorter events, 0.0 us)
Async XLA Ops:
  1.5 11.7 %collective-permute-start.2 = (f32[64,8,128]{2,1,0:T(8,128)S(1)}, f32[64,8,128]{2,1,0:T(8,128)S(1)}, u32[]{:S(2)}, u32[]{:S(2)}) collective-permute-start(f32[64,8,128]{2,1,0:T(8,128)S(1)} %shard_map.100.b0), channel_id=1, source_target_pairs={{0,16},{1,5},{2,18},{3,7},{4,20},{5,1},{6,22},{7,3},{8,24},{9,13},... | collective-permute-start | bytes 786440 | tf_op jit(solution)/shard_map/ppermute | solution.py:50
  4.7 8.5 %collective-permute-start.1 = (f32[64,8,128]{2,1,0:T(8,128)S(1)}, f32[64,8,128]{2,1,0:T(8,128)S(1)}, u32[]{:S(2)}, u32[]{:S(2)}) collective-permute-start(f32[64,8,128]{2,1,0:T(8,128)S(1)} %shard_map.100.b0), channel_id=1, source_target_pairs={{0,24},{1,7},{2,26},{3,1},{4,28},{5,3},{6,30},{7,5},{8,0},{9,15},{... | collective-permute-start | bytes 786440 | tf_op jit(solution)/shard_map/ppermute | solution.py:50
  5.9 7.6 %collective-permute-start = (f32[64,8,128]{2,1,0:T(8,128)S(1)}, f32[64,8,128]{2,1,0:T(8,128)S(1)}, u32[]{:S(2)}, u32[]{:S(2)}) collective-permute-start(f32[64,8,128]{2,1,0:T(8,128)S(1)} %shard_map.100.b0), channel_id=1, source_target_pairs={{0,8},{1,3},{2,10},{3,5},{4,12},{5,7},{6,14},{7,1},{8,16},{9,11},{... | collective-permute-start | bytes 786440 | tf_op jit(solution)/shard_map/ppermute | solution.py:50
  14.1 11.6 %collective-permute-start.3 = (f32[34,4,8,128]{3,2,1,0:T(8,128)S(1)}, f32[34,4,8,128]{3,2,1,0:T(8,128)S(1)}, u32[]{:S(2)}, u32[]{:S(2)}) collective-permute-start(f32[34,4,8,128]{3,2,1,0:T(8,128)S(1)} %get-tuple-element.21.refs_0_), channel_id=1, source_target_pairs={{0,2},{1,9},{2,4},{3,11},{4,6},{5,13},{6,0},{7,15},{8,10},{9,17},{... | collective-permute-start | bytes 1671176 | tf_op jit(solution)/shard_map/ppermute | solution.py:50
  16.1 9.6 %collective-permute-start.4 = (f32[34,4,8,128]{3,2,1,0:T(8,128)S(1)}, f32[34,4,8,128]{3,2,1,0:T(8,128)S(1)}, u32[]{:S(2)}, u32[]{:S(2)}) collective-permute-start(f32[34,4,8,128]{3,2,1,0:T(8,128)S(1)} %get-tuple-element.22.refs_4_), channel_id=1, source_target_pairs={{0,6},{1,25},{2,0},{3,27},{4,2},{5,29},{6,4},{7,31},{8,14},{9,1},{... | collective-permute-start | bytes 1671176 | tf_op jit(solution)/shard_map/ppermute | solution.py:50
  18.3 18.8 %collective-permute-start.5 = (f32[34,4,8,128]{3,2,1,0:T(8,128)S(1)}, f32[34,4,8,128]{3,2,1,0:T(8,128)S(1)}, u32[]{:S(2)}, u32[]{:S(2)}) collective-permute-start(f32[34,4,8,128]{3,2,1,0:T(8,128)S(1)} %get-tuple-element.21.refs_0_), channel_id=1, source_target_pairs={{0,6},{1,25},{2,0},{3,27},{4,2},{5,29},{6,4},{7,31},{8,14},{9,1},{... | collective-permute-start | bytes 1671176 | tf_op jit(solution)/shard_map/ppermute | solution.py:50
  20.2 16.9 %collective-permute-start.7 = (f32[34,4,8,128]{3,2,1,0:T(8,128)S(1)}, f32[34,4,8,128]{3,2,1,0:T(8,128)S(1)}, u32[]{:S(2)}, u32[]{:S(2)}) collective-permute-start(f32[34,4,8,128]{3,2,1,0:T(8,128)S(1)} %get-tuple-element.22.refs_4_), channel_id=1, source_target_pairs={{0,2},{1,9},{2,4},{3,11},{4,6},{5,13},{6,0},{7,15},{8,10},{9,17},{... | collective-permute-start | bytes 1671176 | tf_op jit(solution)/shard_map/ppermute | solution.py:50
  25.7 11.9 %collective-permute-start.6 = (f32[34,4,8,128]{3,2,1,0:T(8,128)S(1)}, f32[34,4,8,128]{3,2,1,0:T(8,128)S(1)}, u32[]{:S(2)}, u32[]{:S(2)}) collective-permute-start(f32[34,4,8,128]{3,2,1,0:T(8,128)S(1)} %collective-permute-done.3.refs_9_.refs_1_), channel_id=1, source_target_pairs={{0,2},{1,9},{2,4},{3,11},{4,6},{5,13},{6,0},{7,15},{8,10},{9,17},{... | collective-permute-start | bytes 1671176 | tf_op jit(solution)/shard_map/ppermute | solution.py:50
  25.7 11.9 %collective-permute-start.8 = (f32[34,4,8,128]{3,2,1,0:T(8,128)S(1)}, f32[34,4,8,128]{3,2,1,0:T(8,128)S(1)}, u32[]{:S(2)}, u32[]{:S(2)}) collective-permute-start(f32[34,4,8,128]{3,2,1,0:T(8,128)S(1)} %collective-permute-done.4.refs_10_.refs_6_), channel_id=1, source_target_pairs={{0,6},{1,25},{2,0},{3,27},{4,2},{5,29},{6,4},{7,31},{8,14},{9,1},{... | collective-permute-start | bytes 1671176 | tf_op jit(solution)/shard_map/ppermute | solution.py:50
  38.6 4.6 %collective-permute-start.10 = (f32[32,16,8,128]{3,2,1,0:T(8,128)S(1)}, f32[32,16,8,128]{3,2,1,0:T(8,128)S(1)}, u32[]{:S(2)}, u32[]{:S(2)}) collective-permute-start(f32[32,16,8,128]{3,2,1,0:T(8,128)S(1)} %get-tuple-element.27.mine), channel_id=1, source_target_pairs={{0,1},{1,0},{2,3},{3,2},{4,5},{5,4},{6,7},{7,6},{8,9},{9,8},{10,11... | collective-permute-start | bytes 6291464 | tf_op jit(solution)/shard_map/ppermute | solution.py:50
  38.7 9.0 %collective-permute-start.9 = (f32[32,16,8,128]{3,2,1,0:T(8,128)S(1)}, f32[32,16,8,128]{3,2,1,0:T(8,128)S(1)}, u32[]{:S(2)}, u32[]{:S(2)}) collective-permute-start(f32[32,16,8,128]{3,2,1,0:T(8,128)S(1)} %get-tuple-element.26.mine), channel_id=1, source_target_pairs={{0,1},{1,0},{2,3},{3,2},{4,5},{5,4},{6,7},{7,6},{8,9},{9,8},{10,11... | collective-permute-start | bytes 6291464 | tf_op jit(solution)/shard_map/ppermute | solution.py:50
  39.2 7.7 %collective-permute-start.11 = (f32[32,64]{1,0:T(8,128)S(1)}, f32[32,64]{1,0:T(8,128)S(1)}, u32[]{:S(2)}, u32[]{:S(2)}) collective-permute-start(f32[32,64]{1,0:T(8,128)S(1)} %get-tuple-element.29), channel_id=1, source_target_pairs={{0,8},{1,3},{2,10},{3,5},{4,12},{5,7},{6,14},{7,1},{8,16},{9,11},{... | collective-permute-start | bytes 24584 | tf_op jit(solution)/shard_map/ppermute | solution.py:50
  39.6 7.2 %collective-permute-start.12 = (f32[32,64]{1,0:T(8,128)S(1)}, f32[32,64]{1,0:T(8,128)S(1)}, u32[]{:S(2)}, u32[]{:S(2)}) collective-permute-start(f32[32,64]{1,0:T(8,128)S(1)} %get-tuple-element.30), channel_id=1, source_target_pairs={{0,24},{1,7},{2,26},{3,1},{4,28},{5,3},{6,30},{7,5},{8,0},{9,15},{... | collective-permute-start | bytes 24584 | tf_op jit(solution)/shard_map/ppermute | solution.py:50
  42.4 5.2 %collective-permute-start.13 = (f32[32,64]{1,0:T(8,128)S(1)}, f32[32,64]{1,0:T(8,128)S(1)}, u32[]{:S(2)}, u32[]{:S(2)}) collective-permute-start(f32[32,64]{1,0:T(8,128)S(1)} %get-tuple-element.31), channel_id=1, source_target_pairs={{0,16},{1,5},{2,18},{3,7},{4,20},{5,1},{6,22},{7,3},{8,24},{9,13},... | collective-permute-start | bytes 24584 | tf_op jit(solution)/shard_map/ppermute | solution.py:50
  51.3 5.3 %collective-permute-start.14 = (f32[8,64]{1,0:T(8,128)S(1)}, f32[8,64]{1,0:T(8,128)S(1)}, u32[]{:S(2)}, u32[]{:S(2)}) collective-permute-start(f32[8,64]{1,0:T(8,128)S(1)} %get-tuple-element.33), channel_id=1, source_target_pairs={{0,32},{1,33},{2,34},{3,35},{4,36},{5,37},{6,38},{7,39},{8,40},{9,... | collective-permute-start | bytes 6152 | tf_op jit(solution)/shard_map/ppermute | solution.py:50
  53.0 3.7 %collective-permute-start.15 = (f32[8,64]{1,0:T(8,128)S(1)}, f32[8,64]{1,0:T(8,128)S(1)}, u32[]{:S(2)}, u32[]{:S(2)}) collective-permute-start(f32[8,64]{1,0:T(8,128)S(1)} %get-tuple-element.34), channel_id=1, source_target_pairs={{0,96},{1,97},{2,98},{3,99},{4,100},{5,101},{6,102},{7,103},{8,104... | collective-permute-start | bytes 6152 | tf_op jit(solution)/shard_map/ppermute | solution.py:50
  54.6 5.1 %collective-permute-start.16 = (f32[8,64]{1,0:T(8,128)S(1)}, f32[8,64]{1,0:T(8,128)S(1)}, u32[]{:S(2)}, u32[]{:S(2)}) collective-permute-start(f32[8,64]{1,0:T(8,128)S(1)} %get-tuple-element.35), channel_id=1, source_target_pairs={{0,64},{1,65},{2,66},{3,67},{4,68},{5,69},{6,70},{7,71},{8,72},{9,... | collective-permute-start | bytes 6152 | tf_op jit(solution)/shard_map/ppermute | solution.py:50
